TPU v7x, 256 devices: a whole 4x4x8 slice. The times are simulated.
256 devices in a mesh: nodes: 64 (over y, z, core), heads: 4 (over x).
Axes of the slice: x: 4, y: 4, z: 8, core: 2. Of those that a mesh axis runs over, the one named last changes fastest.
Arguments:
- node_feats: bfloat16 [16384, 512], P('nodes'), may hold values from -16 to 16
- node_types: int32 [16384], P('nodes'), may hold values from 0 to 4
- queries: bfloat16 [16384, 512], P('nodes', 'heads'), may hold values from -6 to 6
- key_rows: bfloat16 [16384, 512], P('nodes', 'heads'), may hold values from -6 to 6
- value_rows: bfloat16 [16384, 512], P('nodes', 'heads'), may hold values from -6 to 6
- halo_keys: bfloat16 [32768, 512], P('nodes', 'heads'), may hold values from -6 to 6
- halo_values: bfloat16 [32768, 512], P('nodes', 'heads'), may hold values from -6 to 6
- halo_rows: int32 [32768], P('nodes'), may hold values from 0 to 256, as said below
- edge_tiles: int32 [2560, 3], P('nodes'), may hold values from 0 to 14, as said below
- grad_output: bfloat16 [16384, 512], P('nodes', 'heads'), may hold values from -6 to 6
- proj_weight: bfloat16 [3, 5, 512, 512], P(None, None, None, 'heads'), may hold values from -0.25 to 0.25
- rel_weight: bfloat16 [2, 15, 8, 64, 64], P(None, None, 'heads'), may hold values from -0.75 to 0.75
- rel_prior: float32 [15, 8], P(None, 'heads'), may hold values from 0.5 to 2
Outputs:
- grad_feats: bfloat16 [16384, 512], P('nodes', 'heads')
- grad_proj: float32 [512, 3, 5, 512], P('nodes', None, None, 'heads')
- grad_rel: float32 [2, 15, 8, 64, 64], P(None, None, 'heads')
- grad_prior: float32 [15, 8], P(None, 'heads')
Inputs may be any that keep to these rules, and one draw needn't show every extreme that they name: `halo_rows`: slab s's halo is 64 blocks of 8 slots, block j holding distinct rows of slab j first and 256 in its empty slots; block s of slab s is empty; one slab t is copied in full: every slab other than t holds 8 distinct rows of t in block t; every other block of another slab holds between 1 and 8 rows. `edge_tiles`: an entry is live when its destination tile is below 4, and is empty with destination 256 // 64, source 0 and relation 0. A source tile below 4 lies among the slab's own rows, the others among its halo slots. Every destination tile has a live entry whose source lies among the own rows. Some slab has every entry live.
All inputs are finite; a program needn't handle non-finite values.
Results may differ from a plain program's by a relative error of at most 0.012.
The roundings to bfloat16 on the way count: a program that leaves them out, or rounds other values in their place, can miss the bound.
Values may be sent and summed in bfloat16 or wider, within the bound.
No kernel may reach another device: no remote copies, remote signals or barrier semaphores. Data moves between devices by JAX's collectives and lax.ppermute only.
A program may use at most 64 MiB of HBM per device.

v0:
```python
import jax
import jax.numpy as jnp
from jax import lax
from jax.experimental import pallas as pl
from jax.experimental.pallas import tpu as pltpu
from jax.sharding import Mesh, PartitionSpec as P

TYPES = 5
RELS = 15
TILE = 64
WIDE = 128
GROUP = 8
PROJ = 3 * TYPES

F32 = jnp.float32
BF16 = jnp.bfloat16
NN = (((1,), (0,)), ((), ()))
NT = (((1,), (1,)), ((), ()))
TN = (((0,), (0,)), ((), ()))
VMEM = pl.BlockSpec(memory_space=pltpu.VMEM)
SMEM = pl.BlockSpec(memory_space=pltpu.SMEM)


def mul(left, right, dims):
    return lax.dot_general(left, right, dims, preferred_element_type=F32)


def column(row):
    return jnp.transpose(jnp.broadcast_to(row, (WIDE, WIDE)), (1, 0))


def attend_kernel(
    edges, q_ref, ko_ref, vo_ref, kh_ref, vh_ref, g_ref, rows_ref, rel_ref, prior_ref,
    own_out, send_out, rel_out,
    wbd, qg, kv, keep, prior, kvm, probs, exps, logs, grads,
    denom, delta, dprior, dkv, dwk, dwv, dq,
):
    count = edges.shape[1]
    dests = q_ref.shape[0] // TILE
    own_tiles = ko_ref.shape[0] // TILE
    halo_tiles = kh_ref.shape[0] // TILE
    lane = lax.broadcasted_iota(jnp.int32, (TILE, WIDE), 1)
    first = lane < TILE

    wbd[...] = jnp.zeros_like(wbd)
    for r in range(RELS):
        for w in range(2):
            for h in range(2):
                at = (2 * w + h) * TILE
                wbd[r, at : at + TILE, at : at + TILE] = rel_ref[w, r, h]
    none = jnp.zeros((TILE, WIDE), BF16)
    for a in range(dests):
        q = (q_ref[a * TILE : (a + 1) * TILE, :].astype(F32) * 0.125).astype(F32)
        g = g_ref[a * TILE : (a + 1) * TILE, :].astype(F32)
        for h in range(2):
            mine = first if h == 0 else jnp.logical_not(first)
            qg[a, h * TILE : (h + 1) * TILE, :WIDE] = jnp.where(mine, q, 0.0).astype(BF16)
            qg[a, h * TILE : (h + 1) * TILE, WIDE:] = none
            qg[a, (2 + h) * TILE : (3 + h) * TILE, :WIDE] = none
            qg[a, (2 + h) * TILE : (3 + h) * TILE, WIDE:] = jnp.where(mine, g, 0.0).astype(BF16)
    for b in range(own_tiles):
        kv[b, :, :WIDE] = ko_ref[b * TILE : (b + 1) * TILE, :]
        kv[b, :, WIDE:] = vo_ref[b * TILE : (b + 1) * TILE, :]
        keep[b] = jnp.ones((TILE, WIDE), F32)
    for b in range(halo_tiles):
        kv[own_tiles + b, :, :WIDE] = kh_ref[b * TILE : (b + 1) * TILE, :]
        kv[own_tiles + b, :, WIDE:] = vh_ref[b * TILE : (b + 1) * TILE, :]
    for j in range(halo_tiles // 2):
        ids = column(rows_ref[j : j + 1, :].astype(F32))
        send_out[j * WIDE : (j + 1) * WIDE, 2 * WIDE :] = ids.astype(BF16)
        ok = (ids < float(q_ref.shape[0])).astype(F32)
        keep[own_tiles + 2 * j] = ok[:TILE]
        keep[own_tiles + 2 * j + 1] = ok[TILE:]
    wide_first = lax.broadcasted_iota(jnp.int32, (RELS, WIDE), 1) < TILE
    prior[:RELS, :] = jnp.where(wide_first, prior_ref[:, 0:1], prior_ref[:, 1:2])

    denom[...] = jnp.zeros_like(denom)
    delta[...] = jnp.zeros_like(delta)
    dprior[...] = jnp.zeros_like(dprior)
    dkv[...] = jnp.zeros_like(dkv)
    dwk[...] = jnp.zeros_like(dwk)
    dwv[...] = jnp.zeros_like(dwv)
    dq[...] = jnp.zeros_like(dq)

    def entry(e):
        target = edges[0, e]
        return jnp.minimum(target, dests - 1), edges[1, e], edges[2, e], target < dests

    def scores(step, carry):
        for u in range(GROUP):
            e = step * GROUP + u
            a, b, r, live = entry(e)
            mixed = mul(kv[b], wbd[r], NN).astype(BF16)
            kvm[e] = mixed
            both = mul(mixed, qg[a], NT)
            logits = both[:, :WIDE]
            logs[e] = logits
            grads[e] = both[:, WIDE:]
            ex = jnp.exp(prior[pl.ds(r, 1), :] * logits) * (keep[b] * live.astype(F32))
            exps[e] = ex
            denom[a] += jnp.sum(ex, axis=0, keepdims=True)
        return carry

    lax.fori_loop(0, count // GROUP, scores, 0)
    denom[...] = 1.0 / denom[...]

    def normalise(step, carry):
        for u in range(GROUP):
            e = step * GROUP + u
            a, b, r, live = entry(e)
            soft = exps[e] * denom[a]
            exps[e] = soft
            prob = soft.astype(BF16)
            probs[e] = prob
            delta[a] += jnp.sum(prob.astype(F32) * grads[e], axis=0, keepdims=True)
        return carry

    lax.fori_loop(0, count // GROUP, normalise, 0)

    def backward(step, carry):
        for u in range(GROUP):
            e = step * GROUP + u
            a, b, r, live = entry(e)
            score_grad = exps[e] * (grads[e] - delta[a])
            dprior[pl.ds(r, 1), :] += jnp.sum(score_grad * logs[e], axis=0, keepdims=True)
            lgrad = (score_grad * prior[pl.ds(r, 1), :]).astype(BF16)
            pair = jnp.concatenate([lgrad, probs[e]], axis=1)
            mixed_grad = mul(pair, qg[a], NN).astype(BF16)
            dkv[b] += mul(mixed_grad, wbd[r], NT)
            dwk[r] += mul(kv[b, :, :WIDE], mixed_grad[:, :WIDE], TN)
            dwv[r] += mul(kv[b, :, WIDE:], mixed_grad[:, WIDE:], TN)
            dq[a] += mul(lgrad, kvm[e, :, :WIDE], TN)
        return carry

    lax.fori_loop(0, count // GROUP, backward, 0)

    for a in range(dests):
        grad = jnp.where(first, dq[a, :TILE, :], dq[a, TILE:, :]) * 0.125
        own_out[a * TILE : (a + 1) * TILE, :WIDE] = grad.astype(BF16)
    for b in range(own_tiles):
        own_out[b * TILE : (b + 1) * TILE, WIDE:] = dkv[b].astype(BF16)
    for b in range(halo_tiles):
        send_out[b * TILE : (b + 1) * TILE, : 2 * WIDE] = dkv[own_tiles + b].astype(BF16)
    for w, ref in enumerate((dwk, dwv)):
        for r in range(RELS):
            at = (w * RELS + r) * TILE
            rel_out[at : at + TILE, :] = jnp.where(first, ref[r, :TILE, :], ref[r, TILE:, :]).astype(BF16)
    at = 2 * RELS * TILE
    sums = dprior[...]
    left = lax.broadcasted_iota(jnp.int32, sums.shape, 1) < TILE
    one = jnp.sum(jnp.where(left, sums, 0.0), axis=1, keepdims=True)
    two = jnp.sum(jnp.where(left, 0.0, sums), axis=1, keepdims=True)
    total = jnp.where(left, one, two)
    high = total.astype(BF16)
    rel_out[at : at + 16, :] = high
    rel_out[at + 16 : at + 32, :] = (total - high.astype(F32)).astype(BF16)
    rel_out[at + 32 :, :] = jnp.zeros((rel_out.shape[0] - at - 32, WIDE), BF16)


def attend(edges, queries, key_rows, value_rows, halo_keys, halo_values, grad_output, halo_rows, rel_weight, rel_prior):
    rows = queries.shape[0]
    halo = halo_keys.shape[0]
    dests = rows // TILE
    sources = (rows + halo) // TILE
    count = edges.shape[1]
    rel_rows = 64 * 32
    return pl.pallas_call(
        attend_kernel,
        out_shape=(
            jax.ShapeDtypeStruct((rows, 3 * WIDE), BF16),
            jax.ShapeDtypeStruct((halo, 3 * WIDE), BF16),
            jax.ShapeDtypeStruct((rel_rows, WIDE), BF16),
        ),
        in_specs=[SMEM] + [VMEM] * 9,
        out_specs=(VMEM, VMEM, VMEM),
        scratch_shapes=[
            pltpu.VMEM((RELS, 2 * WIDE, 2 * WIDE), BF16),
            pltpu.VMEM((dests, 2 * WIDE, 2 * WIDE), BF16),
            pltpu.VMEM((sources, TILE, 2 * WIDE), BF16),
            pltpu.VMEM((sources, TILE, WIDE), F32),
            pltpu.VMEM((16, WIDE), F32),
            pltpu.VMEM((count, TILE, 2 * WIDE), BF16),
            pltpu.VMEM((count, TILE, WIDE), BF16),
            pltpu.VMEM((count, TILE, WIDE), F32),
            pltpu.VMEM((count, TILE, WIDE), F32),
            pltpu.VMEM((count, TILE, WIDE), F32),
            pltpu.VMEM((dests, 1, WIDE), F32),
            pltpu.VMEM((dests, 1, WIDE), F32),
            pltpu.VMEM((16, WIDE), F32),
            pltpu.VMEM((sources, TILE, 2 * WIDE), F32),
            pltpu.VMEM((RELS, WIDE, WIDE), F32),
            pltpu.VMEM((RELS, WIDE, WIDE), F32),
            pltpu.VMEM((dests, WIDE, WIDE), F32),
        ],
        compiler_params=pltpu.CompilerParams(vmem_limit_bytes=40 * 2**20),
        cost_estimate=pl.CostEstimate(flops=3 * 10**9, bytes_accessed=4 * 10**6, transcendentals=400000),
        name="attend",
    )(edges, queries, key_rows, value_rows, halo_keys, halo_values, grad_output, halo_rows, rel_weight, rel_prior)


def project_kernel(place, own_ref, inc_ref, nf_ref, types_ref, mine_out, theirs_out, masked_out, nft):
    rows = own_ref.shape[0]
    halo = inc_ref.shape[0]
    ids = inc_ref[:, 2 * WIDE :].astype(F32)
    nodes = lax.broadcasted_iota(jnp.int32, (halo, WIDE), 1).astype(F32)
    pick = jnp.concatenate(
        [(ids == nodes + float(j * WIDE)).astype(F32).astype(BF16) for j in range(rows // WIDE)], axis=1
    )
    back = mul(pick, inc_ref[:, : 2 * WIDE], TN)
    own = own_ref[...].astype(F32)
    parts = (own[:, :WIDE], own[:, WIDE : 2 * WIDE] + back[:, :WIDE], own[:, 2 * WIDE :] + back[:, WIDE:])
    kinds = jnp.concatenate(
        [column(types_ref[j : j + 1, :].astype(F32)) for j in range(rows // WIDE)], axis=0
    )
    for p in range(3):
        for t in range(TYPES):
            at = (p * TYPES + t) * WIDE
            masked_out[:, at : at + WIDE] = jnp.where(kinds == float(t), parts[p], 0.0).astype(BF16)
    nft[...] = jnp.transpose(nf_ref[...], (1, 0))
    even = place[0] == 0
    feats = nf_ref.shape[1]
    for j in range(PROJ):
        at = j * WIDE
        part = mul(nft[...], masked_out[:, at : at + WIDE], NN).reshape(feats // 16, 2, 8, WIDE)
        low = part[:, 0].reshape(feats // 2, WIDE)
        high = part[:, 1].reshape(feats // 2, WIDE)
        mine_out[:, at : at + WIDE] = jnp.where(even, low, high).astype(BF16)
        theirs_out[:, at : at + WIDE] = jnp.where(even, high, low).astype(BF16)


def project(place, own, incoming, node_feats, node_types):
    rows, feats = node_feats.shape
    return pl.pallas_call(
        project_kernel,
        out_shape=(
            jax.ShapeDtypeStruct((feats // 2, PROJ * WIDE), BF16),
            jax.ShapeDtypeStruct((feats // 2, PROJ * WIDE), BF16),
            jax.ShapeDtypeStruct((rows, PROJ * WIDE), BF16),
        ),
        in_specs=[SMEM] + [VMEM] * 4,
        out_specs=(VMEM, VMEM, VMEM),
        scratch_shapes=[pltpu.VMEM((feats, rows), BF16)],
        compiler_params=pltpu.CompilerParams(vmem_limit_bytes=40 * 2**20),
        cost_estimate=pl.CostEstimate(flops=10**9, bytes_accessed=4 * 10**6, transcendentals=0),
        name="project",
    )(place, own, incoming, node_feats, node_types)


def features_kernel(masked_ref, w_ref, out_ref):
    total = None
    for j in range(PROJ):
        at = j * WIDE
        term = mul(masked_ref[:, at : at + WIDE], w_ref[j], NT)
        total = term if total is None else total + term
    for h in range(out_ref.shape[0]):
        out_ref[h] = total[:, h * WIDE : (h + 1) * WIDE].astype(BF16)


def features(masked, weights):
    rows = masked.shape[0]
    feats = weights.shape[1]
    return pl.pallas_call(
        features_kernel,
        out_shape=jax.ShapeDtypeStruct((feats // WIDE, rows, WIDE), BF16),
        in_specs=[VMEM, VMEM],
        out_specs=VMEM,
        compiler_params=pltpu.CompilerParams(vmem_limit_bytes=40 * 2**20),
        cost_estimate=pl.CostEstimate(flops=10**9, bytes_accessed=3 * 10**6, transcendentals=0),
        name="features",
    )(masked, weights)


def pair_sum_kernel(place, mine_ref, got_ref, *outs):
    size = outs[0].shape[0]
    count = len(outs)
    for d in range(count):
        block = lax.rem(place[1] + d, count)
        at = pl.ds(pl.multiple_of(block * size, size), size)
        outs[d][...] = (mine_ref[at, :].astype(F32) + got_ref[at, :].astype(F32)).astype(BF16)


def pair_sum(place, mine, got, count):
    rows, columns = mine.shape
    return pl.pallas_call(
        pair_sum_kernel,
        out_shape=(jax.ShapeDtypeStruct((rows // count, columns), BF16),) * count,
        in_specs=[SMEM, VMEM, VMEM],
        out_specs=(VMEM,) * count,
        compiler_params=pltpu.CompilerParams(vmem_limit_bytes=40 * 2**20),
        cost_estimate=pl.CostEstimate(flops=10**6, bytes_accessed=3 * 10**6, transcendentals=0),
        name="pair_sum",
    )(place, mine, got)


def per_device(
    node_feats,
    node_types,
    queries,
    key_rows,
    value_rows,
    halo_keys,
    halo_values,
    halo_rows,
    edge_tiles,
    grad_output,
    proj_weight,
    rel_weight,
    rel_prior,
):
    nodes = ("y", "z", "core")
    y_count = lax.axis_size("y")
    z_count = lax.axis_size("z")
    slabs = y_count * z_count * 2
    place = jnp.stack([lax.axis_index("core"), lax.axis_index("y")]).astype(jnp.int32)
    own, send, rel = attend(
        edge_tiles.T,
        queries,
        key_rows,
        value_rows,
        halo_keys,
        halo_values,
        grad_output,
        halo_rows.reshape(-1, WIDE),
        rel_weight,
        rel_prior,
    )
    cap = send.shape[0] // slabs
    incoming = lax.all_to_all(send.reshape(slabs, cap, 3 * WIDE), nodes, 0, 0, tiled=True)
    rel_parts = lax.all_to_all(rel.reshape(slabs, -1, WIDE), nodes, 0, 0, tiled=True)
    mine, theirs, masked = project(
        place, own, incoming.reshape(-1, 3 * WIDE), node_feats, node_types.reshape(-1, WIDE)
    )
    got = lax.ppermute(theirs, "core", [(0, 1), (1, 0)])
    feat_parts = features(masked, proj_weight.reshape(PROJ, -1, WIDE))
    feat_got = lax.all_to_all(feat_parts, "heads", 0, 0, tiled=True)
    grad_feats = jnp.sum(feat_got.astype(F32), axis=0).astype(BF16)
    blocks = pair_sum(place, mine, got, y_count)
    arrived = [blocks[0]] + [
        lax.ppermute(blocks[d], "y", [(i, (i + d) % y_count) for i in range(y_count)])
        for d in range(1, y_count)
    ]
    by_z = sum(block.astype(F32) for block in arrived).astype(BF16)
    z_parts = lax.all_to_all(by_z.reshape(z_count, -1, PROJ * WIDE), "z", 0, 0, tiled=True)
    grad_proj = jnp.sum(z_parts.astype(F32), axis=0).reshape(-1, 3, TYPES, WIDE)

    rel_mine = jnp.sum(rel_parts.astype(F32), axis=0).astype(BF16)
    rel_all = lax.all_to_all(
        jnp.broadcast_to(rel_mine[None], (slabs,) + rel_mine.shape), nodes, 0, 0, tiled=True
    ).reshape(-1, WIDE)
    at = 2 * RELS * TILE
    grad_rel = rel_all[:at].astype(F32).reshape(2, RELS, TILE, 2, TILE).transpose(0, 1, 3, 2, 4)
    prior_all = rel_all[at : at + RELS].astype(F32) + rel_all[at + 16 : at + 16 + RELS].astype(F32)
    grad_prior = prior_all[:, ::TILE]
    return (grad_feats, grad_proj, grad_rel, grad_prior)


def solution(mesh):
    heads = mesh.devices.shape[1]
    split = Mesh(mesh.devices.reshape(4, 8, 2, heads), ("y", "z", "core", "heads"))
    nodes = ("y", "z", "core")
    return jax.shard_map(
        per_device,
        mesh=split,
        in_specs=(
            P(nodes, None),
            P(nodes),
            P(nodes, "heads"),
            P(nodes, "heads"),
            P(nodes, "heads"),
            P(nodes, "heads"),
            P(nodes, "heads"),
            P(nodes),
            P(nodes, None),
            P(nodes, "heads"),
            P(None, None, None, "heads"),
            P(None, None, "heads", None, None),
            P(None, "heads"),
        ),
        out_specs=(
            P(nodes, "heads"),
            P(nodes, None, None, "heads"),
            P(None, None, "heads", None, None),
            P(None, "heads"),
        ),
        check_vma=False,
    )
```

profile of v0, /device:TPU:1, one launch (start us, length us, event | category | flops | bytes accessed | tf_op | source)
XLA Modules:
  0.0 131.2 jit_solution(17828237706475300878)
XLA Ops:
  1.4 1.2 copy-done.1
  2.6 0.9 copy-done.3
  3.5 0.9 copy-done.4
  9.1 14.0 %attend.1 = (bf16[256,384]{1,0:T(8,128)(2,1)S(1)}, bf16[512,384]{1,0:T(8,128)(2,1)S(1)}, bf16[2048,128]{1,0:T(8,128)(2,1)}) custom-call(s32[3,40]{1,0:T(4,128)S(1)} %bitcast.17, bf16[256,128]{1,0:T(8,128)(2,1)S(1)} %copy-done.5, bf16[256,128]{1,0:T(8,128)(2,1)S(1)} %copy-done.6, bf16[256,128]{1,0:T(8,128)(2,1)S(1)} %copy-done.7, ...), custom_call_target="tpu_custom_call" | custom-call | flops 3000000000 | bytes 4000000 | tf_op jit(solution)/shard_map/attend/pallas_call | solution.py:167
  23.2 27.6 %all_to_all.25 = bf16[64,8,384]{2,1,0:T(8,128)(2,1)S(1)} all-to-all(bf16[64,8,384]{2,1,0:T(8,128)(2,1)S(1)} %bitcast.15), channel_id=1, replica_groups=mesh['y'=4,'z'=8,'core'=2,'heads'=4] {'y','z','core'}, dimensions={0} | all-to-all | bytes 786432 | tf_op jit(solution)/shard_map/all_to_all | solution.py:328
  50.7 6.4 %all-to-all-start.3 = ((bf16[64,32,128]{2,1,0:T(8,128)(2,1)}), bf16[64,32,128]{2,1,0:T(8,128)(2,1)}, u32[]{:S(2)}, u32[]{:S(2)}) async-start(bf16[64,32,128]{2,1,0:T(8,128)(2,1)} %bitcast.10), calls=%async_computation.3 | async-start | bytes 1048576 | tf_op jit(solution)/shard_map/all_to_all | solution.py:329
  57.2 2.0 %project.1 = (bf16[256,1920]{1,0:T(8,128)(2,1)S(1)}, bf16[256,1920]{1,0:T(8,128)(2,1)S(1)}, bf16[256,1920]{1,0:T(8,128)(2,1)S(1)}) custom-call(s32[2]{0:T(128)S(1)} %pad_add_fusion.place, bf16[256,384]{1,0:T(8,128)(2,1)S(1)} %get-tuple-element.14.own_ref, bf16[512,384]{1,0:T(8,128)(2,1)S(1)} %bitcast.14, bf16[256,512]{1,0:T(8,128)(2,1)S(1)} %copy-done.2, ...), custom_call_target="tpu_custom_call" | custom-call | flops 1000000000 | bytes 4000000 | tf_op jit(solution)/shard_map/project/pallas_call | solution.py:233
  59.8 1.5 %copy-done = bf16[3,5,512,128]{3,2,1,0:T(8,128)(2,1)S(1)} copy-done((bf16[3,5,512,128]{3,2,1,0:T(8,128)(2,1)S(1)}, bf16[3,5,512,128]{3,2,1,0:T(8,128)(2,1)}, u32[]{:S(2)}) %copy-start) | copy-done | bytes 1966104
  61.4 1.9 %features.1 = bf16[4,256,128]{2,1,0:T(8,128)(2,1)} custom-call(bf16[256,1920]{1,0:T(8,128)(2,1)S(1)} %get-tuple-element.16.masked_ref, bf16[15,512,128]{2,1,0:T(8,128)(2,1)S(1)} %bitcast.16), custom_call_target="tpu_custom_call" | custom-call | flops 1000000000 | bytes 3000000 | tf_op jit(solution)/shard_map/features/pallas_call | solution.py:262
  63.3 11.1 %all-to-all-done.3 = bf16[64,32,128]{2,1,0:T(8,128)(2,1)} async-done(((bf16[64,32,128]{2,1,0:T(8,128)(2,1)}), bf16[64,32,128]{2,1,0:T(8,128)(2,1)}, u32[]{:S(2)}, u32[]{:S(2)}) %all-to-all-start.3) | async-done | bytes 524320 | tf_op jit(solution)/shard_map/all_to_all | solution.py:329
  74.4 4.0 %all-to-all-start.1 = ((bf16[4,256,128]{2,1,0:T(8,128)(2,1)}), bf16[4,256,128]{2,1,0:T(8,128)(2,1)S(1)}, u32[]{:S(2)}, u32[]{:S(2)}) async-start(bf16[4,256,128]{2,1,0:T(8,128)(2,1)} %features.1), calls=%async_computation.1 | async-start | bytes 524288 | tf_op jit(solution)/shard_map/all_to_all | solution.py:335
  78.4 1.1 reduce_sum.35
  79.5 4.7 %all-to-all-done.1 = bf16[4,256,128]{2,1,0:T(8,128)(2,1)S(1)} async-done(((bf16[4,256,128]{2,1,0:T(8,128)(2,1)}), bf16[4,256,128]{2,1,0:T(8,128)(2,1)S(1)}, u32[]{:S(2)}, u32[]{:S(2)}) %all-to-all-start.1) | async-done | bytes 262176 | tf_op jit(solution)/shard_map/all_to_all | solution.py:335
  85.1 7.6 %all-to-all-start.4 = ((bf16[64,32,128]{2,1,0:T(8,128)(2,1)}), bf16[64,32,128]{2,1,0:T(8,128)(2,1)}, u32[]{:S(2)}, u32[]{:S(2)}) async-start(bf16[64,32,128]{2,1,0:T(8,128)(2,1)} %broadcast_in_dim.2), calls=%async_computation.4 | async-start | bytes 1048576 | tf_op jit(solution)/shard_map/all_to_all | solution.py:347
  93.5 1.5 %collective-permute-start.1 = (bf16[64,1920]{1,0:T(8,128)(2,1)S(1)}, bf16[64,1920]{1,0:T(8,128)(2,1)S(1)}, u32[]{:S(2)}, u32[]{:S(2)}) collective-permute-start(bf16[64,1920]{1,0:T(8,128)(2,1)S(1)} %get-tuple-element.20), channel_id=1, source_target_pairs={{0,64},{64,128},{128,192},{192,0},{1,65},{65,129},{129,193},{193,1... | collective-permute-start | bytes 737288 | tf_op jit(solution)/shard_map/ppermute | solution.py:339
  95.0 2.6 %collective-permute-start.2 = (bf16[64,1920]{1,0:T(8,128)(2,1)S(1)}, bf16[64,1920]{1,0:T(8,128)(2,1)S(1)}, u32[]{:S(2)}, u32[]{:S(2)}) collective-permute-start(bf16[64,1920]{1,0:T(8,128)(2,1)S(1)} %get-tuple-element.21), channel_id=1, source_target_pairs={{0,128},{64,192},{128,0},{192,64},{1,129},{65,193},{129,1},{193,65... | collective-permute-start | bytes 737288 | tf_op jit(solution)/shard_map/ppermute | solution.py:339
  97.6 1.1 collective-permute-start.3
  99.3 6.2 %collective-permute-done.1 = bf16[64,1920]{1,0:T(8,128)(2,1)S(1)} collective-permute-done((bf16[64,1920]{1,0:T(8,128)(2,1)S(1)}, bf16[64,1920]{1,0:T(8,128)(2,1)S(1)}, u32[]{:S(2)}, u32[]{:S(2)}) %collective-permute-start.1) | collective-permute-done | bytes 245792 | tf_op jit(solution)/shard_map/ppermute | solution.py:339
  105.5 8.0 %collective-permute-done.2 = bf16[64,1920]{1,0:T(8,128)(2,1)S(1)} collective-permute-done((bf16[64,1920]{1,0:T(8,128)(2,1)S(1)}, bf16[64,1920]{1,0:T(8,128)(2,1)S(1)}, u32[]{:S(2)}, u32[]{:S(2)}) %collective-permute-start.2) | collective-permute-done | bytes 245792 | tf_op jit(solution)/shard_map/ppermute | solution.py:339
  114.3 6.2 %all-to-all-start.2 = ((bf16[8,8,1920]{2,1,0:T(8,128)(2,1)}), bf16[8,8,1920]{2,1,0:T(8,128)(2,1)S(1)}, u32[]{:S(2)}, u32[]{:S(2)}) async-start(bf16[8,8,1920]{2,1,0:T(8,128)(2,1)} %fusion), calls=%async_computation.2 | async-start | bytes 491520 | tf_op jit(solution)/shard_map/all_to_all | solution.py:343
  120.5 1.1 slice_convert_fusion
  121.6 1.1 reshape.50
  122.8 1.5 %copy.19 = f32[2,15,2,64,64]{4,3,2,1,0:T(8,128)} copy(f32[2,15,2,64,64]{4,2,3,1,0:T(2,128)S(1)} %bitcast.20) | data formatting | bytes 1966080
  125.7 4.8 %all-to-all-done.2 = bf16[8,8,1920]{2,1,0:T(8,128)(2,1)S(1)} async-done(((bf16[8,8,1920]{2,1,0:T(8,128)(2,1)}), bf16[8,8,1920]{2,1,0:T(8,128)(2,1)S(1)}, u32[]{:S(2)}, u32[]{:S(2)}) %all-to-all-start.2) | async-done | bytes 245792 | tf_op jit(solution)/shard_map/all_to_all | solution.py:343
  (34 shorter events, 11.4 us)
Async XLA Ops:
  1.4 1.2 copy-start.1
  2.6 0.9 copy-start.3
  3.5 0.9 copy-start.4
  4.4 0.8 copy-start.5
  5.2 0.8 copy-start.6
  6.1 0.8 copy-start.7
  6.9 0.8 copy-start.8
  7.8 0.7 copy-start.9
  8.5 0.7 copy-start.10
  9.1 48.1 %copy-start.2 = (bf16[256,512]{1,0:T(8,128)(2,1)S(1)}, bf16[256,512]{1,0:T(8,128)(2,1)}, u32[]{:S(2)}) copy-start(bf16[256,512]{1,0:T(8,128)(2,1)} %nf_ref.1) | copy-start | bytes 786436
  9.1 48.1 %copy-start.11 = (s32[256]{0:T(256)S(1)}, s32[256]{0:T(256)}, u32[]{:S(2)}) copy-start(s32[256]{0:T(256)} %param.14) | copy-start | bytes 3076
  50.7 23.6 %all-to-all-start.3 = ((bf16[64,32,128]{2,1,0:T(8,128)(2,1)}), bf16[64,32,128]{2,1,0:T(8,128)(2,1)}, u32[]{:S(2)}, u32[]{:S(2)}) async-start(bf16[64,32,128]{2,1,0:T(8,128)(2,1)} %bitcast.10), calls=%async_computation.3 | async-start | bytes 1048576 | tf_op jit(solution)/shard_map/all_to_all | solution.py:329
  59.2 33.5 %collective-permute-start = (bf16[256,1920]{1,0:T(8,128)(2,1)S(1)}, bf16[256,1920]{1,0:T(8,128)(2,1)S(1)}, u32[]{:S(2)}, u32[]{:S(2)}) collective-permute-start(bf16[256,1920]{1,0:T(8,128)(2,1)S(1)} %get-tuple-element.18), channel_id=1, source_target_pairs={{0,4},{4,0},{1,5},{5,1},{2,6},{6,2},{3,7},{7,3},{8,12},{12,8},{9,1... | collective-permute-start | bytes 2949128 | tf_op jit(solution)/shard_map/ppermute | solution.py:333
  59.8 1.5 %copy-start = (bf16[3,5,512,128]{3,2,1,0:T(8,128)(2,1)S(1)}, bf16[3,5,512,128]{3,2,1,0:T(8,128)(2,1)}, u32[]{:S(2)}) copy-start(bf16[3,5,512,128]{3,2,1,0:T(8,128)(2,1)} %param.23) | copy-start | bytes 5898244
  74.4 9.9 %all-to-all-start.1 = ((bf16[4,256,128]{2,1,0:T(8,128)(2,1)}), bf16[4,256,128]{2,1,0:T(8,128)(2,1)S(1)}, u32[]{:S(2)}, u32[]{:S(2)}) async-start(bf16[4,256,128]{2,1,0:T(8,128)(2,1)} %features.1), calls=%async_computation.1 | async-start | bytes 524288 | tf_op jit(solution)/shard_map/all_to_all | solution.py:335
  85.1 29.2 %all-to-all-start.4 = ((bf16[64,32,128]{2,1,0:T(8,128)(2,1)}), bf16[64,32,128]{2,1,0:T(8,128)(2,1)}, u32[]{:S(2)}, u32[]{:S(2)}) async-start(bf16[64,32,128]{2,1,0:T(8,128)(2,1)} %broadcast_in_dim.2), calls=%async_computation.4 | async-start | bytes 1048576 | tf_op jit(solution)/shard_map/all_to_all | solution.py:347
  93.5 12.0 %collective-permute-start.1 = (bf16[64,1920]{1,0:T(8,128)(2,1)S(1)}, bf16[64,1920]{1,0:T(8,128)(2,1)S(1)}, u32[]{:S(2)}, u32[]{:S(2)}) collective-permute-start(bf16[64,1920]{1,0:T(8,128)(2,1)S(1)} %get-tuple-element.20), channel_id=1, source_target_pairs={{0,64},{64,128},{128,192},{192,0},{1,65},{65,129},{129,193},{193,1... | collective-permute-start | bytes 737288 | tf_op jit(solution)/shard_map/ppermute | solution.py:339
  95.0 18.5 %collective-permute-start.2 = (bf16[64,1920]{1,0:T(8,128)(2,1)S(1)}, bf16[64,1920]{1,0:T(8,128)(2,1)S(1)}, u32[]{:S(2)}, u32[]{:S(2)}) collective-permute-start(bf16[64,1920]{1,0:T(8,128)(2,1)S(1)} %get-tuple-element.21), channel_id=1, source_target_pairs={{0,128},{64,192},{128,0},{192,64},{1,129},{65,193},{129,1},{193,65... | collective-permute-start | bytes 737288 | tf_op jit(solution)/shard_map/ppermute | solution.py:339
  97.6 15.9 %collective-permute-start.3 = (bf16[64,1920]{1,0:T(8,128)(2,1)S(1)}, bf16[64,1920]{1,0:T(8,128)(2,1)S(1)}, u32[]{:S(2)}, u32[]{:S(2)}) collective-permute-start(bf16[64,1920]{1,0:T(8,128)(2,1)S(1)} %get-tuple-element.22), channel_id=1, source_target_pairs={{0,192},{64,0},{128,64},{192,128},{1,193},{65,1},{129,65},{193,129... | collective-permute-start | bytes 737288 | tf_op jit(solution)/shard_map/ppermute | solution.py:339
  114.3 16.1 %all-to-all-start.2 = ((bf16[8,8,1920]{2,1,0:T(8,128)(2,1)}), bf16[8,8,1920]{2,1,0:T(8,128)(2,1)S(1)}, u32[]{:S(2)}, u32[]{:S(2)}) async-start(bf16[8,8,1920]{2,1,0:T(8,128)(2,1)} %fusion), calls=%async_computation.2 | async-start | bytes 491520 | tf_op jit(solution)/shard_map/all_to_all | solution.py:343
where the time goes:
time: 132 us; the launch traced here: 131 us
  waiting for transfers between devices  34.8 us (26%)
  starting transfers between devices  29.9 us (23%)
  blocking collectives  27.6 us (21%)
  Pallas kernels  18.7 us (14%)
  local copies, waits for them, and re-layouts  14.3 us (11%)
  other arithmetic  5.21 us (4%)
    all_to_all x1, blocking collectives, per_device(): lax.all_to_all(send.reshape(slabs, cap, 3 * WIDE), nodes, 0, 0, tiled=True)  27.6 us
    ppermute x3, waiting for transfers between devices, per_device(): lax.ppermute(blocks[d], 'y', [(i, (i + d) % y_count) for i in range(y_cou...  14.2 us
    pallas_call x1, Pallas kernels, attend(): pl.pallas_call(attend_kernel, out_shape=(jax.ShapeDtypeStruct((rows, 3 *...  14 us
    unnamed x27, local copies, waits for them, and re-layouts  12.2 us
    all_to_all x1, waiting for transfers between devices, per_device(): lax.all_to_all(rel.reshape(slabs, -1, WIDE), nodes, 0, 0, tiled=True)  11.1 us
    all_to_all x1, starting transfers between devices, per_device(): lax.all_to_all(jnp.broadcast_to(rel_mine[None], (slabs,) + rel_mine.shape...  7.57 us
    all_to_all x1, starting transfers between devices, per_device(): lax.all_to_all(rel.reshape(slabs, -1, WIDE), nodes, 0, 0, tiled=True)  6.39 us
    all_to_all x1, starting transfers between devices, per_device(): lax.all_to_all(by_z.reshape(z_count, -1, PROJ * WIDE), 'z', 0, 0, tiled=T...  6.15 us
  transfers between devices with their start and end apart: 8, of which 5 were waited for; matrix products, arithmetic and copies ran while one was open for 7% of the time, Pallas kernels for 4%

commit v1 on v0

v1 whole, which is shorter than its diff:
```python
import jax
import jax.numpy as jnp
from jax import lax
from jax.experimental import pallas as pl
from jax.experimental.pallas import tpu as pltpu
from jax.sharding import Mesh, PartitionSpec as P

TYPES = 5
RELS = 15
TILE = 64
WIDE = 128
GROUP = 8
PROJ = 3 * TYPES

F32 = jnp.float32
BF16 = jnp.bfloat16
NN = (((1,), (0,)), ((), ()))
NT = (((1,), (1,)), ((), ()))
TN = (((0,), (0,)), ((), ()))
VMEM = pl.BlockSpec(memory_space=pltpu.VMEM)
SMEM = pl.BlockSpec(memory_space=pltpu.SMEM)
HBM = pl.BlockSpec(memory_space=pltpu.HBM)
HALO_ROWS = 16
REL_ROWS = 30
BLOCK = 48
LIMIT = 24 * 2**20
MOST = 62 * 2**20


def mul(left, right, dims):
    return lax.dot_general(left, right, dims, preferred_element_type=F32)


def column(row):
    return jnp.transpose(jnp.broadcast_to(row, (WIDE, WIDE)), (1, 0))


def attend_kernel(
    edges_hbm, prior_hbm, q_hbm, g_hbm, ko_hbm, vo_hbm, kh_hbm, vh_hbm, rel_hbm, rows_hbm,
    own_out, send_out,
    edges, prior_in, q_ref, g_ref, rel_ref, rows_ref, k_ref, v_ref, sems,
    wbd, qg, keep, prior, kvm, probs, exps, logs, grads,
    denom, delta, dprior, dkv, dwk, dwv, dq, drel,
):
    count = edges.shape[1]
    own = ko_hbm.shape[0]
    dests = own // TILE
    own_tiles = own // TILE
    halo_tiles = kh_hbm.shape[0] // TILE
    slabs = send_out.shape[0]
    copies = [
        pltpu.make_async_copy(source, target, sems.at[i])
        for i, (source, target) in enumerate(
            (
                (rel_hbm, rel_ref),
                (q_hbm, q_ref),
                (g_hbm, g_ref),
                (rows_hbm, rows_ref),
                (edges_hbm, edges),
                (prior_hbm, prior_in),
                (ko_hbm, k_ref.at[:own]),
                (vo_hbm, v_ref.at[:own]),
                (kh_hbm, k_ref.at[own:]),
                (vh_hbm, v_ref.at[own:]),
            )
        )
    ]
    for copy in copies:
        copy.start()

    lane = lax.broadcasted_iota(jnp.int32, (TILE, WIDE), 1)
    first = lane < TILE
    wbd[...] = jnp.zeros_like(wbd)
    denom[...] = jnp.zeros_like(denom)
    delta[...] = jnp.zeros_like(delta)
    dprior[...] = jnp.zeros_like(dprior)
    dkv[...] = jnp.zeros_like(dkv)
    dwk[...] = jnp.zeros_like(dwk)
    dwv[...] = jnp.zeros_like(dwv)
    dq[...] = jnp.zeros_like(dq)
    for copy in copies:
        copy.wait()

    for r in range(RELS):
        for w in range(2):
            for h in range(2):
                at = (2 * w + h) * TILE
                wbd[r, at : at + TILE, at : at + TILE] = rel_ref[w, r, h]
    none = jnp.zeros((TILE, WIDE), BF16)
    for a in range(dests):
        q = q_ref[a * TILE : (a + 1) * TILE, :].astype(F32) * 0.125
        g = g_ref[a * TILE : (a + 1) * TILE, :].astype(F32)
        for h in range(2):
            mine = first if h == 0 else jnp.logical_not(first)
            qg[a, h * TILE : (h + 1) * TILE, :WIDE] = jnp.where(mine, q, 0.0).astype(BF16)
            qg[a, h * TILE : (h + 1) * TILE, WIDE:] = none
            qg[a, (2 + h) * TILE : (3 + h) * TILE, :WIDE] = none
            qg[a, (2 + h) * TILE : (3 + h) * TILE, WIDE:] = jnp.where(mine, g, 0.0).astype(BF16)
    for b in range(own_tiles):
        keep[b] = jnp.ones((TILE, WIDE), F32)
    period = lax.broadcasted_iota(jnp.int32, (16, 8, WIDE), 2) % 8
    slot = lax.broadcasted_iota(jnp.int32, (16, 8, WIDE), 1)
    for j in range(halo_tiles // 2):
        ids = column(rows_ref[j : j + 1, :].astype(F32))
        ok = (ids < float(own)).astype(F32)
        keep[own_tiles + 2 * j] = ok[:TILE]
        keep[own_tiles + 2 * j + 1] = ok[TILE:]
        tiled = jnp.sum(jnp.where(period == slot, ids.reshape(16, 8, WIDE), 0.0), axis=1)
        drel[2 * RELS * TILE + 16 + 16 * j : 2 * RELS * TILE + 32 + 16 * j, :] = tiled
    one_lane = lax.broadcasted_iota(jnp.int32, (1, WIDE), 1)
    for r in range(RELS):
        prior[r : r + 1, :] = jnp.where(one_lane < TILE, prior_in[0, r], prior_in[1, r])

    def entry(e):
        target = edges[0, e]
        return jnp.minimum(target, dests - 1), edges[1, e], edges[2, e], target < dests

    def rows(b):
        return pl.ds(pl.multiple_of(b * TILE, TILE), TILE)

    def scores(step, carry):
        for u in range(GROUP):
            e = step * GROUP + u
            a, b, r, live = entry(e)
            pair = jnp.concatenate([k_ref[rows(b), :], v_ref[rows(b), :]], axis=1)
            mixed = mul(pair, wbd[r], NN).astype(BF16)
            kvm[e] = mixed
            both = mul(mixed, qg[a], NT)
            logits = both[:, :WIDE]
            logs[e] = logits
            grads[e] = both[:, WIDE:]
            ex = jnp.exp(prior[pl.ds(r, 1), :] * logits) * (keep[b] * live.astype(F32))
            exps[e] = ex
            denom[a] += jnp.sum(ex, axis=0, keepdims=True)
        return carry

    lax.fori_loop(0, count // GROUP, scores, 0)
    denom[...] = 1.0 / denom[...]

    def normalise(step, carry):
        for u in range(GROUP):
            e = step * GROUP + u
            a, b, r, live = entry(e)
            soft = exps[e] * denom[a]
            exps[e] = soft
            prob = soft.astype(BF16)
            probs[e] = prob
            delta[a] += jnp.sum(prob.astype(F32) * grads[e], axis=0, keepdims=True)
        return carry

    lax.fori_loop(0, count // GROUP, normalise, 0)

    def backward(step, carry):
        for u in range(GROUP):
            e = step * GROUP + u
            a, b, r, live = entry(e)
            score_grad = exps[e] * (grads[e] - delta[a])
            dprior[pl.ds(r, 1), :] += jnp.sum(score_grad * logs[e], axis=0, keepdims=True)
            lgrad = (score_grad * prior[pl.ds(r, 1), :]).astype(BF16)
            pair = jnp.concatenate([lgrad, probs[e]], axis=1)
            mixed_grad = mul(pair, qg[a], NN).astype(BF16)
            dkv[b] += mul(mixed_grad, wbd[r], NT)
            dwk[r] += mul(k_ref[rows(b), :], mixed_grad[:, :WIDE], TN)
            dwv[r] += mul(v_ref[rows(b), :], mixed_grad[:, WIDE:], TN)
            dq[a] += mul(lgrad, kvm[e, :, :WIDE], TN)
        return carry

    lax.fori_loop(0, count // GROUP, backward, 0)

    for a in range(dests):
        grad = jnp.where(first, dq[a, :TILE, :], dq[a, TILE:, :]) * 0.125
        own_out[a * TILE : (a + 1) * TILE, :WIDE] = grad.astype(BF16)
    for b in range(own_tiles):
        own_out[b * TILE : (b + 1) * TILE, WIDE:] = dkv[b].astype(BF16)
    for b in range(halo_tiles):
        back = dkv[own_tiles + b]
        block = jnp.concatenate(
            [back[:, :WIDE].reshape(8, 8, WIDE), back[:, WIDE:].reshape(8, 8, WIDE)], axis=1
        )
        send_out[8 * b : 8 * b + 8, :HALO_ROWS, :] = block.astype(BF16)
    for w, ref in enumerate((dwk, dwv)):
        for r in range(RELS):
            at = (w * RELS + r) * TILE
            drel[at : at + TILE, :] = jnp.where(first, ref[r, :TILE, :], ref[r, TILE:, :])
    sums = dprior[...]
    spot = lax.broadcasted_iota(jnp.int32, sums.shape, 1)
    row = lax.broadcasted_iota(jnp.int32, sums.shape, 0)
    one = jnp.sum(jnp.where(spot < TILE, sums, 0.0), axis=1, keepdims=True)
    two = jnp.sum(jnp.where(spot < TILE, 0.0, sums), axis=1, keepdims=True)
    chosen = jnp.where((spot // 16) % 2 == 0, one, two)
    line = jnp.sum(jnp.where(spot % 16 == row, chosen, 0.0), axis=0, keepdims=True)
    high = line.astype(BF16).astype(F32)
    line = jnp.where(one_lane < 32, high, line - high)
    within = lax.broadcasted_iota(jnp.int32, (32, WIDE), 0)
    for p in range(slabs):
        at = 2 * RELS * TILE + 16 + p
        block = jnp.where(
            within < REL_ROWS,
            drel[REL_ROWS * p : REL_ROWS * p + 32, :],
            jnp.where(within == REL_ROWS, drel[at : at + 1, :], line),
        )
        send_out[p, HALO_ROWS:, :] = block.astype(BF16)


def attend(edges, rel_prior, queries, grad_output, key_rows, value_rows, halo_keys, halo_values, rel_weight, halo_rows):
    rows = queries.shape[0]
    halo = halo_keys.shape[0]
    dests = rows // TILE
    sources = (rows + halo) // TILE
    count = edges.shape[1]
    slabs = 64
    return pl.pallas_call(
        attend_kernel,
        out_shape=(
            jax.ShapeDtypeStruct((rows, 3 * WIDE), BF16),
            jax.ShapeDtypeStruct((slabs, BLOCK, WIDE), BF16),
        ),
        in_specs=[HBM] * 10,
        out_specs=(VMEM, VMEM),
        scratch_shapes=[
            pltpu.SMEM(edges.shape, jnp.int32),
            pltpu.SMEM(rel_prior.shape, F32),
            pltpu.VMEM(queries.shape, BF16),
            pltpu.VMEM(grad_output.shape, BF16),
            pltpu.VMEM(rel_weight.shape, BF16),
            pltpu.VMEM(halo_rows.shape, jnp.int32),
            pltpu.VMEM((rows + halo, WIDE), BF16),
            pltpu.VMEM((rows + halo, WIDE), BF16),
            pltpu.SemaphoreType.DMA((10,)),
            pltpu.VMEM((RELS, 2 * WIDE, 2 * WIDE), BF16),
            pltpu.VMEM((dests, 2 * WIDE, 2 * WIDE), BF16),
            pltpu.VMEM((sources, TILE, WIDE), F32),
            pltpu.VMEM((16, WIDE), F32),
            pltpu.VMEM((count, TILE, 2 * WIDE), BF16),
            pltpu.VMEM((count, TILE, WIDE), BF16),
            pltpu.VMEM((count, TILE, WIDE), F32),
            pltpu.VMEM((count, TILE, WIDE), F32),
            pltpu.VMEM((count, TILE, WIDE), F32),
            pltpu.VMEM((dests, 1, WIDE), F32),
            pltpu.VMEM((dests, 1, WIDE), F32),
            pltpu.VMEM((16, WIDE), F32),
            pltpu.VMEM((sources, TILE, 2 * WIDE), F32),
            pltpu.VMEM((RELS, WIDE, WIDE), F32),
            pltpu.VMEM((RELS, WIDE, WIDE), F32),
            pltpu.VMEM((dests, WIDE, WIDE), F32),
            pltpu.VMEM((2 * RELS * TILE + 16 + slabs, WIDE), F32),
        ],
        compiler_params=pltpu.CompilerParams(vmem_limit_bytes=MOST),
        cost_estimate=pl.CostEstimate(flops=3 * 10**9, bytes_accessed=4 * 10**6, transcendentals=400000),
        name="attend",
    )(edges, rel_prior, queries, grad_output, key_rows, value_rows, halo_keys, halo_values, rel_weight, halo_rows)


def bundle_kernel(place, own_ref, nf_ref, types_ref, mine_out, send_out):
    rows, feats = nf_ref.shape
    turned = jnp.transpose(nf_ref[...], (1, 0)).astype(F32).reshape(feats // 16, 2, 8, rows)
    low = turned[:, 0].reshape(feats // 2, rows)
    high = turned[:, 1].reshape(feats // 2, rows)
    even = place[0] == 0
    mine_out[...] = jnp.where(even, low, high).astype(BF16)
    send_out[:, :rows] = jnp.where(even, high, low).astype(BF16)
    send_out[:, rows : rows + WIDE] = own_ref[:, :WIDE]
    for j in range(rows // WIDE):
        kinds = column(types_ref[j : j + 1, :].astype(F32)).astype(BF16)
        send_out[j * WIDE : (j + 1) * WIDE, rows + WIDE :] = kinds


def bundle(place, own, node_feats, node_types):
    rows, feats = node_feats.shape
    return pl.pallas_call(
        bundle_kernel,
        out_shape=(
            jax.ShapeDtypeStruct((feats // 2, rows), BF16),
            jax.ShapeDtypeStruct((feats // 2, rows + 2 * WIDE), BF16),
        ),
        in_specs=[SMEM] + [VMEM] * 3,
        out_specs=(VMEM,) * 2,
        compiler_params=pltpu.CompilerParams(vmem_limit_bytes=LIMIT),
        cost_estimate=pl.CostEstimate(flops=10**6, bytes_accessed=2 * 10**6, transcendentals=0),
        name="bundle",
    )(place, own, node_feats, node_types)


def spread(place, products, outs):
    size = outs[0].shape[0]
    for d in range(len(outs)):
        block = lax.rem(place[1] + d, len(outs))
        outs[d][...] = products[pl.ds(pl.multiple_of(block * size, size), size), :]


def project_queries_kernel(place, mine_ref, sent_ref, got_ref, pair_out, *refs):
    outs, products = refs[:-1], refs[-1]
    rows = mine_ref.shape[1]
    pair_out[:, :rows] = mine_ref[...]
    pair_out[:, rows:] = got_ref[:, :rows]
    query = jnp.concatenate([ref[:, rows : rows + WIDE] for ref in (sent_ref, got_ref)], axis=0).astype(F32)
    kinds = jnp.concatenate([ref[:, rows + WIDE :] for ref in (sent_ref, got_ref)], axis=0).astype(F32)
    for t in range(TYPES):
        masked = jnp.where(kinds == float(t), query, 0.0).astype(BF16)
        products[:, t * WIDE : (t + 1) * WIDE] = mul(pair_out[...], masked, NN).astype(BF16)
    spread(place, products, outs)


def project_queries(place, mine, sent, got, count):
    feats, rows = mine.shape
    wide = TYPES * WIDE
    return pl.pallas_call(
        project_queries_kernel,
        out_shape=(jax.ShapeDtypeStruct((feats, 2 * rows), BF16),)
        + (jax.ShapeDtypeStruct((feats // count, wide), BF16),) * count,
        in_specs=[SMEM] + [VMEM] * 3,
        out_specs=(VMEM,) * (1 + count),
        scratch_shapes=[pltpu.VMEM((feats, wide), BF16)],
        compiler_params=pltpu.CompilerParams(vmem_limit_bytes=LIMIT),
        cost_estimate=pl.CostEstimate(flops=10**9, bytes_accessed=2 * 10**6, transcendentals=0),
        name="project_queries",
    )(place, mine, sent, got)


def collect_kernel(own_ref, inc_hbm, kv_out, rel_out, prior_out, inc_ref, sems):
    rows = own_ref.shape[0]
    slabs = inc_ref.shape[0]
    copies = [
        pltpu.make_async_copy(inc_hbm.at[pl.ds(16 * c, 16)], inc_ref.at[pl.ds(16 * c, 16)], sems.at[c])
        for c in range(slabs // 16)
    ]
    for copy in copies:
        copy.start()
    row = lax.broadcasted_iota(jnp.int32, (16, WIDE), 0)
    block = lax.broadcasted_iota(jnp.int32, (16, WIDE), 1) // 8
    node = lax.broadcasted_iota(jnp.int32, (rows, WIDE), 0).astype(F32)
    back = own_ref[:, WIDE:].astype(F32)
    total = None
    for c, copy in enumerate(copies):
        copy.wait()
        ids = inc_ref[16 * c : 16 * c + 16, HALO_ROWS + REL_ROWS - 14 :, :].astype(F32)[:, 14, :]
        line = jnp.sum(jnp.where(row == block, ids, 0.0), axis=0, keepdims=True)
        pick = (node == line).astype(F32).astype(BF16)
        grads = inc_ref[16 * c : 16 * c + 16, :HALO_ROWS, :].astype(F32)
        both = jnp.concatenate(
            [grads[:, :8].reshape(WIDE, WIDE), grads[:, 8:].reshape(WIDE, WIDE)], axis=1
        )
        back = back + mul(pick, both.astype(BF16), NN)
        for s in range(16 * c, 16 * c + 16):
            term = inc_ref[s, HALO_ROWS:, :].astype(F32)
            total = term if total is None else total + term
    kv_out[...] = back.astype(BF16)
    for s in range(rel_out.shape[0]):
        rel_out[s] = total.astype(BF16)
    line = total[REL_ROWS + 1 : REL_ROWS + 2, :]
    line = line + pltpu.roll(line, WIDE - 32, 1)
    prior_out[0:1, :] = line[:, :RELS]
    prior_out[1:2, :] = pltpu.roll(line, WIDE - 16, 1)[:, :RELS]


def collect(own, incoming):
    rows = own.shape[0]
    slabs = incoming.shape[0]
    return pl.pallas_call(
        collect_kernel,
        out_shape=(
            jax.ShapeDtypeStruct((rows, 2 * WIDE), BF16),
            jax.ShapeDtypeStruct((slabs // 2, 32, WIDE), BF16),
            jax.ShapeDtypeStruct((2, RELS), F32),
        ),
        in_specs=[VMEM, HBM],
        out_specs=(VMEM,) * 3,
        scratch_shapes=[pltpu.VMEM(incoming.shape, BF16), pltpu.SemaphoreType.DMA((slabs // 16,))],
        compiler_params=pltpu.CompilerParams(vmem_limit_bytes=LIMIT),
        cost_estimate=pl.CostEstimate(flops=10**8, bytes_accessed=2 * 10**6, transcendentals=0),
        name="collect",
    )(own, incoming)


def project_kernel(place, pair_ref, kv_ref, got_kv_ref, sent_ref, got_ref, *refs):
    outs, products = refs[:-1], refs[-1]
    rows = kv_ref.shape[0]
    kinds = jnp.concatenate([ref[:, rows + WIDE :] for ref in (sent_ref, got_ref)], axis=0).astype(F32)
    for p in range(2):
        part = jnp.concatenate(
            [ref[:, p * WIDE : (p + 1) * WIDE] for ref in (kv_ref, got_kv_ref)], axis=0
        ).astype(F32)
        for t in range(TYPES):
            at = (p * TYPES + t) * WIDE
            masked = jnp.where(kinds == float(t), part, 0.0).astype(BF16)
            products[:, at : at + WIDE] = mul(pair_ref[...], masked, NN).astype(BF16)
    spread(place, products, outs)


def project(place, pair, kv, got_kv, sent, got, count):
    feats = pair.shape[0]
    wide = 2 * TYPES * WIDE
    return pl.pallas_call(
        project_kernel,
        out_shape=(jax.ShapeDtypeStruct((feats // count, wide), BF16),) * count,
        in_specs=[SMEM] + [VMEM] * 5,
        out_specs=(VMEM,) * count,
        scratch_shapes=[pltpu.VMEM((feats, wide), BF16)],
        compiler_params=pltpu.CompilerParams(vmem_limit_bytes=LIMIT),
        cost_estimate=pl.CostEstimate(flops=10**9, bytes_accessed=4 * 10**6, transcendentals=0),
        name="project",
    )(place, pair, kv, got_kv, sent, got)


def features_kernel(place, sent_ref, kv_ref, w_ref, *refs):
    outs, total = refs[:-1], refs[-1]
    rows = kv_ref.shape[0]
    kinds = sent_ref[:, rows + WIDE :].astype(F32)
    acc = None
    for p in range(3):
        part = sent_ref[:, rows : rows + WIDE] if p == 0 else kv_ref[:, (p - 1) * WIDE : p * WIDE]
        part = part.astype(F32)
        for t in range(TYPES):
            masked = jnp.where(kinds == float(t), part, 0.0).astype(BF16)
            term = mul(masked, w_ref[p * TYPES + t], NT)
            acc = term if acc is None else acc + term
    for h in range(len(outs)):
        total[h] = acc[:, h * WIDE : (h + 1) * WIDE]
    for d in range(len(outs)):
        outs[d][...] = total[lax.rem(place[2] + d, len(outs))].astype(BF16)


def features(place, sent, kv, weights):
    rows = kv.shape[0]
    count = weights.shape[1] // WIDE
    return pl.pallas_call(
        features_kernel,
        out_shape=(jax.ShapeDtypeStruct((rows, WIDE), BF16),) * count,
        in_specs=[SMEM, VMEM, VMEM, VMEM],
        out_specs=(VMEM,) * count,
        scratch_shapes=[pltpu.VMEM((count, rows, WIDE), F32)],
        compiler_params=pltpu.CompilerParams(vmem_limit_bytes=LIMIT),
        cost_estimate=pl.CostEstimate(flops=10**9, bytes_accessed=3 * 10**6, transcendentals=0),
        name="features",
    )(place, sent, kv, weights)


def relation_kernel(place, mine_ref, other_ref, out_ref, flat):
    even = place[0] == 0
    for s in range(mine_ref.shape[0]):
        mine = mine_ref[s].astype(F32)
        other = other_ref[s].astype(F32)
        at = 2 * s * REL_ROWS
        flat[at : at + 32, :] = jnp.where(even, mine, other)
        flat[at + REL_ROWS : at + REL_ROWS + 32, :] = jnp.where(even, other, mine)
    for w in range(2):
        for r in range(RELS):
            at = (w * RELS + r) * TILE
            for h in range(2):
                out_ref[w, r, h] = flat[at : at + TILE, h * TILE : (h + 1) * TILE]


def relations(place, mine, other):
    return pl.pallas_call(
        relation_kernel,
        out_shape=jax.ShapeDtypeStruct((2, RELS, 2, TILE, TILE), F32),
        in_specs=[SMEM, VMEM, VMEM],
        out_specs=VMEM,
        scratch_shapes=[pltpu.VMEM((2 * RELS * TILE + 8, WIDE), F32)],
        compiler_params=pltpu.CompilerParams(vmem_limit_bytes=LIMIT),
        cost_estimate=pl.CostEstimate(flops=10**6, bytes_accessed=3 * 10**6, transcendentals=0),
        name="relations",
    )(place, mine, other)


def place_sum_kernel(*refs):
    out = refs[-1]
    half = (len(refs) - 1) // 2
    narrow = refs[0].shape[1]
    for at, group in ((0, refs[:half]), (narrow, refs[half:-1])):
        total = group[0][...].astype(F32)
        for ref in group[1:]:
            total = total + ref[...].astype(F32)
        out[:, at : at + total.shape[1]] = total.astype(BF16)


def place_sum(query, rest):
    rows = query[0].shape[0]
    return pl.pallas_call(
        place_sum_kernel,
        out_shape=jax.ShapeDtypeStruct((rows, PROJ * WIDE), BF16),
        in_specs=[VMEM] * (len(query) + len(rest)),
        out_specs=VMEM,
        compiler_params=pltpu.CompilerParams(vmem_limit_bytes=LIMIT),
        cost_estimate=pl.CostEstimate(flops=10**6, bytes_accessed=10**6, transcendentals=0),
        name="place_sum",
    )(*query, *rest)


def shifted(blocks, axis):
    count = len(blocks)
    return [blocks[0]] + [
        lax.ppermute(blocks[d], axis, [(i, (i + d) % count) for i in range(count)])
        for d in range(1, count)
    ]


def per_device(
    node_feats,
    node_types,
    queries,
    key_rows,
    value_rows,
    halo_keys,
    halo_values,
    halo_rows,
    edge_tiles,
    grad_output,
    proj_weight,
    rel_weight,
    rel_prior,
):
    y_count = lax.axis_size("y")
    z_count = lax.axis_size("z")
    place = jnp.stack(
        [lax.axis_index("core"), lax.axis_index("y"), lax.axis_index("heads")]
    ).astype(jnp.int32)
    swap = [(0, 1), (1, 0)]
    own, send = attend(
        edge_tiles.T,
        rel_prior.T,
        queries,
        grad_output,
        key_rows,
        value_rows,
        halo_keys,
        halo_values,
        rel_weight,
        halo_rows.reshape(-1, WIDE),
    )
    incoming = lax.all_to_all(send, ("y", "z", "core"), 0, 0, tiled=True)
    feats_t, sent = bundle(place, own, node_feats, node_types.reshape(-1, WIDE))
    got = lax.ppermute(sent, "core", swap)
    pair, *q_blocks = project_queries(place, feats_t, sent, got, y_count)
    q_arrived = shifted(q_blocks, "y")
    own, *q_arrived = lax.optimization_barrier((own, *q_arrived))
    kv, rel_send, prior = collect(own, incoming)
    got_kv = lax.ppermute(kv, "core", swap)
    rel_half = lax.all_to_all(rel_send, ("y", "z"), 0, 0, tiled=True)
    arrived = shifted(project(place, pair, kv, got_kv, sent, got, y_count), "y")
    feat_blocks = features(place, sent, kv, proj_weight.reshape(PROJ, -1, WIDE))
    arrived[0], *feat_blocks = lax.optimization_barrier((arrived[0], *feat_blocks))
    grad_feats = sum(block.astype(F32) for block in shifted(feat_blocks, "heads")).astype(BF16)
    by_y = place_sum(q_arrived, arrived)
    by_z = lax.all_to_all(by_y.reshape(z_count, -1, PROJ * WIDE), "z", 0, 0, tiled=True)
    grad_proj = jnp.sum(by_z.astype(F32), axis=0).reshape(-1, 3, TYPES, WIDE)
    grad_rel = relations(place, rel_half, lax.ppermute(rel_half, "core", swap))
    grad_prior = prior.T
    return (grad_feats, grad_proj, grad_rel, grad_prior)


def solution(mesh):
    heads = mesh.devices.shape[1]
    split = Mesh(mesh.devices.reshape(4, 8, 2, heads), ("y", "z", "core", "heads"))
    nodes = ("y", "z", "core")
    return jax.shard_map(
        per_device,
        mesh=split,
        in_specs=(
            P(nodes, None),
            P(nodes),
            P(nodes, "heads"),
            P(nodes, "heads"),
            P(nodes, "heads"),
            P(nodes, "heads"),
            P(nodes, "heads"),
            P(nodes),
            P(nodes, None),
            P(nodes, "heads"),
            P(None, None, None, "heads"),
            P(None, None, "heads", None, None),
            P(None, "heads"),
        ),
        out_specs=(
            P(nodes, "heads"),
            P(nodes, None, None, "heads"),
            P(None, None, "heads", None, None),
            P(None, "heads"),
        ),
        check_vma=False,
    )
```

time: 132 us -> 96.1 us (0.73)
  blocking collectives: 27.6 us -> 0 us
  local copies, waits for them, and re-layouts: 14.3 us -> 0.95 us
  starting transfers between devices: 29.9 us -> 42.2 us
  waiting for transfers between devices: 34.8 us -> 24.1 us
  Pallas kernels: 18.7 us -> 25 us
  other arithmetic: 5.21 us -> 1.41 us
    all_to_all x1 -> x0, blocking collectives: 27.6 us -> none  [per_device(): lax.all_to_all(send.reshape(slabs, cap, 3 * WIDE), nodes, 0, 0, tiled=True)]
    ppermute x4 -> x12, starting transfers between devices: 5.75 us -> 18.5 us  [the longest x9 15.1 us: shifted(): lax.ppermute(blocks[d], axis, [(i, (i + d) % count) for i in range(count)])]
    all_to_all x4 -> x3, waiting for transfers between devices: 20.6 us -> 8.23 us  [the longest x1 6.9 us: per_device(): incoming = lax.all_to_all(send, ('y', 'z', 'core'), 0, 0, tiled=True)]
    unnamed x27 -> x10, local copies, waits for them, and re-layouts: 12.2 us -> 0.95 us
    pallas_call x2 -> x6, Pallas kernels: 2.65 us -> 8.82 us  [the longest x1 2.29 us: collect(): pl.pallas_call(collect_kernel, out_shape=(jax.ShapeDtypeStruct((rows, 2 *...]
    reduce_sum x3 -> x1, other arithmetic: 2.47 us -> 0.66 us  [per_device(): grad_proj = jnp.sum(by_z.astype(F32), axis=0).reshape(-1, 3, TYPES, WIDE)]
    ppermute x4 -> x12, waiting for transfers between devices: 14.2 us -> 15.9 us  [the longest x9 13.7 us: shifted(): lax.ppermute(blocks[d], axis, [(i, (i + d) % count) for i in range(count)])]
    all_to_all x4 -> x3, starting transfers between devices: 24.1 us -> 23.7 us  [the longest x1 13.2 us: per_device(): incoming = lax.all_to_all(send, ('y', 'z', 'core'), 0, 0, tiled=True)]
  transfers between devices with their start and end apart: 8 -> 15, of which waited for: 5 -> 9; matrix products, arithmetic and copies ran while one was open for 7% -> 1% of each run, Pallas kernels for 4% -> 6%
where the time goes in v1:
time: 96.1 us; the launch traced here: 94.5 us
  starting transfers between devices  42.2 us (44%)
  Pallas kernels  25 us (26%)
  waiting for transfers between devices  24.1 us (25%)
  other arithmetic  1.41 us (1%)
    ppermute x9, starting transfers between devices, shifted(): lax.ppermute(blocks[d], axis, [(i, (i + d) % count) for i in range(count)])  15.1 us
    pallas_call x1, Pallas kernels, attend(): pl.pallas_call(attend_kernel, out_shape=(jax.ShapeDtypeStruct((rows, 3 *...  14.7 us
    ppermute x9, waiting for transfers between devices, shifted(): lax.ppermute(blocks[d], axis, [(i, (i + d) % count) for i in range(count)])  13.7 us
    all_to_all x1, starting transfers between devices, per_device(): incoming = lax.all_to_all(send, ('y', 'z', 'core'), 0, 0, tiled=True)  13.2 us
    all_to_all x1, waiting for transfers between devices, per_device(): incoming = lax.all_to_all(send, ('y', 'z', 'core'), 0, 0, tiled=True)  6.9 us
    all_to_all x1, starting transfers between devices, per_device(): lax.all_to_all(by_y.reshape(z_count, -1, PROJ * WIDE), 'z', 0, 0, tiled=T...  5.36 us
    all_to_all x1, starting transfers between devices, per_device(): rel_half = lax.all_to_all(rel_send, ('y', 'z'), 0, 0, tiled=True)  5.15 us
    pallas_call x1, Pallas kernels, collect(): pl.pallas_call(collect_kernel, out_shape=(jax.ShapeDtypeStruct((rows, 2 *...  2.29 us
  transfers between devices with their start and end apart: 15, of which 9 were waited for; matrix products, arithmetic and copies ran while one was open for 1% of the time, Pallas kernels for 6%

profile of v1, /device:TPU:1, one launch (start us, length us, event | category | flops | bytes accessed | tf_op | source)
XLA Modules:
  0.0 94.5 jit_solution(4764448018379295163)
XLA Ops:
  0.7 14.7 %attend.1 = (bf16[256,384]{1,0:T(8,128)(2,1)}, bf16[64,48,128]{2,1,0:T(8,128)(2,1)}) custom-call(s32[3,40]{1,0:T(4,128)} %bitcast.14, f32[2,15]{1,0:T(2,128)} %bitcast.16, bf16[256,128]{1,0:T(8,128)(2,1)} %q_hbm.1, bf16[256,128]{1,0:T(8,128)(2,1)} %g_hbm.1, bf16[256,128]{1,0:T(8,128)(2,1)} %ko_hbm.1, bf16[256,128]{1,0:T(8,128)(2,1)} %vo_hbm.1, ...), custom_call_target="tpu_custom_call" | custom-call | flops 3000000000 | bytes 4000000 | tf_op jit(solution)/shard_map/attend/pallas_call | solution.py:212
  15.4 13.2 %all-to-all-start = ((bf16[64,48,128]{2,1,0:T(8,128)(2,1)}), bf16[64,48,128]{2,1,0:T(8,128)(2,1)S(1)}, u32[]{:S(2)}, u32[]{:S(2)}) async-start(bf16[64,48,128]{2,1,0:T(8,128)(2,1)} %get-tuple-element.43), calls=%async_computation | async-start | bytes 1572864 | tf_op jit(solution)/shard_map/all_to_all | solution.py:531
  30.9 1.2 %collective-permute-done.got_ref = bf16[256,512]{1,0:T(8,128)(2,1)S(1)} collective-permute-done((bf16[256,512]{1,0:T(8,128)(2,1)S(1)}, bf16[256,512]{1,0:T(8,128)(2,1)S(1)}, u32[]{:S(2)}, u32[]{:S(2)}) %collective-permute-start) | collective-permute-done | bytes 262176 | tf_op jit(solution)/shard_map/ppermute | solution.py:533
  33.1 1.4 %collective-permute-start.1 = (bf16[64,640]{1,0:T(8,128)(2,1)S(1)}, bf16[64,640]{1,0:T(8,128)(2,1)S(1)}, u32[]{:S(2)}, u32[]{:S(2)}) collective-permute-start(bf16[64,640]{1,0:T(8,128)(2,1)S(1)} %get-tuple-element.39), channel_id=1, source_target_pairs={{0,64},{64,128},{128,192},{192,0},{1,65},{65,129},{129,193},{193,1... | collective-permute-start | bytes 245768 | tf_op jit(solution)/shard_map/ppermute | solution.py:493
  34.5 2.6 %collective-permute-start.2 = (bf16[64,640]{1,0:T(8,128)(2,1)S(1)}, bf16[64,640]{1,0:T(8,128)(2,1)S(1)}, u32[]{:S(2)}, u32[]{:S(2)}) collective-permute-start(bf16[64,640]{1,0:T(8,128)(2,1)S(1)} %get-tuple-element.40), channel_id=1, source_target_pairs={{0,128},{64,192},{128,0},{192,64},{1,129},{65,193},{129,1},{193,65... | collective-permute-start | bytes 245768 | tf_op jit(solution)/shard_map/ppermute | solution.py:493
  38.2 1.5 %collective-permute-done.1.refs_1_ = bf16[64,640]{1,0:T(8,128)(2,1)S(1)} collective-permute-done((bf16[64,640]{1,0:T(8,128)(2,1)S(1)}, bf16[64,640]{1,0:T(8,128)(2,1)S(1)}, u32[]{:S(2)}, u32[]{:S(2)}) %collective-permute-start.1) | collective-permute-done | bytes 81952 | tf_op jit(solution)/shard_map/ppermute | solution.py:493
  39.7 5.0 %collective-permute-done.2.refs_2_ = bf16[64,640]{1,0:T(8,128)(2,1)S(1)} collective-permute-done((bf16[64,640]{1,0:T(8,128)(2,1)S(1)}, bf16[64,640]{1,0:T(8,128)(2,1)S(1)}, u32[]{:S(2)}, u32[]{:S(2)}) %collective-permute-start.2) | collective-permute-done | bytes 81952 | tf_op jit(solution)/shard_map/ppermute | solution.py:493
  44.7 6.9 %all-to-all-done.inc_hbm = bf16[64,48,128]{2,1,0:T(8,128)(2,1)S(1)} async-done(((bf16[64,48,128]{2,1,0:T(8,128)(2,1)}), bf16[64,48,128]{2,1,0:T(8,128)(2,1)S(1)}, u32[]{:S(2)}, u32[]{:S(2)}) %all-to-all-start) | async-done | bytes 786464 | tf_op jit(solution)/shard_map/all_to_all | solution.py:531
  51.6 2.3 %collect.1 = (bf16[256,256]{1,0:T(8,128)(2,1)S(1)}, bf16[32,32,128]{2,1,0:T(8,128)(2,1)}, f32[2,15]{1,0:T(2,128)}) custom-call(bf16[256,384]{1,0:T(8,128)(2,1)S(1)} %copy-done.1, bf16[64,48,128]{2,1,0:T(8,128)(2,1)S(1)} %all-to-all-done.inc_hbm), custom_call_target="tpu_custom_call" | custom-call | flops 100000000 | bytes 2000000 | tf_op jit(solution)/shard_map/collect/pallas_call | solution.py:359
  53.9 5.1 %all-to-all-start.2 = ((bf16[32,32,128]{2,1,0:T(8,128)(2,1)}), bf16[32,32,128]{2,1,0:T(8,128)(2,1)S(1)}, u32[]{:S(2)}, u32[]{:S(2)}) async-start(bf16[32,32,128]{2,1,0:T(8,128)(2,1)} %get-tuple-element.62), calls=%async_computation.2 | async-start | bytes 524288 | tf_op jit(solution)/shard_map/all_to_all | solution.py:539
  61.0 1.5 %project.1 = (bf16[64,1280]{1,0:T(8,128)(2,1)S(1)}, bf16[64,1280]{1,0:T(8,128)(2,1)S(1)}, bf16[64,1280]{1,0:T(8,128)(2,1)S(1)}, bf16[64,1280]{1,0:T(8,128)(2,1)S(1)}) custom-call(s32[3]{0:T(128)S(1)} %pad_add_fusion.place, bf16[256,512]{1,0:T(8,128)(2,1)S(1)} %get-tuple-element.37.pair_ref, bf16[256,256]{1,0:T(8,128)(2,1)S(1)} %get-tuple-element.44.kv_ref, ...), custom_call_target="tpu_custom_call" | custom-call | flops 1000000000 | bytes 4000000 | tf_op jit(solution)/shard_map/project/pallas_call | solution.py:393
  62.5 1.6 %collective-permute-start.8 = (bf16[64,1280]{1,0:T(8,128)(2,1)S(1)}, bf16[64,1280]{1,0:T(8,128)(2,1)S(1)}, u32[]{:S(2)}, u32[]{:S(2)}) collective-permute-start(bf16[64,1280]{1,0:T(8,128)(2,1)S(1)} %get-tuple-element.59), channel_id=1, source_target_pairs={{0,64},{64,128},{128,192},{192,0},{1,65},{65,129},{129,193},{193,1... | collective-permute-start | bytes 491528 | tf_op jit(solution)/shard_map/ppermute | solution.py:493
  64.1 2.4 %collective-permute-start.9 = (bf16[64,1280]{1,0:T(8,128)(2,1)S(1)}, bf16[64,1280]{1,0:T(8,128)(2,1)S(1)}, u32[]{:S(2)}, u32[]{:S(2)}) collective-permute-start(bf16[64,1280]{1,0:T(8,128)(2,1)S(1)} %get-tuple-element.60), channel_id=1, source_target_pairs={{0,128},{64,192},{128,0},{192,64},{1,129},{65,193},{129,1},{193,65... | collective-permute-start | bytes 491528 | tf_op jit(solution)/shard_map/ppermute | solution.py:493
  66.5 1.2 %collective-permute-start.10 = (bf16[64,1280]{1,0:T(8,128)(2,1)S(1)}, bf16[64,1280]{1,0:T(8,128)(2,1)S(1)}, u32[]{:S(2)}, u32[]{:S(2)}) collective-permute-start(bf16[64,1280]{1,0:T(8,128)(2,1)S(1)} %get-tuple-element.61), channel_id=1, source_target_pairs={{0,192},{64,0},{128,64},{192,128},{1,193},{65,1},{129,65},{193,129... | collective-permute-start | bytes 491528 | tf_op jit(solution)/shard_map/ppermute | solution.py:493
  67.7 1.8 %features.1 = (bf16[256,128]{1,0:T(8,128)(2,1)S(1)}, bf16[256,128]{1,0:T(8,128)(2,1)S(1)}, bf16[256,128]{1,0:T(8,128)(2,1)S(1)}, bf16[256,128]{1,0:T(8,128)(2,1)S(1)}) custom-call(s32[3]{0:T(128)S(1)} %pad_add_fusion.place, bf16[256,512]{1,0:T(8,128)(2,1)S(1)} %get-tuple-element.36.sent_ref, bf16[256,256]{1,0:T(8,128)(2,1)S(1)} %get-tuple-element.44.kv_ref, ...), custom_call_target="tpu_custom_call" | custom-call | flops 1000000000 | bytes 3000000 | tf_op jit(solution)/shard_map/features/pallas_call | solution.py:426
  69.4 2.2 %collective-permute-done.8.refs_5_ = bf16[64,1280]{1,0:T(8,128)(2,1)S(1)} collective-permute-done((bf16[64,1280]{1,0:T(8,128)(2,1)S(1)}, bf16[64,1280]{1,0:T(8,128)(2,1)S(1)}, u32[]{:S(2)}, u32[]{:S(2)}) %collective-permute-start.8) | collective-permute-done | bytes 163872 | tf_op jit(solution)/shard_map/ppermute | solution.py:493
  71.7 4.1 %collective-permute-done.9.refs_6_ = bf16[64,1280]{1,0:T(8,128)(2,1)S(1)} collective-permute-done((bf16[64,1280]{1,0:T(8,128)(2,1)S(1)}, bf16[64,1280]{1,0:T(8,128)(2,1)S(1)}, u32[]{:S(2)}, u32[]{:S(2)}) %collective-permute-start.9) | collective-permute-done | bytes 163872 | tf_op jit(solution)/shard_map/ppermute | solution.py:493
  76.5 5.4 %all-to-all-start.1 = ((bf16[8,8,1920]{2,1,0:T(8,128)(2,1)}), bf16[8,8,1920]{2,1,0:T(8,128)(2,1)S(1)}, u32[]{:S(2)}, u32[]{:S(2)}) async-start(bf16[8,8,1920]{2,1,0:T(8,128)(2,1)} %bitcast.8), calls=%async_computation.1 | async-start | bytes 491520 | tf_op jit(solution)/shard_map/all_to_all | solution.py:545
  81.9 1.2 %collective-permute-start.5 = (bf16[256,128]{1,0:T(8,128)(2,1)S(1)}, bf16[256,128]{1,0:T(8,128)(2,1)S(1)}, u32[]{:S(2)}, u32[]{:S(2)}) collective-permute-start(bf16[256,128]{1,0:T(8,128)(2,1)S(1)} %get-tuple-element.51), channel_id=1, source_target_pairs={{0,1},{1,2},{2,3},{3,0},{4,5},{5,6},{6,7},{7,4},{8,9},{9,10},{10,1... | collective-permute-start | bytes 196616 | tf_op jit(solution)/shard_map/ppermute | solution.py:493
  83.1 2.5 %collective-permute-start.6 = (bf16[256,128]{1,0:T(8,128)(2,1)S(1)}, bf16[256,128]{1,0:T(8,128)(2,1)S(1)}, u32[]{:S(2)}, u32[]{:S(2)}) collective-permute-start(bf16[256,128]{1,0:T(8,128)(2,1)S(1)} %get-tuple-element.52), channel_id=1, source_target_pairs={{0,2},{1,3},{2,0},{3,1},{4,6},{5,7},{6,4},{7,5},{8,10},{9,11},{10,... | collective-permute-start | bytes 196616 | tf_op jit(solution)/shard_map/ppermute | solution.py:493
  85.6 1.2 %collective-permute-start.7 = (bf16[256,128]{1,0:T(8,128)(2,1)S(1)}, bf16[256,128]{1,0:T(8,128)(2,1)S(1)}, u32[]{:S(2)}, u32[]{:S(2)}) collective-permute-start(bf16[256,128]{1,0:T(8,128)(2,1)S(1)} %get-tuple-element.53), channel_id=1, source_target_pairs={{0,3},{1,0},{2,1},{3,2},{4,7},{5,4},{6,5},{7,6},{8,11},{9,8},{10,9... | collective-permute-start | bytes 196616 | tf_op jit(solution)/shard_map/ppermute | solution.py:493
  86.7 2.0 %collective-permute-start.11 = (bf16[32,32,128]{2,1,0:T(8,128)(2,1)S(1)}, bf16[32,32,128]{2,1,0:T(8,128)(2,1)S(1)}, u32[]{:S(2)}, u32[]{:S(2)}) collective-permute-start(bf16[32,32,128]{2,1,0:T(8,128)(2,1)S(1)} %all-to-all-done.2.mine_ref), channel_id=1, source_target_pairs={{0,4},{4,0},{1,5},{5,1},{2,6},{6,2},{3,7},{7,3},{8,12},{12,8},{9,1... | collective-permute-start | bytes 786440 | tf_op jit(solution)/shard_map/ppermute | solution.py:547
  90.3 1.3 %all-to-all-done.1 = bf16[8,8,1920]{2,1,0:T(8,128)(2,1)S(1)} async-done(((bf16[8,8,1920]{2,1,0:T(8,128)(2,1)}), bf16[8,8,1920]{2,1,0:T(8,128)(2,1)S(1)}, u32[]{:S(2)}, u32[]{:S(2)}) %all-to-all-start.1) | async-done | bytes 245792 | tf_op jit(solution)/shard_map/all_to_all | solution.py:545
  92.3 2.1 %relations.1 = f32[2,15,2,64,64]{4,3,2,1,0:T(8,128)} custom-call(s32[3]{0:T(128)S(1)} %pad_add_fusion.place, bf16[32,32,128]{2,1,0:T(8,128)(2,1)S(1)} %all-to-all-done.2.mine_ref, bf16[32,32,128]{2,1,0:T(8,128)(2,1)S(1)} %collective-permute-done.11.other_ref), custom_call_target="tpu_custom_call" | custom-call | flops 1000000 | bytes 3000000 | tf_op jit(solution)/shard_map/relations/pallas_call | solution.py:454
  (27 shorter events, 9.6 us)
Async XLA Ops:
  0.6 28.0 %copy-start.2 = (bf16[256,512]{1,0:T(8,128)(2,1)S(1)}, bf16[256,512]{1,0:T(8,128)(2,1)}, u32[]{:S(2)}) copy-start(bf16[256,512]{1,0:T(8,128)(2,1)} %nf_ref.1) | copy-start | bytes 786436
  0.6 28.0 %copy-start.3 = (s32[256]{0:T(256)S(1)}, s32[256]{0:T(256)}, u32[]{:S(2)}) copy-start(s32[256]{0:T(256)} %param.14) | copy-start | bytes 3076
  15.4 36.2 %all-to-all-start = ((bf16[64,48,128]{2,1,0:T(8,128)(2,1)}), bf16[64,48,128]{2,1,0:T(8,128)(2,1)S(1)}, u32[]{:S(2)}, u32[]{:S(2)}) async-start(bf16[64,48,128]{2,1,0:T(8,128)(2,1)} %get-tuple-element.43), calls=%async_computation | async-start | bytes 1572864 | tf_op jit(solution)/shard_map/all_to_all | solution.py:531
  28.7 0.9 copy-start
  30.3 21.3 %copy-start.1 = (bf16[256,384]{1,0:T(8,128)(2,1)S(1)}, bf16[256,384]{1,0:T(8,128)(2,1)}, u32[]{:S(2)}) copy-start(bf16[256,384]{1,0:T(8,128)(2,1)} %get-tuple-element.42.own_ref) | copy-start | bytes 589828
  30.3 1.7 %collective-permute-start = (bf16[256,512]{1,0:T(8,128)(2,1)S(1)}, bf16[256,512]{1,0:T(8,128)(2,1)S(1)}, u32[]{:S(2)}, u32[]{:S(2)}) collective-permute-start(bf16[256,512]{1,0:T(8,128)(2,1)S(1)} %get-tuple-element.36.sent_ref), channel_id=1, source_target_pairs={{0,4},{4,0},{1,5},{5,1},{2,6},{6,2},{3,7},{7,3},{8,12},{12,8},{9,1... | collective-permute-start | bytes 786440 | tf_op jit(solution)/shard_map/ppermute | solution.py:533
  33.1 6.6 %collective-permute-start.1 = (bf16[64,640]{1,0:T(8,128)(2,1)S(1)}, bf16[64,640]{1,0:T(8,128)(2,1)S(1)}, u32[]{:S(2)}, u32[]{:S(2)}) collective-permute-start(bf16[64,640]{1,0:T(8,128)(2,1)S(1)} %get-tuple-element.39), channel_id=1, source_target_pairs={{0,64},{64,128},{128,192},{192,0},{1,65},{65,129},{129,193},{193,1... | collective-permute-start | bytes 245768 | tf_op jit(solution)/shard_map/ppermute | solution.py:493
  34.5 10.1 %collective-permute-start.2 = (bf16[64,640]{1,0:T(8,128)(2,1)S(1)}, bf16[64,640]{1,0:T(8,128)(2,1)S(1)}, u32[]{:S(2)}, u32[]{:S(2)}) collective-permute-start(bf16[64,640]{1,0:T(8,128)(2,1)S(1)} %get-tuple-element.40), channel_id=1, source_target_pairs={{0,128},{64,192},{128,0},{192,64},{1,129},{65,193},{129,1},{193,65... | collective-permute-start | bytes 245768 | tf_op jit(solution)/shard_map/ppermute | solution.py:493
  37.1 7.5 %collective-permute-start.3 = (bf16[64,640]{1,0:T(8,128)(2,1)S(1)}, bf16[64,640]{1,0:T(8,128)(2,1)S(1)}, u32[]{:S(2)}, u32[]{:S(2)}) collective-permute-start(bf16[64,640]{1,0:T(8,128)(2,1)S(1)} %get-tuple-element.41), channel_id=1, source_target_pairs={{0,192},{64,0},{128,64},{192,128},{1,193},{65,1},{129,65},{193,129... | collective-permute-start | bytes 245768 | tf_op jit(solution)/shard_map/ppermute | solution.py:493
  53.9 22.7 %all-to-all-start.2 = ((bf16[32,32,128]{2,1,0:T(8,128)(2,1)}), bf16[32,32,128]{2,1,0:T(8,128)(2,1)S(1)}, u32[]{:S(2)}, u32[]{:S(2)}) async-start(bf16[32,32,128]{2,1,0:T(8,128)(2,1)} %get-tuple-element.62), calls=%async_computation.2 | async-start | bytes 524288 | tf_op jit(solution)/shard_map/all_to_all | solution.py:539
  59.0 8.6 %copy-start.4 = (bf16[3,5,512,128]{3,2,1,0:T(8,128)(2,1)S(1)}, bf16[3,5,512,128]{3,2,1,0:T(8,128)(2,1)}, u32[]{:S(2)}) copy-start(bf16[3,5,512,128]{3,2,1,0:T(8,128)(2,1)} %param.23) | copy-start | bytes 5898244
  59.0 2.0 %collective-permute-start.4 = (bf16[256,256]{1,0:T(8,128)(2,1)S(1)}, bf16[256,256]{1,0:T(8,128)(2,1)S(1)}, u32[]{:S(2)}, u32[]{:S(2)}) collective-permute-start(bf16[256,256]{1,0:T(8,128)(2,1)S(1)} %get-tuple-element.44.kv_ref), channel_id=1, source_target_pairs={{0,4},{4,0},{1,5},{5,1},{2,6},{6,2},{3,7},{7,3},{8,12},{12,8},{9,1... | collective-permute-start | bytes 393224 | tf_op jit(solution)/shard_map/ppermute | solution.py:538
  62.5 9.2 %collective-permute-start.8 = (bf16[64,1280]{1,0:T(8,128)(2,1)S(1)}, bf16[64,1280]{1,0:T(8,128)(2,1)S(1)}, u32[]{:S(2)}, u32[]{:S(2)}) collective-permute-start(bf16[64,1280]{1,0:T(8,128)(2,1)S(1)} %get-tuple-element.59), channel_id=1, source_target_pairs={{0,64},{64,128},{128,192},{192,0},{1,65},{65,129},{129,193},{193,1... | collective-permute-start | bytes 491528 | tf_op jit(solution)/shard_map/ppermute | solution.py:493
  64.1 11.6 %collective-permute-start.9 = (bf16[64,1280]{1,0:T(8,128)(2,1)S(1)}, bf16[64,1280]{1,0:T(8,128)(2,1)S(1)}, u32[]{:S(2)}, u32[]{:S(2)}) collective-permute-start(bf16[64,1280]{1,0:T(8,128)(2,1)S(1)} %get-tuple-element.60), channel_id=1, source_target_pairs={{0,128},{64,192},{128,0},{192,64},{1,129},{65,193},{129,1},{193,65... | collective-permute-start | bytes 491528 | tf_op jit(solution)/shard_map/ppermute | solution.py:493
  66.5 9.2 %collective-permute-start.10 = (bf16[64,1280]{1,0:T(8,128)(2,1)S(1)}, bf16[64,1280]{1,0:T(8,128)(2,1)S(1)}, u32[]{:S(2)}, u32[]{:S(2)}) collective-permute-start(bf16[64,1280]{1,0:T(8,128)(2,1)S(1)} %get-tuple-element.61), channel_id=1, source_target_pairs={{0,192},{64,0},{128,64},{192,128},{1,193},{65,1},{129,65},{193,129... | collective-permute-start | bytes 491528 | tf_op jit(solution)/shard_map/ppermute | solution.py:493
  76.5 15.1 %all-to-all-start.1 = ((bf16[8,8,1920]{2,1,0:T(8,128)(2,1)}), bf16[8,8,1920]{2,1,0:T(8,128)(2,1)S(1)}, u32[]{:S(2)}, u32[]{:S(2)}) async-start(bf16[8,8,1920]{2,1,0:T(8,128)(2,1)} %bitcast.8), calls=%async_computation.1 | async-start | bytes 491520 | tf_op jit(solution)/shard_map/all_to_all | solution.py:545
  81.9 6.8 %collective-permute-start.5 = (bf16[256,128]{1,0:T(8,128)(2,1)S(1)}, bf16[256,128]{1,0:T(8,128)(2,1)S(1)}, u32[]{:S(2)}, u32[]{:S(2)}) collective-permute-start(bf16[256,128]{1,0:T(8,128)(2,1)S(1)} %get-tuple-element.51), channel_id=1, source_target_pairs={{0,1},{1,2},{2,3},{3,0},{4,5},{5,6},{6,7},{7,4},{8,9},{9,10},{10,1... | collective-permute-start | bytes 196616 | tf_op jit(solution)/shard_map/ppermute | solution.py:493
  83.1 5.6 %collective-permute-start.6 = (bf16[256,128]{1,0:T(8,128)(2,1)S(1)}, bf16[256,128]{1,0:T(8,128)(2,1)S(1)}, u32[]{:S(2)}, u32[]{:S(2)}) collective-permute-start(bf16[256,128]{1,0:T(8,128)(2,1)S(1)} %get-tuple-element.52), channel_id=1, source_target_pairs={{0,2},{1,3},{2,0},{3,1},{4,6},{5,7},{6,4},{7,5},{8,10},{9,11},{10,... | collective-permute-start | bytes 196616 | tf_op jit(solution)/shard_map/ppermute | solution.py:493
  85.6 4.1 %collective-permute-start.7 = (bf16[256,128]{1,0:T(8,128)(2,1)S(1)}, bf16[256,128]{1,0:T(8,128)(2,1)S(1)}, u32[]{:S(2)}, u32[]{:S(2)}) collective-permute-start(bf16[256,128]{1,0:T(8,128)(2,1)S(1)} %get-tuple-element.53), channel_id=1, source_target_pairs={{0,3},{1,0},{2,1},{3,2},{4,7},{5,4},{6,5},{7,6},{8,11},{9,8},{10,9... | collective-permute-start | bytes 196616 | tf_op jit(solution)/shard_map/ppermute | solution.py:493
  86.7 5.6 %collective-permute-start.11 = (bf16[32,32,128]{2,1,0:T(8,128)(2,1)S(1)}, bf16[32,32,128]{2,1,0:T(8,128)(2,1)S(1)}, u32[]{:S(2)}, u32[]{:S(2)}) collective-permute-start(bf16[32,32,128]{2,1,0:T(8,128)(2,1)S(1)} %all-to-all-done.2.mine_ref), channel_id=1, source_target_pairs={{0,4},{4,0},{1,5},{5,1},{2,6},{6,2},{3,7},{7,3},{8,12},{12,8},{9,1... | collective-permute-start | bytes 786440 | tf_op jit(solution)/shard_map/ppermute | solution.py:547

commit v2 on v1

v2 whole, which is shorter than its diff:
```python
import jax
import jax.numpy as jnp
from jax import lax
from jax.experimental import pallas as pl
from jax.experimental.pallas import tpu as pltpu
from jax.sharding import Mesh, PartitionSpec as P

TYPES = 5
RELS = 15
TILE = 64
WIDE = 128
GROUP = 4
UNROLL = 7
PROJ = 3 * TYPES

F32 = jnp.float32
BF16 = jnp.bfloat16
NN = (((1,), (0,)), ((), ()))
NT = (((1,), (1,)), ((), ()))
TN = (((0,), (0,)), ((), ()))
VMEM = pl.BlockSpec(memory_space=pltpu.VMEM)
SMEM = pl.BlockSpec(memory_space=pltpu.SMEM)
HBM = pl.BlockSpec(memory_space=pltpu.HBM)
BLOCK = 24
REL_ROWS = 240
REL_BLOCK = 256
LIMIT = 24 * 2**20
MOST = 62 * 2**20


def mul(left, right, dims):
    return lax.dot_general(left, right, dims, preferred_element_type=F32)


def column(row):
    return jnp.transpose(jnp.broadcast_to(row, (WIDE, WIDE)), (1, 0))


def high_and_low(line):
    line = line + pltpu.roll(line, WIDE - 32, 1)
    high = line.astype(BF16).astype(F32)
    lane = lax.broadcasted_iota(jnp.int32, line.shape, 1)
    return jnp.where(lane < 32, high, pltpu.roll(line - high, 32, 1))


def with_line(block):
    row = lax.broadcasted_iota(jnp.int32, block.shape, 0)
    return jnp.where(row == REL_ROWS, high_and_low(block[REL_ROWS : REL_ROWS + 1, :]), block)


def attend_kernel(
    edges_hbm, prior_hbm, q_hbm, g_hbm, ko_hbm, vo_hbm, kh_hbm, vh_hbm, rel_hbm, rows_hbm,
    own_out, send_out, rel_out,
    edges, listed, prior_in, q_ref, g_ref, rel_ref, rows_ref, k_ref, v_ref, sems,
    wbd, qg, keep, prior, kvm, probs, exps, logs, grads,
    denom, delta, dprior, dkv, dwk, dwv, dq, drel, ids_ref,
):
    count = edges.shape[1]
    places = kvm.shape[0]
    own = ko_hbm.shape[0]
    dests = own // TILE
    own_tiles = own // TILE
    halo_tiles = kh_hbm.shape[0] // TILE
    copies = [
        pltpu.make_async_copy(source, target, sems.at[i])
        for i, (source, target) in enumerate(
            (
                (rel_hbm, rel_ref),
                (q_hbm, q_ref),
                (g_hbm, g_ref),
                (rows_hbm, rows_ref),
                (edges_hbm, edges),
                (prior_hbm, prior_in),
                (ko_hbm, k_ref.at[:own]),
                (vo_hbm, v_ref.at[:own]),
                (kh_hbm, k_ref.at[own:]),
                (vh_hbm, v_ref.at[own:]),
            )
        )
    ]
    for copy in copies:
        copy.start()

    lane = lax.broadcasted_iota(jnp.int32, (TILE, WIDE), 1)
    first = lane < TILE
    wbd[...] = jnp.zeros_like(wbd)
    denom[...] = jnp.zeros_like(denom)
    delta[...] = jnp.zeros_like(delta)
    dprior[...] = jnp.zeros_like(dprior)
    dkv[...] = jnp.zeros_like(dkv)
    dwk[...] = jnp.zeros_like(dwk)
    dwv[...] = jnp.zeros_like(dwv)
    dq[...] = jnp.zeros_like(dq)
    copies[4].wait()
    for i in range(listed.shape[0]):
        listed[i] = 0
    targets = [edges[0, e] for e in range(count)]
    sizes = [sum((target == a).astype(jnp.int32) for target in targets) for a in range(dests)]
    starts = [jnp.int32(0)]
    for a in range(dests):
        starts.append(starts[a] + (sizes[a] + GROUP - 1) // GROUP * GROUP)
    heads = list(starts[:dests])
    for e, target in enumerate(targets):
        at = jnp.int32(places)
        for a in range(dests):
            at = jnp.where(target == a, heads[a], at)
            heads[a] = heads[a] + (target == a).astype(jnp.int32)
        listed[at] = 256 + 16 * edges[1, e] + edges[2, e]
    used = starts[dests] // GROUP
    for i, copy in enumerate(copies):
        if i != 4:
            copy.wait()

    for r in range(RELS):
        for w in range(2):
            for h in range(2):
                at = (2 * w + h) * TILE
                wbd[r, at : at + TILE, at : at + TILE] = rel_ref[w, r, h]
    none = jnp.zeros((TILE, WIDE), BF16)
    for a in range(dests):
        q = q_ref[a * TILE : (a + 1) * TILE, :].astype(F32) * 0.125
        g = g_ref[a * TILE : (a + 1) * TILE, :].astype(F32)
        for h in range(2):
            mine = first if h == 0 else jnp.logical_not(first)
            qg[a, h * TILE : (h + 1) * TILE, :WIDE] = jnp.where(mine, q, 0.0).astype(BF16)
            qg[a, h * TILE : (h + 1) * TILE, WIDE:] = none
            qg[a, (2 + h) * TILE : (3 + h) * TILE, :WIDE] = none
            qg[a, (2 + h) * TILE : (3 + h) * TILE, WIDE:] = jnp.where(mine, g, 0.0).astype(BF16)
    for b in range(own_tiles):
        keep[b] = jnp.ones((TILE, WIDE), F32)
    period = lax.broadcasted_iota(jnp.int32, (16, 8, WIDE), 2) % 8
    slot = lax.broadcasted_iota(jnp.int32, (16, 8, WIDE), 1)
    for j in range(halo_tiles // 2):
        ids = column(rows_ref[j : j + 1, :].astype(F32))
        ok = (ids < float(own)).astype(F32)
        keep[own_tiles + 2 * j] = ok[:TILE]
        keep[own_tiles + 2 * j + 1] = ok[TILE:]
        tiled = jnp.sum(jnp.where(period == slot, ids.reshape(16, 8, WIDE), 0.0), axis=1)
        ids_ref[16 * j : 16 * j + 16, :] = tiled
    one_lane = lax.broadcasted_iota(jnp.int32, (1, WIDE), 1)
    for r in range(RELS):
        prior[r : r + 1, :] = jnp.where(one_lane < TILE, prior_in[0, r], prior_in[1, r])

    def entry(i):
        code = listed[i]
        return (code >> 4) & 15, code & 15, (code >= 256).astype(F32)

    def rows(b):
        return pl.ds(pl.multiple_of(b * TILE, TILE), TILE)

    def tile_of(group):
        at = group * GROUP
        return sum((at >= starts[a]).astype(jnp.int32) for a in range(1, dests))

    def scores(group):
        i = group * GROUP
        a = tile_of(group)
        parts = []
        for u in range(GROUP):
            b, r, live = entry(i + u)
            pair = jnp.concatenate([k_ref[rows(b), :], v_ref[rows(b), :]], axis=1)
            parts.append(mul(pair, wbd[r], NN).astype(BF16))
        mixed = jnp.concatenate(parts, axis=0)
        kvm[pl.ds(i, GROUP)] = mixed[:, :WIDE].reshape(GROUP, TILE, WIDE)
        both = mul(mixed, qg[a], NT)
        logs[pl.ds(i, GROUP)] = both[:, :WIDE].reshape(GROUP, TILE, WIDE)
        grads[pl.ds(i, GROUP)] = both[:, WIDE:].reshape(GROUP, TILE, WIDE)
        total = None
        for u in range(GROUP):
            b, r, live = entry(i + u)
            ex = jnp.exp(prior[pl.ds(r, 1), :] * both[u * TILE : (u + 1) * TILE, :WIDE]) * (keep[b] * live)
            exps[i + u] = ex
            total = ex if total is None else total + ex
        denom[a] += jnp.sum(total, axis=0, keepdims=True)

    def normalise(group):
        i = group * GROUP
        a = tile_of(group)
        total = None
        for u in range(GROUP):
            soft = exps[i + u] * denom[a]
            exps[i + u] = soft
            prob = soft.astype(BF16)
            probs[i + u] = prob
            term = prob.astype(F32) * grads[i + u]
            total = term if total is None else total + term
        delta[a] += jnp.sum(total, axis=0, keepdims=True)

    def backward(group):
        i = group * GROUP
        a = tile_of(group)
        parts = []
        for u in range(GROUP):
            b, r, live = entry(i + u)
            score_grad = exps[i + u] * (grads[i + u] - delta[a])
            dprior[pl.ds(r, 1), :] += jnp.sum(score_grad * logs[i + u], axis=0, keepdims=True)
            parts.append((score_grad * prior[pl.ds(r, 1), :]).astype(BF16))
        lgrad = jnp.concatenate(parts, axis=0)
        pair = jnp.concatenate([lgrad, probs[pl.ds(i, GROUP)].reshape(GROUP * TILE, WIDE)], axis=1)
        mixed_grad = mul(pair, qg[a], NN).astype(BF16)
        dq[a] += mul(lgrad, kvm[pl.ds(i, GROUP)].reshape(GROUP * TILE, WIDE), TN)
        for u in range(GROUP):
            b, r, live = entry(i + u)
            part = mixed_grad[u * TILE : (u + 1) * TILE]
            dkv[b] += mul(part, wbd[r], NT)
            dwk[r] += mul(k_ref[rows(b), :], part[:, :WIDE], TN)
            dwv[r] += mul(v_ref[rows(b), :], part[:, WIDE:], TN)

    def sweep(work):
        def some(step, carry):
            for u in range(UNROLL):
                work(step * UNROLL + u)
            return carry

        lax.fori_loop(0, (used + UNROLL - 1) // UNROLL, some, 0)

    sweep(scores)
    denom[...] = 1.0 / denom[...]
    sweep(normalise)
    sweep(backward)

    for a in range(dests):
        grad = jnp.where(first, dq[a, :TILE, :], dq[a, TILE:, :]) * 0.125
        own_out[a * TILE : (a + 1) * TILE, :WIDE] = grad.astype(BF16)
    for b in range(own_tiles):
        own_out[b * TILE : (b + 1) * TILE, WIDE:] = dkv[b].astype(BF16)
    for b in range(halo_tiles):
        back = dkv[own_tiles + b]
        block = jnp.concatenate(
            [
                back[:, :WIDE].reshape(8, 8, WIDE),
                back[:, WIDE:].reshape(8, 8, WIDE),
                jnp.broadcast_to(ids_ref[8 * b : 8 * b + 8, :].reshape(8, 1, WIDE), (8, 8, WIDE)),
            ],
            axis=1,
        )
        send_out[8 * b : 8 * b + 8] = block.astype(BF16)
    for w, ref in enumerate((dwk, dwv)):
        for r in range(RELS):
            at = (w * RELS + r) * TILE
            drel[at : at + TILE, :] = jnp.where(first, ref[r, :TILE, :], ref[r, TILE:, :])
    sums = dprior[...]
    spot = lax.broadcasted_iota(jnp.int32, sums.shape, 1)
    row = lax.broadcasted_iota(jnp.int32, sums.shape, 0)
    one = jnp.sum(jnp.where(spot < TILE, sums, 0.0), axis=1, keepdims=True)
    two = jnp.sum(jnp.where(spot < TILE, 0.0, sums), axis=1, keepdims=True)
    chosen = jnp.where((spot // 16) % 2 == 0, one, two)
    line = jnp.sum(jnp.where(spot % 16 == row, chosen, 0.0), axis=0, keepdims=True)
    high = line.astype(BF16).astype(F32)
    line = jnp.where(one_lane < 32, high, line - high)
    tail = jnp.where(lax.broadcasted_iota(jnp.int32, (16, WIDE), 0) == 0, line, 0.0).astype(BF16)
    for w in range(2):
        for y in range(rel_out.shape[1]):
            at = (w * rel_out.shape[1] + y) * REL_ROWS
            rel_out[w, y, :REL_ROWS, :] = drel[at : at + REL_ROWS, :].astype(BF16)
            rel_out[w, y, REL_ROWS:, :] = tail


def attend(edges, rel_prior, queries, grad_output, key_rows, value_rows, halo_keys, halo_values, rel_weight, halo_rows):
    rows = queries.shape[0]
    halo = halo_keys.shape[0]
    dests = rows // TILE
    sources = (rows + halo) // TILE
    count = edges.shape[1]
    groups = -(-(count // GROUP + dests - 1) // UNROLL) * UNROLL
    places = groups * GROUP
    slabs = 64
    return pl.pallas_call(
        attend_kernel,
        out_shape=(
            jax.ShapeDtypeStruct((rows, 3 * WIDE), BF16),
            jax.ShapeDtypeStruct((slabs, BLOCK, WIDE), BF16),
            jax.ShapeDtypeStruct((2, 2 * RELS * TILE // (2 * REL_ROWS), REL_BLOCK, WIDE), BF16),
        ),
        in_specs=[HBM] * 10,
        out_specs=(VMEM,) * 3,
        scratch_shapes=[
            pltpu.SMEM(edges.shape, jnp.int32),
            pltpu.SMEM((places + 1,), jnp.int32),
            pltpu.SMEM(rel_prior.shape, F32),
            pltpu.VMEM(queries.shape, BF16),
            pltpu.VMEM(grad_output.shape, BF16),
            pltpu.VMEM(rel_weight.shape, BF16),
            pltpu.VMEM(halo_rows.shape, jnp.int32),
            pltpu.VMEM((rows + halo, WIDE), BF16),
            pltpu.VMEM((rows + halo, WIDE), BF16),
            pltpu.SemaphoreType.DMA((10,)),
            pltpu.VMEM((RELS, 2 * WIDE, 2 * WIDE), BF16),
            pltpu.VMEM((dests, 2 * WIDE, 2 * WIDE), BF16),
            pltpu.VMEM((sources, TILE, WIDE), F32),
            pltpu.VMEM((16, WIDE), F32),
            pltpu.VMEM((places, TILE, WIDE), BF16),
            pltpu.VMEM((places, TILE, WIDE), BF16),
            pltpu.VMEM((places, TILE, WIDE), F32),
            pltpu.VMEM((places, TILE, WIDE), F32),
            pltpu.VMEM((places, TILE, WIDE), F32),
            pltpu.VMEM((dests, 1, WIDE), F32),
            pltpu.VMEM((dests, 1, WIDE), F32),
            pltpu.VMEM((16, WIDE), F32),
            pltpu.VMEM((sources, TILE, 2 * WIDE), F32),
            pltpu.VMEM((RELS, WIDE, WIDE), F32),
            pltpu.VMEM((RELS, WIDE, WIDE), F32),
            pltpu.VMEM((dests, WIDE, WIDE), F32),
            pltpu.VMEM((2 * RELS * TILE, WIDE), F32),
            pltpu.VMEM((slabs, WIDE), F32),
        ],
        compiler_params=pltpu.CompilerParams(vmem_limit_bytes=MOST),
        cost_estimate=pl.CostEstimate(flops=3 * 10**9, bytes_accessed=4 * 10**6, transcendentals=400000),
        name="attend",
    )(edges, rel_prior, queries, grad_output, key_rows, value_rows, halo_keys, halo_values, rel_weight, halo_rows)


def bundle_kernel(place, own_ref, nf_ref, types_ref, rel_ref, mine_out, send_out, keep_out, rel_out):
    rel_out[...] = rel_ref[1 - place[0]]
    keep_out[...] = rel_ref[place[0]]
    rows, feats = nf_ref.shape
    turned = jnp.transpose(nf_ref[...], (1, 0)).astype(F32).reshape(feats // 16, 2, 8, rows)
    low = turned[:, 0].reshape(feats // 2, rows)
    high = turned[:, 1].reshape(feats // 2, rows)
    even = place[0] == 0
    mine_out[...] = jnp.where(even, low, high).astype(BF16)
    send_out[:, :rows] = jnp.where(even, high, low).astype(BF16)
    for j in range(rows // WIDE):
        kinds = column(types_ref[j : j + 1, :].astype(F32)).astype(BF16)
        send_out[j * WIDE : (j + 1) * WIDE, rows + WIDE :] = kinds
    send_out[:, rows : rows + WIDE] = own_ref[:, :WIDE]


def bundle(place, own, node_feats, node_types, rel):
    rows, feats = node_feats.shape
    return pl.pallas_call(
        bundle_kernel,
        out_shape=(
            jax.ShapeDtypeStruct((feats // 2, rows), BF16),
            jax.ShapeDtypeStruct((feats // 2, rows + 2 * WIDE), BF16),
            jax.ShapeDtypeStruct(rel.shape[1:], BF16),
            jax.ShapeDtypeStruct(rel.shape[1:], BF16),
        ),
        in_specs=[SMEM] + [VMEM] * 4,
        out_specs=(VMEM,) * 4,
        compiler_params=pltpu.CompilerParams(vmem_limit_bytes=LIMIT),
        cost_estimate=pl.CostEstimate(flops=10**6, bytes_accessed=2 * 10**6, transcendentals=0),
        name="bundle",
    )(place, own, node_feats, node_types, rel)


def spread(place, products, outs):
    size = outs[0].shape[0]
    for d in range(len(outs)):
        block = lax.rem(place[1] + d, len(outs))
        outs[d][:, : products.shape[1]] = products[pl.ds(pl.multiple_of(block * size, size), size), :]


def project_queries_kernel(place, mine_ref, sent_ref, got_ref, rel_ref, rel_got_ref, pair_out, *refs):
    outs, products = refs[:-1], refs[-1]
    rows = mine_ref.shape[1]
    pair_out[:, :rows] = mine_ref[...]
    pair_out[:, rows:] = got_ref[:, :rows]
    query = jnp.concatenate([ref[:, rows : rows + WIDE] for ref in (sent_ref, got_ref)], axis=0).astype(F32)
    kinds = jnp.concatenate([ref[:, rows + WIDE :] for ref in (sent_ref, got_ref)], axis=0).astype(F32)
    for t in range(TYPES):
        masked = jnp.where(kinds == float(t), query, 0.0).astype(BF16)
        products[:, t * WIDE : (t + 1) * WIDE] = mul(pair_out[...], masked, NN).astype(BF16)
    spread(place, products, outs)
    for d in range(len(outs)):
        block = lax.rem(place[1] + d, len(outs))
        both = with_line(rel_ref[block].astype(F32) + rel_got_ref[block].astype(F32)).astype(BF16)
        for k in range(REL_BLOCK // TILE):
            at = (TYPES + k) * WIDE
            outs[d][:, at : at + WIDE] = both[k * TILE : (k + 1) * TILE, :]


def project_queries(place, mine, sent, got, rel, rel_got, count):
    feats, rows = mine.shape
    wide = TYPES * WIDE
    more = REL_BLOCK // TILE * WIDE
    return pl.pallas_call(
        project_queries_kernel,
        out_shape=(jax.ShapeDtypeStruct((feats, 2 * rows), BF16),)
        + (jax.ShapeDtypeStruct((feats // count, wide + more), BF16),) * count,
        in_specs=[SMEM] + [VMEM] * 5,
        out_specs=(VMEM,) * (1 + count),
        scratch_shapes=[pltpu.VMEM((feats, wide), BF16)],
        compiler_params=pltpu.CompilerParams(vmem_limit_bytes=LIMIT),
        cost_estimate=pl.CostEstimate(flops=10**9, bytes_accessed=2 * 10**6, transcendentals=0),
        name="project_queries",
    )(place, mine, sent, got, rel, rel_got)


def collect_kernel(own_ref, inc_ref, kv_out):
    rows = own_ref.shape[0]
    slabs = inc_ref.shape[0]
    row = lax.broadcasted_iota(jnp.int32, (16, WIDE), 0)
    block = lax.broadcasted_iota(jnp.int32, (16, WIDE), 1) // 8
    node = lax.broadcasted_iota(jnp.int32, (rows, WIDE), 0).astype(F32)
    back = own_ref[:, WIDE:].astype(F32)
    for c in range(slabs // 16):
        grads = inc_ref[16 * c : 16 * c + 16].astype(F32)
        ids = grads[:, 16, :]
        line = jnp.sum(jnp.where(row == block, ids, 0.0), axis=0, keepdims=True)
        pick = (node == line).astype(F32).astype(BF16)
        both = jnp.concatenate(
            [grads[:, :8].reshape(WIDE, WIDE), grads[:, 8:16].reshape(WIDE, WIDE)], axis=1
        )
        back = back + mul(pick, both.astype(BF16), NN)
    kv_out[...] = back.astype(BF16)


def collect(own, incoming):
    rows = own.shape[0]
    return pl.pallas_call(
        collect_kernel,
        out_shape=jax.ShapeDtypeStruct((rows, 2 * WIDE), BF16),
        in_specs=[VMEM, VMEM],
        out_specs=VMEM,
        compiler_params=pltpu.CompilerParams(vmem_limit_bytes=LIMIT),
        cost_estimate=pl.CostEstimate(flops=10**8, bytes_accessed=10**6, transcendentals=0),
        name="collect",
    )(own, incoming)


def relation_places_kernel(*refs):
    out = refs[-1]
    parts = []
    for k in range(REL_BLOCK // TILE):
        at = (TYPES + k) * WIDE
        total = refs[0][:, at : at + WIDE].astype(F32)
        for ref in refs[1:-1]:
            total = total + ref[:, at : at + WIDE].astype(F32)
        parts.append(total)
    total = with_line(jnp.concatenate(parts, axis=0)).astype(BF16)
    for z in range(out.shape[0]):
        out[z] = total


def relation_places(arrived, count):
    return pl.pallas_call(
        relation_places_kernel,
        out_shape=jax.ShapeDtypeStruct((count, REL_BLOCK, WIDE), BF16),
        in_specs=[VMEM] * len(arrived),
        out_specs=VMEM,
        compiler_params=pltpu.CompilerParams(vmem_limit_bytes=LIMIT),
        cost_estimate=pl.CostEstimate(flops=10**6, bytes_accessed=10**6, transcendentals=0),
        name="relation_places",
    )(*arrived)


def relation_sum_kernel(inc_ref, rel_out, prior_out):
    total = inc_ref[0].astype(F32)
    for s in range(1, inc_ref.shape[0]):
        total = total + inc_ref[s].astype(F32)
    rel_out[...] = total.astype(BF16)
    line = total[REL_ROWS : REL_ROWS + 1, :]
    line = line + pltpu.roll(line, WIDE - 32, 1)
    prior_out[0:1, :] = line[:, :RELS]
    prior_out[1:2, :] = pltpu.roll(line, WIDE - 16, 1)[:, :RELS]


def relation_sum(incoming):
    return pl.pallas_call(
        relation_sum_kernel,
        out_shape=(
            jax.ShapeDtypeStruct(incoming.shape[1:], BF16),
            jax.ShapeDtypeStruct((2, RELS), F32),
        ),
        in_specs=[VMEM],
        out_specs=(VMEM,) * 2,
        compiler_params=pltpu.CompilerParams(vmem_limit_bytes=LIMIT),
        cost_estimate=pl.CostEstimate(flops=10**6, bytes_accessed=10**6, transcendentals=0),
        name="relation_sum",
    )(incoming)


def project_kernel(place, pair_ref, kv_ref, got_kv_ref, sent_ref, got_ref, *refs):
    outs, products = refs[:-1], refs[-1]
    rows = kv_ref.shape[0]
    kinds = jnp.concatenate([ref[:, rows + WIDE :] for ref in (sent_ref, got_ref)], axis=0).astype(F32)
    for p in range(2):
        part = jnp.concatenate(
            [ref[:, p * WIDE : (p + 1) * WIDE] for ref in (kv_ref, got_kv_ref)], axis=0
        ).astype(F32)
        for t in range(TYPES):
            at = (p * TYPES + t) * WIDE
            masked = jnp.where(kinds == float(t), part, 0.0).astype(BF16)
            products[:, at : at + WIDE] = mul(pair_ref[...], masked, NN).astype(BF16)
    spread(place, products, outs)


def project(place, pair, kv, got_kv, sent, got, count):
    feats = pair.shape[0]
    wide = 2 * TYPES * WIDE
    return pl.pallas_call(
        project_kernel,
        out_shape=(jax.ShapeDtypeStruct((feats // count, wide), BF16),) * count,
        in_specs=[SMEM] + [VMEM] * 5,
        out_specs=(VMEM,) * count,
        scratch_shapes=[pltpu.VMEM((feats, wide), BF16)],
        compiler_params=pltpu.CompilerParams(vmem_limit_bytes=LIMIT),
        cost_estimate=pl.CostEstimate(flops=10**9, bytes_accessed=4 * 10**6, transcendentals=0),
        name="project",
    )(place, pair, kv, got_kv, sent, got)


def features_kernel(place, sent_ref, kv_ref, w_ref, *refs):
    outs, total = refs[:-1], refs[-1]
    rows = kv_ref.shape[0]
    kinds = sent_ref[:, rows + WIDE :].astype(F32)
    acc = None
    for p in range(3):
        part = sent_ref[:, rows : rows + WIDE] if p == 0 else kv_ref[:, (p - 1) * WIDE : p * WIDE]
        part = part.astype(F32)
        for t in range(TYPES):
            masked = jnp.where(kinds == float(t), part, 0.0).astype(BF16)
            term = mul(masked, w_ref[p * TYPES + t], NT)
            acc = term if acc is None else acc + term
    for h in range(len(outs)):
        total[h] = acc[:, h * WIDE : (h + 1) * WIDE]
    me = place[2]
    first = me + 1 - 2 * lax.rem(me, 2)
    for out, owner in zip(outs, (me, 3 - me, first, 3 - first)):
        out[...] = total[owner].astype(BF16)


def features(place, sent, kv, weights):
    rows = kv.shape[0]
    count = weights.shape[1] // WIDE
    return pl.pallas_call(
        features_kernel,
        out_shape=(jax.ShapeDtypeStruct((rows, WIDE), BF16),) * count,
        in_specs=[SMEM, VMEM, VMEM, VMEM],
        out_specs=(VMEM,) * count,
        scratch_shapes=[pltpu.VMEM((count, rows, WIDE), F32)],
        compiler_params=pltpu.CompilerParams(vmem_limit_bytes=LIMIT),
        cost_estimate=pl.CostEstimate(flops=10**9, bytes_accessed=3 * 10**6, transcendentals=0),
        name="features",
    )(place, sent, kv, weights)


def relation_kernel(place, mine_ref, first_ref, last_ref, c_mine_ref, c_first_ref, c_last_ref, out_ref, flat):
    y = place[1]
    last = 3 - y
    owners = (y, y + 1 - 2 * lax.rem(y, 2), last, last + 1 - 2 * lax.rem(last, 2))
    for core, refs in (
        (place[0], (mine_ref, first_ref, last_ref.at[0], last_ref.at[1])),
        (1 - place[0], (c_mine_ref, c_first_ref, c_last_ref.at[0], c_last_ref.at[1])),
    ):
        for owner, ref in zip(owners, refs):
            at = pl.multiple_of((core * len(owners) + owner) * REL_ROWS, 16)
            flat[pl.ds(at, REL_ROWS), :] = ref[:REL_ROWS, :].astype(F32)
    for w in range(2):
        for r in range(RELS):
            at = (w * RELS + r) * TILE
            for h in range(2):
                out_ref[w, r, h] = flat[at : at + TILE, h * TILE : (h + 1) * TILE]


def relations(place, *blocks):
    return pl.pallas_call(
        relation_kernel,
        out_shape=jax.ShapeDtypeStruct((2, RELS, 2, TILE, TILE), F32),
        in_specs=[SMEM] + [VMEM] * 6,
        out_specs=VMEM,
        scratch_shapes=[pltpu.VMEM((2 * RELS * TILE, WIDE), F32)],
        compiler_params=pltpu.CompilerParams(vmem_limit_bytes=LIMIT),
        cost_estimate=pl.CostEstimate(flops=10**6, bytes_accessed=3 * 10**6, transcendentals=0),
        name="relations",
    )(place, *blocks)


def place_sum_kernel(*refs):
    out = refs[-1]
    half = (len(refs) - 1) // 2
    narrow = TYPES * WIDE
    for at, group in ((0, refs[:half]), (narrow, refs[half:-1])):
        width = narrow if at == 0 else group[0].shape[1]
        total = group[0][:, :width].astype(F32)
        for ref in group[1:]:
            total = total + ref[:, :width].astype(F32)
        out[:, at : at + width] = total.astype(BF16)


def place_sum(query, rest):
    rows = query[0].shape[0]
    return pl.pallas_call(
        place_sum_kernel,
        out_shape=jax.ShapeDtypeStruct((rows, PROJ * WIDE), BF16),
        in_specs=[VMEM] * (len(query) + len(rest)),
        out_specs=VMEM,
        compiler_params=pltpu.CompilerParams(vmem_limit_bytes=LIMIT),
        cost_estimate=pl.CostEstimate(flops=10**6, bytes_accessed=10**6, transcendentals=0),
        name="place_sum",
    )(*query, *rest)


def shifted(blocks, axis):
    count = len(blocks)
    return [blocks[0]] + [
        lax.ppermute(blocks[d], axis, [(i, (i + d) % count) for i in range(count)])
        for d in range(1, count)
    ]


def per_device(
    node_feats,
    node_types,
    queries,
    key_rows,
    value_rows,
    halo_keys,
    halo_values,
    halo_rows,
    edge_tiles,
    grad_output,
    proj_weight,
    rel_weight,
    rel_prior,
):
    y_count = lax.axis_size("y")
    z_count = lax.axis_size("z")
    place = jnp.stack(
        [lax.axis_index("core"), lax.axis_index("y"), lax.axis_index("heads")]
    ).astype(jnp.int32)
    swap = [(0, 1), (1, 0)]
    own, send, rel = attend(
        edge_tiles.T,
        rel_prior.T,
        queries,
        grad_output,
        key_rows,
        value_rows,
        halo_keys,
        halo_values,
        rel_weight,
        halo_rows.reshape(-1, WIDE),
    )
    incoming = lax.all_to_all(send, ("y", "z", "core"), 0, 0, tiled=True)
    feats_t, sent, rel, rel_theirs = bundle(place, own, node_feats, node_types.reshape(-1, WIDE), rel)
    got = lax.ppermute(sent, "core", swap)
    rel_got = lax.ppermute(rel_theirs, "core", swap)
    pair, *q_blocks = project_queries(place, feats_t, sent, got, rel, rel_got, y_count)
    q_arrived = shifted(q_blocks, "y")
    own, *q_blocks = lax.optimization_barrier((own, *q_blocks))
    kv = collect(own, incoming)
    got_kv = lax.ppermute(kv, "core", swap)
    kv, *q_arrived = lax.optimization_barrier((kv, *q_arrived))
    rel_z = lax.all_to_all(relation_places(q_arrived, z_count), "z", 0, 0, tiled=True)
    arrived = shifted(project(place, pair, kv, got_kv, sent, got, y_count), "y")
    feat_blocks = features(place, sent, kv, proj_weight.reshape(PROJ, -1, WIDE))
    mine, partners, *away = feat_blocks
    away = [lax.ppermute(block, "heads", [(0, 1), (1, 0), (2, 3), (3, 2)]) for block in away]
    arrived[0], got_mine, got_partners = lax.optimization_barrier((arrived[0], *away))
    partners = partners.astype(F32) + got_partners.astype(F32)
    last = lax.ppermute(partners.astype(BF16), "heads", [(0, 3), (3, 0), (1, 2), (2, 1)])
    grad_feats = (mine.astype(F32) + got_mine.astype(F32) + last.astype(F32)).astype(BF16)
    by_y = place_sum(q_arrived, arrived)
    next_y = [(0, 1), (1, 0), (2, 3), (3, 2)]
    last_y = [(0, 3), (3, 0), (1, 2), (2, 1)]
    rel_z, by_y = lax.optimization_barrier((rel_z, by_y))
    by_z = lax.all_to_all(by_y.reshape(z_count, -1, PROJ * WIDE), "z", 0, 0, tiled=True)
    rel_mine, prior = relation_sum(rel_z)
    rel_first = lax.ppermute(rel_mine, "y", next_y)
    rel_last = lax.ppermute(jnp.stack([rel_mine, rel_first]), "y", last_y)
    blocks = (rel_mine, rel_first, rel_last)
    grad_rel = relations(place, *blocks, *(lax.ppermute(block, "core", swap) for block in blocks))
    by_z, grad_rel, grad_feats = lax.optimization_barrier((by_z, grad_rel, grad_feats))
    grad_proj = jnp.sum(by_z.astype(F32), axis=0).reshape(-1, 3, TYPES, WIDE)
    grad_prior = prior.T
    return (grad_feats, grad_proj, grad_rel, grad_prior)


def solution(mesh):
    heads = mesh.devices.shape[1]
    split = Mesh(mesh.devices.reshape(4, 8, 2, heads), ("y", "z", "core", "heads"))
    nodes = ("y", "z", "core")
    return jax.shard_map(
        per_device,
        mesh=split,
        in_specs=(
            P(nodes, None),
            P(nodes),
            P(nodes, "heads"),
            P(nodes, "heads"),
            P(nodes, "heads"),
            P(nodes, "heads"),
            P(nodes, "heads"),
            P(nodes),
            P(nodes, None),
            P(nodes, "heads"),
            P(None, None, None, "heads"),
            P(None, None, "heads", None, None),
            P(None, "heads"),
        ),
        out_specs=(
            P(nodes, "heads"),
            P(nodes, None, None, "heads"),
            P(None, None, "heads", None, None),
            P(None, "heads"),
        ),
        check_vma=False,
    )
```

time: 96.1 us -> 86.3 us (0.90)
  waiting for transfers between devices: 24.1 us -> 14.1 us
  starting transfers between devices: 42.2 us -> 49.9 us
  Pallas kernels: 25 us -> 17.4 us
  local copies, waits for them, and re-layouts: 0.95 us -> 1.98 us
    ppermute x9 -> x6, waiting for transfers between devices: 13.7 us -> 3.47 us  [shifted(): lax.ppermute(blocks[d], axis, [(i, (i + d) % count) for i in range(count)])]
    ppermute x1 -> x9, starting transfers between devices: 1.96 us -> 10.4 us  [the longest x3 3.56 us: per_device(): lax.ppermute(block, 'core', swap)]
    pallas_call x1, Pallas kernels: 14.7 us -> 7.27 us  [attend(): pl.pallas_call(attend_kernel, out_shape=(jax.ShapeDtypeStruct((rows, 3 *...]
    ppermute x9 -> x6, starting transfers between devices: 15.1 us -> 9.29 us  [shifted(): lax.ppermute(blocks[d], axis, [(i, (i + d) % count) for i in range(count)])]
    ppermute x1 -> x9, waiting for transfers between devices: 0.01 us -> 4.87 us  [the longest x2 3.48 us: per_device(): lax.ppermute(block, 'heads', [(0, 1), (1, 0), (2, 3), (3, 2)])]
    all_to_all x1, waiting for transfers between devices: 6.9 us -> 3.51 us  [per_device(): incoming = lax.all_to_all(send, ('y', 'z', 'core'), 0, 0, tiled=True)]
    all_to_all x1, starting transfers between devices: 13.2 us -> 16.5 us  [per_device(): incoming = lax.all_to_all(send, ('y', 'z', 'core'), 0, 0, tiled=True)]
    all_to_all x1, starting transfers between devices: 5.36 us -> 6.85 us  [per_device(): lax.all_to_all(by_y.reshape(z_count, -1, PROJ * WIDE), 'z', 0, 0, tiled=T...]
  transfers between devices with their start and end apart: 15 -> 20, of which waited for: 9 -> 10; matrix products, arithmetic and copies ran while one was open for 1% -> 1% of each run, Pallas kernels for 6% -> 10%
where the time goes in v2:
time: 86.3 us; the launch traced here: 85.6 us
  starting transfers between devices  49.9 us (58%)
  Pallas kernels  17.4 us (20%)
  waiting for transfers between devices  14.1 us (16%)
  local copies, waits for them, and re-layouts  1.98 us (2%)
  other arithmetic  1.43 us (2%)
    all_to_all x1, starting transfers between devices, per_device(): incoming = lax.all_to_all(send, ('y', 'z', 'core'), 0, 0, tiled=True)  16.5 us
    ppermute x6, starting transfers between devices, shifted(): lax.ppermute(blocks[d], axis, [(i, (i + d) % count) for i in range(count)])  9.29 us
    pallas_call x1, Pallas kernels, attend(): pl.pallas_call(attend_kernel, out_shape=(jax.ShapeDtypeStruct((rows, 3 *...  7.27 us
    all_to_all x1, starting transfers between devices, per_device(): lax.all_to_all(by_y.reshape(z_count, -1, PROJ * WIDE), 'z', 0, 0, tiled=T...  6.85 us
    all_to_all x1, starting transfers between devices, per_device(): lax.all_to_all(relation_places(q_arrived, z_count), 'z', 0, 0, tiled=True)  5.29 us
    ppermute x3, starting transfers between devices, per_device(): lax.ppermute(block, 'core', swap)  3.56 us
    all_to_all x1, waiting for transfers between devices, per_device(): incoming = lax.all_to_all(send, ('y', 'z', 'core'), 0, 0, tiled=True)  3.51 us
    ppermute x2, waiting for transfers between devices, per_device(): lax.ppermute(block, 'heads', [(0, 1), (1, 0), (2, 3), (3, 2)])  3.48 us
  transfers between devices with their start and end apart: 20, of which 10 were waited for; matrix products, arithmetic and copies ran while one was open for 1% of the time, Pallas kernels for 10%

profile of v2, /device:TPU:1, one launch (start us, length us, event | category | flops | bytes accessed | tf_op | source)
XLA Modules:
  0.0 85.6 jit_solution(1427243473994873514)
XLA Ops:
  0.7 7.3 %attend.1 = (bf16[256,384]{1,0:T(8,128)(2,1)}, bf16[64,24,128]{2,1,0:T(8,128)(2,1)}, bf16[2,4,256,128]{3,2,1,0:T(8,128)(2,1)}) custom-call(s32[3,40]{1,0:T(4,128)} %bitcast.18, f32[2,15]{1,0:T(2,128)} %bitcast.20, bf16[256,128]{1,0:T(8,128)(2,1)} %q_hbm.1, bf16[256,128]{1,0:T(8,128)(2,1)} %g_hbm.1, bf16[256,128]{1,0:T(8,128)(2,1)} %ko_hbm.1, ...), custom_call_target="tpu_custom_call" | custom-call | flops 3000000000 | bytes 4000000 | tf_op jit(solution)/shard_map/attend/pallas_call | solution.py:268
  7.9 16.5 %all-to-all-start = ((bf16[64,24,128]{2,1,0:T(8,128)(2,1)}), bf16[64,24,128]{2,1,0:T(8,128)(2,1)S(1)}, u32[]{:S(2)}, u32[]{:S(2)}) async-start(bf16[64,24,128]{2,1,0:T(8,128)(2,1)} %get-tuple-element.51), calls=%async_computation | async-start | bytes 786432 | tf_op jit(solution)/shard_map/all_to_all | solution.py:636
  27.9 1.1 %collective-permute-done.1.rel_got_ref = bf16[4,256,128]{2,1,0:T(8,128)(2,1)S(1)} collective-permute-done((bf16[4,256,128]{2,1,0:T(8,128)(2,1)S(1)}, bf16[4,256,128]{2,1,0:T(8,128)(2,1)S(1)}, u32[]{:S(2)}, u32[]{:S(2)}) %collective-permute-start.1) | collective-permute-done | bytes 262176 | tf_op jit(solution)/shard_map/ppermute | solution.py:639
  29.3 1.2 %project_queries.1 = (bf16[256,512]{1,0:T(8,128)(2,1)S(1)}, bf16[64,1152]{1,0:T(8,128)(2,1)S(1)}, bf16[64,1152]{1,0:T(8,128)(2,1)S(1)}, bf16[64,1152]{1,0:T(8,128)(2,1)S(1)}, bf16[64,1152]{1,0:T(8,128)(2,1)S(1)}) custom-call(s32[3]{0:T(128)S(1)} %pad_add_fusion.place, bf16[256,256]{1,0:T(8,128)(2,1)S(1)} %get-tuple-element.42.mine_ref, ...), custom_call_target="tpu_custom_call" | custom-call | flops 1000000000 | bytes 2000000 | tf_op jit(solution)/shard_map/project_queries/pallas_call | solution.py:377
  30.5 1.4 %collective-permute-start.2 = (bf16[64,1152]{1,0:T(8,128)(2,1)S(1)}, bf16[64,1152]{1,0:T(8,128)(2,1)S(1)}, u32[]{:S(2)}, u32[]{:S(2)}) collective-permute-start(bf16[64,1152]{1,0:T(8,128)(2,1)S(1)} %get-tuple-element.47), channel_id=1, source_target_pairs={{0,64},{64,128},{128,192},{192,0},{1,65},{65,129},{129,193},{193,1... | collective-permute-start | bytes 442376 | tf_op jit(solution)/shard_map/ppermute | solution.py:598
  31.9 2.6 %collective-permute-start.3 = (bf16[64,1152]{1,0:T(8,128)(2,1)S(1)}, bf16[64,1152]{1,0:T(8,128)(2,1)S(1)}, u32[]{:S(2)}, u32[]{:S(2)}) collective-permute-start(bf16[64,1152]{1,0:T(8,128)(2,1)S(1)} %get-tuple-element.48), channel_id=1, source_target_pairs={{0,128},{64,192},{128,0},{192,64},{1,129},{65,193},{129,1},{193,65... | collective-permute-start | bytes 442376 | tf_op jit(solution)/shard_map/ppermute | solution.py:598
  34.5 1.1 %collective-permute-start.4 = (bf16[64,1152]{1,0:T(8,128)(2,1)S(1)}, bf16[64,1152]{1,0:T(8,128)(2,1)S(1)}, u32[]{:S(2)}, u32[]{:S(2)}) collective-permute-start(bf16[64,1152]{1,0:T(8,128)(2,1)S(1)} %get-tuple-element.49), channel_id=1, source_target_pairs={{0,192},{64,0},{128,64},{192,128},{1,193},{65,1},{129,65},{193,129... | collective-permute-start | bytes 442376 | tf_op jit(solution)/shard_map/ppermute | solution.py:598
  35.5 3.5 %all-to-all-done.inc_ref = bf16[64,24,128]{2,1,0:T(8,128)(2,1)S(1)} async-done(((bf16[64,24,128]{2,1,0:T(8,128)(2,1)}), bf16[64,24,128]{2,1,0:T(8,128)(2,1)S(1)}, u32[]{:S(2)}, u32[]{:S(2)}) %all-to-all-start) | async-done | bytes 393248 | tf_op jit(solution)/shard_map/all_to_all | solution.py:636
  39.5 3.3 %collective-permute-done.3.refs_2_ = bf16[64,1152]{1,0:T(8,128)(2,1)S(1)} collective-permute-done((bf16[64,1152]{1,0:T(8,128)(2,1)S(1)}, bf16[64,1152]{1,0:T(8,128)(2,1)S(1)}, u32[]{:S(2)}, u32[]{:S(2)}) %collective-permute-start.3) | collective-permute-done | bytes 147488 | tf_op jit(solution)/shard_map/ppermute | solution.py:598
  43.8 5.3 %all-to-all-start.1 = ((bf16[8,256,128]{2,1,0:T(8,128)(2,1)}), bf16[8,256,128]{2,1,0:T(8,128)(2,1)S(1)}, u32[]{:S(2)}, u32[]{:S(2)}) async-start(bf16[8,256,128]{2,1,0:T(8,128)(2,1)} %relation_places.1), calls=%async_computation.1 | async-start | bytes 1048576 | tf_op jit(solution)/shard_map/all_to_all | solution.py:646
  49.1 1.4 %collective-permute-start.5 = (bf16[256,256]{1,0:T(8,128)(2,1)S(1)}, bf16[256,256]{1,0:T(8,128)(2,1)S(1)}, u32[]{:S(2)}, u32[]{:S(2)}) collective-permute-start(bf16[256,256]{1,0:T(8,128)(2,1)S(1)} %collect.1.kv_ref), channel_id=1, source_target_pairs={{0,4},{4,0},{1,5},{5,1},{2,6},{6,2},{3,7},{7,3},{8,12},{12,8},{9,1... | collective-permute-start | bytes 393224 | tf_op jit(solution)/shard_map/ppermute | solution.py:644
  51.5 1.5 %project.1 = (bf16[64,1280]{1,0:T(8,128)(2,1)S(1)}, bf16[64,1280]{1,0:T(8,128)(2,1)S(1)}, bf16[64,1280]{1,0:T(8,128)(2,1)S(1)}, bf16[64,1280]{1,0:T(8,128)(2,1)S(1)}) custom-call(s32[3]{0:T(128)S(1)} %pad_add_fusion.place, bf16[256,512]{1,0:T(8,128)(2,1)S(1)} %get-tuple-element.56.pair_ref, bf16[256,256]{1,0:T(8,128)(2,1)S(1)} %collect.1.kv_ref, ...), custom_call_target="tpu_custom_call" | custom-call | flops 1000000000 | bytes 4000000 | tf_op jit(solution)/shard_map/project/pallas_call | solution.py:492
  54.0 2.0 %collective-permute-start.9 = (bf16[64,1280]{1,0:T(8,128)(2,1)S(1)}, bf16[64,1280]{1,0:T(8,128)(2,1)S(1)}, u32[]{:S(2)}, u32[]{:S(2)}) collective-permute-start(bf16[64,1280]{1,0:T(8,128)(2,1)S(1)} %get-tuple-element.63), channel_id=1, source_target_pairs={{0,128},{64,192},{128,0},{192,64},{1,129},{65,193},{129,1},{193,65... | collective-permute-start | bytes 491528 | tf_op jit(solution)/shard_map/ppermute | solution.py:598
  56.0 1.2 %collective-permute-start.10 = (bf16[64,1280]{1,0:T(8,128)(2,1)S(1)}, bf16[64,1280]{1,0:T(8,128)(2,1)S(1)}, u32[]{:S(2)}, u32[]{:S(2)}) collective-permute-start(bf16[64,1280]{1,0:T(8,128)(2,1)S(1)} %get-tuple-element.64), channel_id=1, source_target_pairs={{0,192},{64,0},{128,64},{192,128},{1,193},{65,1},{129,65},{193,129... | collective-permute-start | bytes 491528 | tf_op jit(solution)/shard_map/ppermute | solution.py:598
  57.2 1.7 %features.1 = (bf16[256,128]{1,0:T(8,128)(2,1)S(1)}, bf16[256,128]{1,0:T(8,128)(2,1)S(1)}, bf16[256,128]{1,0:T(8,128)(2,1)S(1)}, bf16[256,128]{1,0:T(8,128)(2,1)S(1)}) custom-call(s32[3]{0:T(128)S(1)} %pad_add_fusion.place, bf16[256,512]{1,0:T(8,128)(2,1)S(1)} %get-tuple-element.43.sent_ref, bf16[256,256]{1,0:T(8,128)(2,1)S(1)} %collect.1.kv_ref, ...), custom_call_target="tpu_custom_call" | custom-call | flops 1000000000 | bytes 3000000 | tf_op jit(solution)/shard_map/features/pallas_call | solution.py:527
  59.0 1.3 %collective-permute-start.6 = (bf16[256,128]{1,0:T(8,128)(2,1)S(1)}, bf16[256,128]{1,0:T(8,128)(2,1)S(1)}, u32[]{:S(2)}, u32[]{:S(2)}) collective-permute-start(bf16[256,128]{1,0:T(8,128)(2,1)S(1)} %get-tuple-element.59), channel_id=1, source_target_pairs={{0,1},{1,0},{2,3},{3,2},{4,5},{5,4},{6,7},{7,6},{8,9},{9,8},{10,11... | collective-permute-start | bytes 196616 | tf_op jit(solution)/shard_map/ppermute | solution.py:650
  60.5 1.9 %collective-permute-done.6 = bf16[256,128]{1,0:T(8,128)(2,1)S(1)} collective-permute-done((bf16[256,128]{1,0:T(8,128)(2,1)S(1)}, bf16[256,128]{1,0:T(8,128)(2,1)S(1)}, u32[]{:S(2)}, u32[]{:S(2)}) %collective-permute-start.6) | collective-permute-done | bytes 65568 | tf_op jit(solution)/shard_map/ppermute | solution.py:650
  62.5 1.5 %collective-permute-done.7 = bf16[256,128]{1,0:T(8,128)(2,1)S(1)} collective-permute-done((bf16[256,128]{1,0:T(8,128)(2,1)S(1)}, bf16[256,128]{1,0:T(8,128)(2,1)S(1)}, u32[]{:S(2)}, u32[]{:S(2)}) %collective-permute-start.7) | collective-permute-done | bytes 65568 | tf_op jit(solution)/shard_map/ppermute | solution.py:650
  67.5 6.8 %all-to-all-start.2 = ((bf16[8,8,1920]{2,1,0:T(8,128)(2,1)}), bf16[8,8,1920]{2,1,0:T(8,128)(2,1)S(1)}, u32[]{:S(2)}, u32[]{:S(2)}) async-start(bf16[8,8,1920]{2,1,0:T(8,128)(2,1)} %bitcast.8), calls=%async_computation.2 | async-start | bytes 491520 | tf_op jit(solution)/shard_map/all_to_all | solution.py:659
  74.4 1.2 %collective-permute-start.12 = (bf16[2,256,128]{2,1,0:T(8,128)(2,1)S(1)}, bf16[2,256,128]{2,1,0:T(8,128)(2,1)S(1)}, u32[]{:S(2)}, u32[]{:S(2)}) collective-permute-start(bf16[2,256,128]{2,1,0:T(8,128)(2,1)S(1)} %pad_maximum_fusion), channel_id=1, source_target_pairs={{0,192},{192,0},{64,128},{128,64},{1,193},{193,1},{65,129},{129,65... | collective-permute-start | bytes 393224 | tf_op jit(solution)/shard_map/ppermute | solution.py:662
  75.6 2.6 %collective-permute-start.16 = (bf16[256,128]{1,0:T(8,128)(2,1)S(1)}, bf16[256,128]{1,0:T(8,128)(2,1)S(1)}, u32[]{:S(2)}, u32[]{:S(2)}) collective-permute-start(bf16[256,128]{1,0:T(8,128)(2,1)S(1)} %add_convert_fusion.1), channel_id=1, source_target_pairs={{0,3},{3,0},{1,2},{2,1},{4,7},{7,4},{5,6},{6,5},{8,11},{11,8},{9,1... | collective-permute-start | bytes 196616 | tf_op jit(solution)/shard_map/ppermute | solution.py:653
  78.1 1.5 %collective-permute-start.13 = (bf16[256,128]{1,0:T(8,128)(2,1)S(1)}, bf16[256,128]{1,0:T(8,128)(2,1)S(1)}, u32[]{:S(2)}, u32[]{:S(2)}) collective-permute-start(bf16[256,128]{1,0:T(8,128)(2,1)S(1)} %get-tuple-element.67.mine_ref), channel_id=1, source_target_pairs={{0,4},{4,0},{1,5},{5,1},{2,6},{6,2},{3,7},{7,3},{8,12},{12,8},{9,1... | collective-permute-start | bytes 196616 | tf_op jit(solution)/shard_map/ppermute | solution.py:664
  79.6 2.1 %collective-permute-start.15 = (bf16[2,256,128]{2,1,0:T(8,128)(2,1)S(1)}, bf16[2,256,128]{2,1,0:T(8,128)(2,1)S(1)}, u32[]{:S(2)}, u32[]{:S(2)}) collective-permute-start(bf16[2,256,128]{2,1,0:T(8,128)(2,1)S(1)} %collective-permute-done.12.last_ref), channel_id=1, source_target_pairs={{0,4},{4,0},{1,5},{5,1},{2,6},{6,2},{3,7},{7,3},{8,12},{12,8},{9,1... | collective-permute-start | bytes 393224 | tf_op jit(solution)/shard_map/ppermute | solution.py:664
  82.7 2.2 %relations.1 = f32[2,15,2,64,64]{4,3,2,1,0:T(8,128)} custom-call(s32[3]{0:T(128)S(1)} %pad_add_fusion.place, bf16[256,128]{1,0:T(8,128)(2,1)S(1)} %get-tuple-element.67.mine_ref, bf16[256,128]{1,0:T(8,128)(2,1)S(1)} %collective-permute-done.11.first_ref, bf16[2,256,128]{2,1,0:T(8,128)(2,1)S(1)} %collective-permute-done.12.last_ref, ...), custom_call_target="tpu_custom_call" | custom-call | flops 1000000 | bytes 3000000 | tf_op jit(solution)/shard_map/relations/pallas_call | solution.py:558
  (43 shorter events, 12.6 us)
Async XLA Ops:
  0.6 23.9 %copy-start.3 = (bf16[256,512]{1,0:T(8,128)(2,1)S(1)}, bf16[256,512]{1,0:T(8,128)(2,1)}, u32[]{:S(2)}) copy-start(bf16[256,512]{1,0:T(8,128)(2,1)} %nf_ref.1) | copy-start | bytes 786436
  0.6 23.9 %copy-start.4 = (s32[256]{0:T(256)S(1)}, s32[256]{0:T(256)}, u32[]{:S(2)}) copy-start(s32[256]{0:T(256)} %param.14) | copy-start | bytes 3076
  7.9 31.1 %all-to-all-start = ((bf16[64,24,128]{2,1,0:T(8,128)(2,1)}), bf16[64,24,128]{2,1,0:T(8,128)(2,1)S(1)}, u32[]{:S(2)}, u32[]{:S(2)}) async-start(bf16[64,24,128]{2,1,0:T(8,128)(2,1)} %get-tuple-element.51), calls=%async_computation | async-start | bytes 786432 | tf_op jit(solution)/shard_map/all_to_all | solution.py:636
  27.2 11.8 %copy-start.1 = (bf16[256,384]{1,0:T(8,128)(2,1)S(1)}, bf16[256,384]{1,0:T(8,128)(2,1)}, u32[]{:S(2)}) copy-start(bf16[256,384]{1,0:T(8,128)(2,1)} %get-tuple-element.50.own_ref) | copy-start | bytes 589828
  27.2 1.7 %collective-permute-start.1 = (bf16[4,256,128]{2,1,0:T(8,128)(2,1)S(1)}, bf16[4,256,128]{2,1,0:T(8,128)(2,1)S(1)}, u32[]{:S(2)}, u32[]{:S(2)}) collective-permute-start(bf16[4,256,128]{2,1,0:T(8,128)(2,1)S(1)} %get-tuple-element.45), channel_id=1, source_target_pairs={{0,4},{4,0},{1,5},{5,1},{2,6},{6,2},{3,7},{7,3},{8,12},{12,8},{9,1... | collective-permute-start | bytes 786440 | tf_op jit(solution)/shard_map/ppermute | solution.py:639
  27.8 1.5 %collective-permute-start = (bf16[256,512]{1,0:T(8,128)(2,1)S(1)}, bf16[256,512]{1,0:T(8,128)(2,1)S(1)}, u32[]{:S(2)}, u32[]{:S(2)}) collective-permute-start(bf16[256,512]{1,0:T(8,128)(2,1)S(1)} %get-tuple-element.43.sent_ref), channel_id=1, source_target_pairs={{0,4},{4,0},{1,5},{5,1},{2,6},{6,2},{3,7},{7,3},{8,12},{12,8},{9,1... | collective-permute-start | bytes 786440 | tf_op jit(solution)/shard_map/ppermute | solution.py:638
  30.5 9.0 %collective-permute-start.2 = (bf16[64,1152]{1,0:T(8,128)(2,1)S(1)}, bf16[64,1152]{1,0:T(8,128)(2,1)S(1)}, u32[]{:S(2)}, u32[]{:S(2)}) collective-permute-start(bf16[64,1152]{1,0:T(8,128)(2,1)S(1)} %get-tuple-element.47), channel_id=1, source_target_pairs={{0,64},{64,128},{128,192},{192,0},{1,65},{65,129},{129,193},{193,1... | collective-permute-start | bytes 442376 | tf_op jit(solution)/shard_map/ppermute | solution.py:598
  31.9 11.0 %collective-permute-start.3 = (bf16[64,1152]{1,0:T(8,128)(2,1)S(1)}, bf16[64,1152]{1,0:T(8,128)(2,1)S(1)}, u32[]{:S(2)}, u32[]{:S(2)}) collective-permute-start(bf16[64,1152]{1,0:T(8,128)(2,1)S(1)} %get-tuple-element.48), channel_id=1, source_target_pairs={{0,128},{64,192},{128,0},{192,64},{1,129},{65,193},{129,1},{193,65... | collective-permute-start | bytes 442376 | tf_op jit(solution)/shard_map/ppermute | solution.py:598
  34.5 8.4 %collective-permute-start.4 = (bf16[64,1152]{1,0:T(8,128)(2,1)S(1)}, bf16[64,1152]{1,0:T(8,128)(2,1)S(1)}, u32[]{:S(2)}, u32[]{:S(2)}) collective-permute-start(bf16[64,1152]{1,0:T(8,128)(2,1)S(1)} %get-tuple-element.49), channel_id=1, source_target_pairs={{0,192},{64,0},{128,64},{192,128},{1,193},{65,1},{129,65},{193,129... | collective-permute-start | bytes 442376 | tf_op jit(solution)/shard_map/ppermute | solution.py:598
  43.8 22.0 %all-to-all-start.1 = ((bf16[8,256,128]{2,1,0:T(8,128)(2,1)}), bf16[8,256,128]{2,1,0:T(8,128)(2,1)S(1)}, u32[]{:S(2)}, u32[]{:S(2)}) async-start(bf16[8,256,128]{2,1,0:T(8,128)(2,1)} %relation_places.1), calls=%async_computation.1 | async-start | bytes 1048576 | tf_op jit(solution)/shard_map/all_to_all | solution.py:646
  49.1 8.2 %copy-start.5 = (bf16[3,5,512,128]{3,2,1,0:T(8,128)(2,1)S(1)}, bf16[3,5,512,128]{3,2,1,0:T(8,128)(2,1)}, u32[]{:S(2)}) copy-start(bf16[3,5,512,128]{3,2,1,0:T(8,128)(2,1)} %param.23) | copy-start | bytes 5898244
  49.1 2.4 %collective-permute-start.5 = (bf16[256,256]{1,0:T(8,128)(2,1)S(1)}, bf16[256,256]{1,0:T(8,128)(2,1)S(1)}, u32[]{:S(2)}, u32[]{:S(2)}) collective-permute-start(bf16[256,256]{1,0:T(8,128)(2,1)S(1)} %collect.1.kv_ref), channel_id=1, source_target_pairs={{0,4},{4,0},{1,5},{5,1},{2,6},{6,2},{3,7},{7,3},{8,12},{12,8},{9,1... | collective-permute-start | bytes 393224 | tf_op jit(solution)/shard_map/ppermute | solution.py:644
  53.0 11.0 %collective-permute-start.8 = (bf16[64,1280]{1,0:T(8,128)(2,1)S(1)}, bf16[64,1280]{1,0:T(8,128)(2,1)S(1)}, u32[]{:S(2)}, u32[]{:S(2)}) collective-permute-start(bf16[64,1280]{1,0:T(8,128)(2,1)S(1)} %get-tuple-element.62), channel_id=1, source_target_pairs={{0,64},{64,128},{128,192},{192,0},{1,65},{65,129},{129,193},{193,1... | collective-permute-start | bytes 491528 | tf_op jit(solution)/shard_map/ppermute | solution.py:598
  54.0 10.0 %collective-permute-start.9 = (bf16[64,1280]{1,0:T(8,128)(2,1)S(1)}, bf16[64,1280]{1,0:T(8,128)(2,1)S(1)}, u32[]{:S(2)}, u32[]{:S(2)}) collective-permute-start(bf16[64,1280]{1,0:T(8,128)(2,1)S(1)} %get-tuple-element.63), channel_id=1, source_target_pairs={{0,128},{64,192},{128,0},{192,64},{1,129},{65,193},{129,1},{193,65... | collective-permute-start | bytes 491528 | tf_op jit(solution)/shard_map/ppermute | solution.py:598
  56.0 8.0 %collective-permute-start.10 = (bf16[64,1280]{1,0:T(8,128)(2,1)S(1)}, bf16[64,1280]{1,0:T(8,128)(2,1)S(1)}, u32[]{:S(2)}, u32[]{:S(2)}) collective-permute-start(bf16[64,1280]{1,0:T(8,128)(2,1)S(1)} %get-tuple-element.64), channel_id=1, source_target_pairs={{0,192},{64,0},{128,64},{192,128},{1,193},{65,1},{129,65},{193,129... | collective-permute-start | bytes 491528 | tf_op jit(solution)/shard_map/ppermute | solution.py:598
  59.0 3.5 %collective-permute-start.6 = (bf16[256,128]{1,0:T(8,128)(2,1)S(1)}, bf16[256,128]{1,0:T(8,128)(2,1)S(1)}, u32[]{:S(2)}, u32[]{:S(2)}) collective-permute-start(bf16[256,128]{1,0:T(8,128)(2,1)S(1)} %get-tuple-element.59), channel_id=1, source_target_pairs={{0,1},{1,0},{2,3},{3,2},{4,5},{5,4},{6,7},{7,6},{8,9},{9,8},{10,11... | collective-permute-start | bytes 196616 | tf_op jit(solution)/shard_map/ppermute | solution.py:650
  60.3 3.7 %collective-permute-start.7 = (bf16[256,128]{1,0:T(8,128)(2,1)S(1)}, bf16[256,128]{1,0:T(8,128)(2,1)S(1)}, u32[]{:S(2)}, u32[]{:S(2)}) collective-permute-start(bf16[256,128]{1,0:T(8,128)(2,1)S(1)} %get-tuple-element.60), channel_id=1, source_target_pairs={{0,1},{1,0},{2,3},{3,2},{4,5},{5,4},{6,7},{7,6},{8,9},{9,8},{10,11... | collective-permute-start | bytes 196616 | tf_op jit(solution)/shard_map/ppermute | solution.py:650
  66.5 7.9 %collective-permute-start.11 = (bf16[256,128]{1,0:T(8,128)(2,1)S(1)}, bf16[256,128]{1,0:T(8,128)(2,1)S(1)}, u32[]{:S(2)}, u32[]{:S(2)}) collective-permute-start(bf16[256,128]{1,0:T(8,128)(2,1)S(1)} %get-tuple-element.67.mine_ref), channel_id=1, source_target_pairs={{0,64},{64,0},{128,192},{192,128},{1,65},{65,1},{129,193},{193,129... | collective-permute-start | bytes 196616 | tf_op jit(solution)/shard_map/ppermute | solution.py:661
  67.5 17.4 %all-to-all-start.2 = ((bf16[8,8,1920]{2,1,0:T(8,128)(2,1)}), bf16[8,8,1920]{2,1,0:T(8,128)(2,1)S(1)}, u32[]{:S(2)}, u32[]{:S(2)}) async-start(bf16[8,8,1920]{2,1,0:T(8,128)(2,1)} %bitcast.8), calls=%async_computation.2 | async-start | bytes 491520 | tf_op jit(solution)/shard_map/all_to_all | solution.py:659
  74.4 5.2 %collective-permute-start.12 = (bf16[2,256,128]{2,1,0:T(8,128)(2,1)S(1)}, bf16[2,256,128]{2,1,0:T(8,128)(2,1)S(1)}, u32[]{:S(2)}, u32[]{:S(2)}) collective-permute-start(bf16[2,256,128]{2,1,0:T(8,128)(2,1)S(1)} %pad_maximum_fusion), channel_id=1, source_target_pairs={{0,192},{192,0},{64,128},{128,64},{1,193},{193,1},{65,129},{129,65... | collective-permute-start | bytes 393224 | tf_op jit(solution)/shard_map/ppermute | solution.py:662
  75.6 6.1 %collective-permute-start.16 = (bf16[256,128]{1,0:T(8,128)(2,1)S(1)}, bf16[256,128]{1,0:T(8,128)(2,1)S(1)}, u32[]{:S(2)}, u32[]{:S(2)}) collective-permute-start(bf16[256,128]{1,0:T(8,128)(2,1)S(1)} %add_convert_fusion.1), channel_id=1, source_target_pairs={{0,3},{3,0},{1,2},{2,1},{4,7},{7,4},{5,6},{6,5},{8,11},{11,8},{9,1... | collective-permute-start | bytes 196616 | tf_op jit(solution)/shard_map/ppermute | solution.py:653
  78.1 4.2 %collective-permute-start.13 = (bf16[256,128]{1,0:T(8,128)(2,1)S(1)}, bf16[256,128]{1,0:T(8,128)(2,1)S(1)}, u32[]{:S(2)}, u32[]{:S(2)}) collective-permute-start(bf16[256,128]{1,0:T(8,128)(2,1)S(1)} %get-tuple-element.67.mine_ref), channel_id=1, source_target_pairs={{0,4},{4,0},{1,5},{5,1},{2,6},{6,2},{3,7},{7,3},{8,12},{12,8},{9,1... | collective-permute-start | bytes 196616 | tf_op jit(solution)/shard_map/ppermute | solution.py:664
  79.6 2.8 %collective-permute-start.14 = (bf16[256,128]{1,0:T(8,128)(2,1)S(1)}, bf16[256,128]{1,0:T(8,128)(2,1)S(1)}, u32[]{:S(2)}, u32[]{:S(2)}) collective-permute-start(bf16[256,128]{1,0:T(8,128)(2,1)S(1)} %collective-permute-done.11.first_ref), channel_id=1, source_target_pairs={{0,4},{4,0},{1,5},{5,1},{2,6},{6,2},{3,7},{7,3},{8,12},{12,8},{9,1... | collective-permute-start | bytes 196616 | tf_op jit(solution)/shard_map/ppermute | solution.py:664
  79.6 3.1 %collective-permute-start.15 = (bf16[2,256,128]{2,1,0:T(8,128)(2,1)S(1)}, bf16[2,256,128]{2,1,0:T(8,128)(2,1)S(1)}, u32[]{:S(2)}, u32[]{:S(2)}) collective-permute-start(bf16[2,256,128]{2,1,0:T(8,128)(2,1)S(1)} %collective-permute-done.12.last_ref), channel_id=1, source_target_pairs={{0,4},{4,0},{1,5},{5,1},{2,6},{6,2},{3,7},{7,3},{8,12},{12,8},{9,1... | collective-permute-start | bytes 393224 | tf_op jit(solution)/shard_map/ppermute | solution.py:664
  (2 other events, 2.0 us)

commit v3 on v2

--- a/solution.py
+++ b/solution.py
@@ -10,7 +10,7 @@
 TILE = 64
 WIDE = 128
 GROUP = 4
-UNROLL = 7
+UNROLL = 6
 PROJ = 3 * TYPES
 
 F32 = jnp.float32
@@ -50,7 +50,7 @@
 
 def attend_kernel(
     edges_hbm, prior_hbm, q_hbm, g_hbm, ko_hbm, vo_hbm, kh_hbm, vh_hbm, rel_hbm, rows_hbm,
-    own_out, send_out, rel_out,
+    pack_out, send_out,
     edges, listed, prior_in, q_ref, g_ref, rel_ref, rows_ref, k_ref, v_ref, sems,
     wbd, qg, keep, prior, kvm, probs, exps, logs, grads,
     denom, delta, dprior, dkv, dwk, dwv, dq, drel, ids_ref,
@@ -78,8 +78,10 @@
             )
         )
     ]
-    for copy in copies:
-        copy.start()
+    copies[4].start()
+    for i, copy in enumerate(copies):
+        if i != 4:
+            copy.start()
 
     lane = lax.broadcasted_iota(jnp.int32, (TILE, WIDE), 1)
     first = lane < TILE
@@ -107,15 +109,9 @@
             heads[a] = heads[a] + (target == a).astype(jnp.int32)
         listed[at] = 256 + 16 * edges[1, e] + edges[2, e]
     used = starts[dests] // GROUP
-    for i, copy in enumerate(copies):
-        if i != 4:
-            copy.wait()
-
-    for r in range(RELS):
-        for w in range(2):
-            for h in range(2):
-                at = (2 * w + h) * TILE
-                wbd[r, at : at + TILE, at : at + TILE] = rel_ref[w, r, h]
+
+    copies[1].wait()
+    copies[2].wait()
     none = jnp.zeros((TILE, WIDE), BF16)
     for a in range(dests):
         q = q_ref[a * TILE : (a + 1) * TILE, :].astype(F32) * 0.125
@@ -126,6 +122,7 @@
             qg[a, h * TILE : (h + 1) * TILE, WIDE:] = none
             qg[a, (2 + h) * TILE : (3 + h) * TILE, :WIDE] = none
             qg[a, (2 + h) * TILE : (3 + h) * TILE, WIDE:] = jnp.where(mine, g, 0.0).astype(BF16)
+    copies[3].wait()
     for b in range(own_tiles):
         keep[b] = jnp.ones((TILE, WIDE), F32)
     period = lax.broadcasted_iota(jnp.int32, (16, 8, WIDE), 2) % 8
@@ -137,9 +134,18 @@
         keep[own_tiles + 2 * j + 1] = ok[TILE:]
         tiled = jnp.sum(jnp.where(period == slot, ids.reshape(16, 8, WIDE), 0.0), axis=1)
         ids_ref[16 * j : 16 * j + 16, :] = tiled
+    copies[5].wait()
     one_lane = lax.broadcasted_iota(jnp.int32, (1, WIDE), 1)
     for r in range(RELS):
         prior[r : r + 1, :] = jnp.where(one_lane < TILE, prior_in[0, r], prior_in[1, r])
+    copies[0].wait()
+    for r in range(RELS):
+        for w in range(2):
+            for h in range(2):
+                at = (2 * w + h) * TILE
+                wbd[r, at : at + TILE, at : at + TILE] = rel_ref[w, r, h]
+    for copy in copies[6:]:
+        copy.wait()
 
     def entry(i):
         code = listed[i]
@@ -219,11 +225,15 @@
     sweep(normalise)
     sweep(backward)
 
+    at_own = 2 * (dests * REL_BLOCK)
     for a in range(dests):
         grad = jnp.where(first, dq[a, :TILE, :], dq[a, TILE:, :]) * 0.125
-        own_out[a * TILE : (a + 1) * TILE, :WIDE] = grad.astype(BF16)
+        at = at_own + a * TILE
+        pack_out[at : at + TILE, :] = grad.astype(BF16)
     for b in range(own_tiles):
-        own_out[b * TILE : (b + 1) * TILE, WIDE:] = dkv[b].astype(BF16)
+        for w in range(2):
+            at = at_own + (1 + w) * own + b * TILE
+            pack_out[at : at + TILE, :] = dkv[b, :, w * WIDE : (w + 1) * WIDE].astype(BF16)
     for b in range(halo_tiles):
         back = dkv[own_tiles + b]
         block = jnp.concatenate(
@@ -250,10 +260,11 @@
     line = jnp.where(one_lane < 32, high, line - high)
     tail = jnp.where(lax.broadcasted_iota(jnp.int32, (16, WIDE), 0) == 0, line, 0.0).astype(BF16)
     for w in range(2):
-        for y in range(rel_out.shape[1]):
-            at = (w * rel_out.shape[1] + y) * REL_ROWS
-            rel_out[w, y, :REL_ROWS, :] = drel[at : at + REL_ROWS, :].astype(BF16)
-            rel_out[w, y, REL_ROWS:, :] = tail
+        for y in range(dests):
+            at = (w * dests + y) * REL_ROWS
+            to = (w * dests + y) * REL_BLOCK
+            pack_out[to : to + REL_ROWS, :] = drel[at : at + REL_ROWS, :].astype(BF16)
+            pack_out[to + REL_ROWS : to + REL_BLOCK, :] = tail
 
 
 def attend(edges, rel_prior, queries, grad_output, key_rows, value_rows, halo_keys, halo_values, rel_weight, halo_rows):
@@ -268,12 +279,11 @@
     return pl.pallas_call(
         attend_kernel,
         out_shape=(
-            jax.ShapeDtypeStruct((rows, 3 * WIDE), BF16),
+            jax.ShapeDtypeStruct((2 * dests * REL_BLOCK + 3 * rows, WIDE), BF16),
             jax.ShapeDtypeStruct((slabs, BLOCK, WIDE), BF16),
-            jax.ShapeDtypeStruct((2, 2 * RELS * TILE // (2 * REL_ROWS), REL_BLOCK, WIDE), BF16),
         ),
         in_specs=[HBM] * 10,
-        out_specs=(VMEM,) * 3,
+        out_specs=(VMEM,) * 2,
         scratch_shapes=[
             pltpu.SMEM(edges.shape, jnp.int32),
             pltpu.SMEM((places + 1,), jnp.int32),
@@ -310,9 +320,10 @@
     )(edges, rel_prior, queries, grad_output, key_rows, value_rows, halo_keys, halo_values, rel_weight, halo_rows)
 
 
-def bundle_kernel(place, own_ref, nf_ref, types_ref, rel_ref, mine_out, send_out, keep_out, rel_out):
-    rel_out[...] = rel_ref[1 - place[0]]
-    keep_out[...] = rel_ref[place[0]]
+def bundle_kernel(place, pack_ref, nf_ref, types_ref, mine_out, send_out, own_out, keep_out, rel_out):
+    half = rel_out.shape[0]
+    for out, core in ((rel_out, 1 - place[0]), (keep_out, place[0])):
+        out[...] = pack_ref[pl.ds(pl.multiple_of(core * half, half), half), :]
     rows, feats = nf_ref.shape
     turned = jnp.transpose(nf_ref[...], (1, 0)).astype(F32).reshape(feats // 16, 2, 8, rows)
     low = turned[:, 0].reshape(feats // 2, rows)
@@ -323,25 +334,30 @@
     for j in range(rows // WIDE):
         kinds = column(types_ref[j : j + 1, :].astype(F32)).astype(BF16)
         send_out[j * WIDE : (j + 1) * WIDE, rows + WIDE :] = kinds
-    send_out[:, rows : rows + WIDE] = own_ref[:, :WIDE]
-
-
-def bundle(place, own, node_feats, node_types, rel):
+    send_out[:, rows : rows + WIDE] = pack_ref[2 * half : 2 * half + rows, :]
+    for w in range(2):
+        at = 2 * half + (1 + w) * rows
+        own_out[:, w * WIDE : (w + 1) * WIDE] = pack_ref[at : at + rows, :]
+
+
+def bundle(place, pack, node_feats, node_types):
     rows, feats = node_feats.shape
+    half = (pack.shape[0] - 3 * rows) // 2
     return pl.pallas_call(
         bundle_kernel,
         out_shape=(
             jax.ShapeDtypeStruct((feats // 2, rows), BF16),
             jax.ShapeDtypeStruct((feats // 2, rows + 2 * WIDE), BF16),
-            jax.ShapeDtypeStruct(rel.shape[1:], BF16),
-            jax.ShapeDtypeStruct(rel.shape[1:], BF16),
+            jax.ShapeDtypeStruct((rows, 2 * WIDE), BF16),
+            jax.ShapeDtypeStruct((half, WIDE), BF16),
+            jax.ShapeDtypeStruct((half, WIDE), BF16),
         ),
-        in_specs=[SMEM] + [VMEM] * 4,
-        out_specs=(VMEM,) * 4,
+        in_specs=[SMEM] + [VMEM] * 3,
+        out_specs=(VMEM,) * 5,
         compiler_params=pltpu.CompilerParams(vmem_limit_bytes=LIMIT),
         cost_estimate=pl.CostEstimate(flops=10**6, bytes_accessed=2 * 10**6, transcendentals=0),
         name="bundle",
-    )(place, own, node_feats, node_types, rel)
+    )(place, pack, node_feats, node_types)
 
 
 def spread(place, products, outs):
@@ -364,7 +380,8 @@
     spread(place, products, outs)
     for d in range(len(outs)):
         block = lax.rem(place[1] + d, len(outs))
-        both = with_line(rel_ref[block].astype(F32) + rel_got_ref[block].astype(F32)).astype(BF16)
+        here = pl.ds(pl.multiple_of(block * REL_BLOCK, REL_BLOCK), REL_BLOCK)
+        both = with_line(rel_ref[here, :].astype(F32) + rel_got_ref[here, :].astype(F32)).astype(BF16)
         for k in range(REL_BLOCK // TILE):
             at = (TYPES + k) * WIDE
             outs[d][:, at : at + WIDE] = both[k * TILE : (k + 1) * TILE, :]
@@ -393,7 +410,7 @@
     row = lax.broadcasted_iota(jnp.int32, (16, WIDE), 0)
     block = lax.broadcasted_iota(jnp.int32, (16, WIDE), 1) // 8
     node = lax.broadcasted_iota(jnp.int32, (rows, WIDE), 0).astype(F32)
-    back = own_ref[:, WIDE:].astype(F32)
+    back = own_ref[...].astype(F32)
     for c in range(slabs // 16):
         grads = inc_ref[16 * c : 16 * c + 16].astype(F32)
         ids = grads[:, 16, :]
@@ -621,7 +638,7 @@
         [lax.axis_index("core"), lax.axis_index("y"), lax.axis_index("heads")]
     ).astype(jnp.int32)
     swap = [(0, 1), (1, 0)]
-    own, send, rel = attend(
+    pack, send = attend(
         edge_tiles.T,
         rel_prior.T,
         queries,
@@ -634,7 +651,7 @@
         halo_rows.reshape(-1, WIDE),
     )
     incoming = lax.all_to_all(send, ("y", "z", "core"), 0, 0, tiled=True)
-    feats_t, sent, rel, rel_theirs = bundle(place, own, node_feats, node_types.reshape(-1, WIDE), rel)
+    feats_t, sent, own, rel, rel_theirs = bundle(place, pack, node_feats, node_types.reshape(-1, WIDE))
     got = lax.ppermute(sent, "core", swap)
     rel_got = lax.ppermute(rel_theirs, "core", swap)
     pair, *q_blocks = project_queries(place, feats_t, sent, got, rel, rel_got, y_count)
@@ -642,7 +659,7 @@
     own, *q_blocks = lax.optimization_barrier((own, *q_blocks))
     kv = collect(own, incoming)
     got_kv = lax.ppermute(kv, "core", swap)
-    kv, *q_arrived = lax.optimization_barrier((kv, *q_arrived))
+    got_kv, *q_arrived = lax.optimization_barrier((got_kv, *q_arrived))
     rel_z = lax.all_to_all(relation_places(q_arrived, z_count), "z", 0, 0, tiled=True)
     arrived = shifted(project(place, pair, kv, got_kv, sent, got, y_count), "y")
     feat_blocks = features(place, sent, kv, proj_weight.reshape(PROJ, -1, WIDE))

time: 86.3 us -> 83.6 us (0.969)
  starting transfers between devices: 49.9 us -> 46.1 us
  waiting for transfers between devices: 14.1 us -> 16.7 us
    all_to_all x1, waiting for transfers between devices: 0.93 us -> 4.39 us  [per_device(): lax.all_to_all(relation_places(q_arrived, z_count), 'z', 0, 0, tiled=True)]
    all_to_all x1, starting transfers between devices: 6.85 us -> 3.43 us  [per_device(): lax.all_to_all(by_y.reshape(z_count, -1, PROJ * WIDE), 'z', 0, 0, tiled=T...]
    ppermute x1, starting transfers between devices: 1.17 us -> 2.84 us  [per_device(): rel_last = lax.ppermute(jnp.stack([rel_mine, rel_first]), 'y', last_y)]
    ppermute x1, starting transfers between devices: 1.02 us -> 0.01 us  [per_device(): rel_first = lax.ppermute(rel_mine, 'y', next_y)]
    ppermute x1, waiting for transfers between devices: 0.99 us -> 0.01 us  [per_device(): got_kv = lax.ppermute(kv, 'core', swap)]
    ppermute x1, starting transfers between devices: 1.43 us -> 0.49 us  [per_device(): got_kv = lax.ppermute(kv, 'core', swap)]
    unnamed x12 -> x8, local copies, waits for them, and re-layouts: 1.98 us -> 1.12 us
  transfers between devices with their start and end apart: 20 -> 20, of which waited for: 10 -> 8; matrix products, arithmetic and copies ran while one was open for 1% -> 1% of each run, Pallas kernels for 10% -> 10%
where the time goes in v3:
time: 83.6 us; the launch traced here: 83.1 us
  starting transfers between devices  46.1 us (55%)
  Pallas kernels  17 us (20%)
  waiting for transfers between devices  16.7 us (20%)
  other arithmetic  1.43 us (2%)
  local copies, waits for them, and re-layouts  1.12 us (1%)
    all_to_all x1, starting transfers between devices, per_device(): incoming = lax.all_to_all(send, ('y', 'z', 'core'), 0, 0, tiled=True)  16.5 us
    ppermute x6, starting transfers between devices, shifted(): lax.ppermute(blocks[d], axis, [(i, (i + d) % count) for i in range(count)])  8.93 us
    pallas_call x1, Pallas kernels, attend(): pl.pallas_call(attend_kernel, out_shape=(jax.ShapeDtypeStruct((2 * dests...  6.93 us
    all_to_all x1, starting transfers between devices, per_device(): lax.all_to_all(relation_places(q_arrived, z_count), 'z', 0, 0, tiled=True)  4.76 us
    all_to_all x1, waiting for transfers between devices, per_device(): lax.all_to_all(relation_places(q_arrived, z_count), 'z', 0, 0, tiled=True)  4.39 us
    all_to_all x1, waiting for transfers between devices, per_device(): incoming = lax.all_to_all(send, ('y', 'z', 'core'), 0, 0, tiled=True)  4.37 us
    ppermute x3, starting transfers between devices, per_device(): lax.ppermute(block, 'core', swap)  4.32 us
    all_to_all x1, starting transfers between devices, per_device(): lax.all_to_all(by_y.reshape(z_count, -1, PROJ * WIDE), 'z', 0, 0, tiled=T...  3.43 us
  transfers between devices with their start and end apart: 20, of which 8 were waited for; matrix products, arithmetic and copies ran while one was open for 1% of the time, Pallas kernels for 10%

profile of v3, /device:TPU:1, one launch (start us, length us, event | category | flops | bytes accessed | tf_op | source)
XLA Modules:
  0.0 83.1 jit_solution(3161212422159507719)
XLA Ops:
  0.7 6.9 %attend.1 = (bf16[2816,128]{1,0:T(8,128)(2,1)}, bf16[64,24,128]{2,1,0:T(8,128)(2,1)}) custom-call(s32[3,40]{1,0:T(4,128)} %bitcast.18, f32[2,15]{1,0:T(2,128)} %bitcast.20, bf16[256,128]{1,0:T(8,128)(2,1)} %q_hbm.1, bf16[256,128]{1,0:T(8,128)(2,1)} %g_hbm.1, bf16[256,128]{1,0:T(8,128)(2,1)} %ko_hbm.1, bf16[256,128]{1,0:T(8,128)(2,1)} %vo_hbm.1, ...), custom_call_target="tpu_custom_call" | custom-call | flops 3000000000 | bytes 4000000 | tf_op jit(solution)/shard_map/attend/pallas_call | solution.py:279
  7.6 16.5 %all-to-all-start = ((bf16[64,24,128]{2,1,0:T(8,128)(2,1)}), bf16[64,24,128]{2,1,0:T(8,128)(2,1)S(1)}, u32[]{:S(2)}, u32[]{:S(2)}) async-start(bf16[64,24,128]{2,1,0:T(8,128)(2,1)} %get-tuple-element.51), calls=%async_computation | async-start | bytes 786432 | tf_op jit(solution)/shard_map/all_to_all | solution.py:653
  24.2 1.1 %copy-done = bf16[2816,128]{1,0:T(8,128)(2,1)S(1)} copy-done((bf16[2816,128]{1,0:T(8,128)(2,1)S(1)}, bf16[2816,128]{1,0:T(8,128)(2,1)}, u32[]{:S(2)}) %copy-start) | copy-done | bytes 720920
  26.7 1.1 %collective-permute-done.1.rel_got_ref = bf16[1024,128]{1,0:T(8,128)(2,1)S(1)} collective-permute-done((bf16[1024,128]{1,0:T(8,128)(2,1)S(1)}, bf16[1024,128]{1,0:T(8,128)(2,1)S(1)}, u32[]{:S(2)}, u32[]{:S(2)}) %collective-permute-start.1) | collective-permute-done | bytes 262176 | tf_op jit(solution)/shard_map/ppermute | solution.py:656
  28.1 1.2 %project_queries.1 = (bf16[256,512]{1,0:T(8,128)(2,1)S(1)}, bf16[64,1152]{1,0:T(8,128)(2,1)S(1)}, bf16[64,1152]{1,0:T(8,128)(2,1)S(1)}, bf16[64,1152]{1,0:T(8,128)(2,1)S(1)}, bf16[64,1152]{1,0:T(8,128)(2,1)S(1)}) custom-call(s32[3]{0:T(128)S(1)} %pad_add_fusion.place, bf16[256,256]{1,0:T(8,128)(2,1)S(1)} %get-tuple-element.42.mine_ref, ...), custom_call_target="tpu_custom_call" | custom-call | flops 1000000000 | bytes 2000000 | tf_op jit(solution)/shard_map/project_queries/pallas_call | solution.py:394
  29.3 1.4 %collective-permute-start.3 = (bf16[64,1152]{1,0:T(8,128)(2,1)S(1)}, bf16[64,1152]{1,0:T(8,128)(2,1)S(1)}, u32[]{:S(2)}, u32[]{:S(2)}) collective-permute-start(bf16[64,1152]{1,0:T(8,128)(2,1)S(1)} %get-tuple-element.47), channel_id=1, source_target_pairs={{0,64},{64,128},{128,192},{192,0},{1,65},{65,129},{129,193},{193,1... | collective-permute-start | bytes 442376 | tf_op jit(solution)/shard_map/ppermute | solution.py:615
  30.7 2.6 %collective-permute-start.4 = (bf16[64,1152]{1,0:T(8,128)(2,1)S(1)}, bf16[64,1152]{1,0:T(8,128)(2,1)S(1)}, u32[]{:S(2)}, u32[]{:S(2)}) collective-permute-start(bf16[64,1152]{1,0:T(8,128)(2,1)S(1)} %get-tuple-element.48), channel_id=1, source_target_pairs={{0,128},{64,192},{128,0},{192,64},{1,129},{65,193},{129,1},{193,65... | collective-permute-start | bytes 442376 | tf_op jit(solution)/shard_map/ppermute | solution.py:615
  33.3 1.1 %collective-permute-start.5 = (bf16[64,1152]{1,0:T(8,128)(2,1)S(1)}, bf16[64,1152]{1,0:T(8,128)(2,1)S(1)}, u32[]{:S(2)}, u32[]{:S(2)}) collective-permute-start(bf16[64,1152]{1,0:T(8,128)(2,1)S(1)} %get-tuple-element.49), channel_id=1, source_target_pairs={{0,192},{64,0},{128,64},{192,128},{1,193},{65,1},{129,65},{193,129... | collective-permute-start | bytes 442376 | tf_op jit(solution)/shard_map/ppermute | solution.py:615
  34.4 4.4 %all-to-all-done.inc_ref = bf16[64,24,128]{2,1,0:T(8,128)(2,1)S(1)} async-done(((bf16[64,24,128]{2,1,0:T(8,128)(2,1)}), bf16[64,24,128]{2,1,0:T(8,128)(2,1)S(1)}, u32[]{:S(2)}, u32[]{:S(2)}) %all-to-all-start) | async-done | bytes 393248 | tf_op jit(solution)/shard_map/all_to_all | solution.py:653
  39.6 3.0 %collective-permute-done.4.refs_2_ = bf16[64,1152]{1,0:T(8,128)(2,1)S(1)} collective-permute-done((bf16[64,1152]{1,0:T(8,128)(2,1)S(1)}, bf16[64,1152]{1,0:T(8,128)(2,1)S(1)}, u32[]{:S(2)}, u32[]{:S(2)}) %collective-permute-start.4) | collective-permute-done | bytes 147488 | tf_op jit(solution)/shard_map/ppermute | solution.py:615
  43.5 4.8 %all-to-all-start.1 = ((bf16[8,256,128]{2,1,0:T(8,128)(2,1)}), bf16[8,256,128]{2,1,0:T(8,128)(2,1)S(1)}, u32[]{:S(2)}, u32[]{:S(2)}) async-start(bf16[8,256,128]{2,1,0:T(8,128)(2,1)} %relation_places.1), calls=%async_computation.1 | async-start | bytes 1048576 | tf_op jit(solution)/shard_map/all_to_all | solution.py:663
  48.3 1.5 %project.1 = (bf16[64,1280]{1,0:T(8,128)(2,1)S(1)}, bf16[64,1280]{1,0:T(8,128)(2,1)S(1)}, bf16[64,1280]{1,0:T(8,128)(2,1)S(1)}, bf16[64,1280]{1,0:T(8,128)(2,1)S(1)}) custom-call(s32[3]{0:T(128)S(1)} %pad_add_fusion.place, bf16[256,512]{1,0:T(8,128)(2,1)S(1)} %get-tuple-element.56.pair_ref, bf16[256,256]{1,0:T(8,128)(2,1)S(1)} %collect.1.kv_ref, ...), custom_call_target="tpu_custom_call" | custom-call | flops 1000000000 | bytes 4000000 | tf_op jit(solution)/shard_map/project/pallas_call | solution.py:509
  50.5 2.6 %collective-permute-start.9 = (bf16[64,1280]{1,0:T(8,128)(2,1)S(1)}, bf16[64,1280]{1,0:T(8,128)(2,1)S(1)}, u32[]{:S(2)}, u32[]{:S(2)}) collective-permute-start(bf16[64,1280]{1,0:T(8,128)(2,1)S(1)} %get-tuple-element.63), channel_id=1, source_target_pairs={{0,128},{64,192},{128,0},{192,64},{1,129},{65,193},{129,1},{193,65... | collective-permute-start | bytes 491528 | tf_op jit(solution)/shard_map/ppermute | solution.py:615
  53.6 1.7 %features.1 = (bf16[256,128]{1,0:T(8,128)(2,1)S(1)}, bf16[256,128]{1,0:T(8,128)(2,1)S(1)}, bf16[256,128]{1,0:T(8,128)(2,1)S(1)}, bf16[256,128]{1,0:T(8,128)(2,1)S(1)}) custom-call(s32[3]{0:T(128)S(1)} %pad_add_fusion.place, bf16[256,512]{1,0:T(8,128)(2,1)S(1)} %get-tuple-element.43.sent_ref, bf16[256,256]{1,0:T(8,128)(2,1)S(1)} %collect.1.kv_ref, ...), custom_call_target="tpu_custom_call" | custom-call | flops 1000000000 | bytes 3000000 | tf_op jit(solution)/shard_map/features/pallas_call | solution.py:544
  55.4 1.3 %collective-permute-start.6 = (bf16[256,128]{1,0:T(8,128)(2,1)S(1)}, bf16[256,128]{1,0:T(8,128)(2,1)S(1)}, u32[]{:S(2)}, u32[]{:S(2)}) collective-permute-start(bf16[256,128]{1,0:T(8,128)(2,1)S(1)} %get-tuple-element.59), channel_id=1, source_target_pairs={{0,1},{1,0},{2,3},{3,2},{4,5},{5,4},{6,7},{7,6},{8,9},{9,8},{10,11... | collective-permute-start | bytes 196616 | tf_op jit(solution)/shard_map/ppermute | solution.py:667
  56.9 1.9 %collective-permute-done.6 = bf16[256,128]{1,0:T(8,128)(2,1)S(1)} collective-permute-done((bf16[256,128]{1,0:T(8,128)(2,1)S(1)}, bf16[256,128]{1,0:T(8,128)(2,1)S(1)}, u32[]{:S(2)}, u32[]{:S(2)}) %collective-permute-start.6) | collective-permute-done | bytes 65568 | tf_op jit(solution)/shard_map/ppermute | solution.py:667
  58.9 1.2 %collective-permute-done.7 = bf16[256,128]{1,0:T(8,128)(2,1)S(1)} collective-permute-done((bf16[256,128]{1,0:T(8,128)(2,1)S(1)}, bf16[256,128]{1,0:T(8,128)(2,1)S(1)}, u32[]{:S(2)}, u32[]{:S(2)}) %collective-permute-start.7) | collective-permute-done | bytes 65568 | tf_op jit(solution)/shard_map/ppermute | solution.py:667
  60.9 4.4 %all-to-all-done.1.inc_ref = bf16[8,256,128]{2,1,0:T(8,128)(2,1)S(1)} async-done(((bf16[8,256,128]{2,1,0:T(8,128)(2,1)}), bf16[8,256,128]{2,1,0:T(8,128)(2,1)S(1)}, u32[]{:S(2)}, u32[]{:S(2)}) %all-to-all-start.1) | async-done | bytes 524320 | tf_op jit(solution)/shard_map/all_to_all | solution.py:663
  66.0 3.4 %all-to-all-start.2 = ((bf16[8,8,1920]{2,1,0:T(8,128)(2,1)}), bf16[8,8,1920]{2,1,0:T(8,128)(2,1)S(1)}, u32[]{:S(2)}, u32[]{:S(2)}) async-start(bf16[8,8,1920]{2,1,0:T(8,128)(2,1)} %bitcast.8), calls=%async_computation.2 | async-start | bytes 491520 | tf_op jit(solution)/shard_map/all_to_all | solution.py:676
  69.5 2.8 %collective-permute-start.12 = (bf16[2,256,128]{2,1,0:T(8,128)(2,1)S(1)}, bf16[2,256,128]{2,1,0:T(8,128)(2,1)S(1)}, u32[]{:S(2)}, u32[]{:S(2)}) collective-permute-start(bf16[2,256,128]{2,1,0:T(8,128)(2,1)S(1)} %pad_maximum_fusion), channel_id=1, source_target_pairs={{0,192},{192,0},{64,128},{128,64},{1,193},{193,1},{65,129},{129,65... | collective-permute-start | bytes 393224 | tf_op jit(solution)/shard_map/ppermute | solution.py:679
  72.3 2.6 %collective-permute-start.16 = (bf16[256,128]{1,0:T(8,128)(2,1)S(1)}, bf16[256,128]{1,0:T(8,128)(2,1)S(1)}, u32[]{:S(2)}, u32[]{:S(2)}) collective-permute-start(bf16[256,128]{1,0:T(8,128)(2,1)S(1)} %add_convert_fusion.1), channel_id=1, source_target_pairs={{0,3},{3,0},{1,2},{2,1},{4,7},{7,4},{5,6},{6,5},{8,11},{11,8},{9,1... | collective-permute-start | bytes 196616 | tf_op jit(solution)/shard_map/ppermute | solution.py:670
  74.9 1.9 %collective-permute-start.13 = (bf16[256,128]{1,0:T(8,128)(2,1)S(1)}, bf16[256,128]{1,0:T(8,128)(2,1)S(1)}, u32[]{:S(2)}, u32[]{:S(2)}) collective-permute-start(bf16[256,128]{1,0:T(8,128)(2,1)S(1)} %get-tuple-element.67.mine_ref), channel_id=1, source_target_pairs={{0,4},{4,0},{1,5},{5,1},{2,6},{6,2},{3,7},{7,3},{8,12},{12,8},{9,1... | collective-permute-start | bytes 196616 | tf_op jit(solution)/shard_map/ppermute | solution.py:681
  76.8 2.4 %collective-permute-start.15 = (bf16[2,256,128]{2,1,0:T(8,128)(2,1)S(1)}, bf16[2,256,128]{2,1,0:T(8,128)(2,1)S(1)}, u32[]{:S(2)}, u32[]{:S(2)}) collective-permute-start(bf16[2,256,128]{2,1,0:T(8,128)(2,1)S(1)} %collective-permute-done.12.last_ref), channel_id=1, source_target_pairs={{0,4},{4,0},{1,5},{5,1},{2,6},{6,2},{3,7},{7,3},{8,12},{12,8},{9,1... | collective-permute-start | bytes 393224 | tf_op jit(solution)/shard_map/ppermute | solution.py:681
  80.2 2.2 %relations.1 = f32[2,15,2,64,64]{4,3,2,1,0:T(8,128)} custom-call(s32[3]{0:T(128)S(1)} %pad_add_fusion.place, bf16[256,128]{1,0:T(8,128)(2,1)S(1)} %get-tuple-element.67.mine_ref, bf16[256,128]{1,0:T(8,128)(2,1)S(1)} %collective-permute-done.11.first_ref, bf16[2,256,128]{2,1,0:T(8,128)(2,1)S(1)} %collective-permute-done.12.last_ref, ...), custom_call_target="tpu_custom_call" | custom-call | flops 1000000 | bytes 3000000 | tf_op jit(solution)/shard_map/relations/pallas_call | solution.py:575
  (39 shorter events, 8.4 us)
Async XLA Ops:
  0.6 23.6 %copy-start.1 = (bf16[256,512]{1,0:T(8,128)(2,1)S(1)}, bf16[256,512]{1,0:T(8,128)(2,1)}, u32[]{:S(2)}) copy-start(bf16[256,512]{1,0:T(8,128)(2,1)} %nf_ref.1) | copy-start | bytes 786436
  0.6 23.6 %copy-start.2 = (s32[256]{0:T(256)S(1)}, s32[256]{0:T(256)}, u32[]{:S(2)}) copy-start(s32[256]{0:T(256)} %param.14) | copy-start | bytes 3076
  7.6 31.2 %all-to-all-start = ((bf16[64,24,128]{2,1,0:T(8,128)(2,1)}), bf16[64,24,128]{2,1,0:T(8,128)(2,1)S(1)}, u32[]{:S(2)}, u32[]{:S(2)}) async-start(bf16[64,24,128]{2,1,0:T(8,128)(2,1)} %get-tuple-element.51), calls=%async_computation | async-start | bytes 786432 | tf_op jit(solution)/shard_map/all_to_all | solution.py:653
  24.2 1.1 %copy-start = (bf16[2816,128]{1,0:T(8,128)(2,1)S(1)}, bf16[2816,128]{1,0:T(8,128)(2,1)}, u32[]{:S(2)}) copy-start(bf16[2816,128]{1,0:T(8,128)(2,1)} %get-tuple-element.40.pack_ref) | copy-start | bytes 2162692
  26.1 1.7 %collective-permute-start.1 = (bf16[1024,128]{1,0:T(8,128)(2,1)S(1)}, bf16[1024,128]{1,0:T(8,128)(2,1)S(1)}, u32[]{:S(2)}, u32[]{:S(2)}) collective-permute-start(bf16[1024,128]{1,0:T(8,128)(2,1)S(1)} %get-tuple-element.45), channel_id=1, source_target_pairs={{0,4},{4,0},{1,5},{5,1},{2,6},{6,2},{3,7},{7,3},{8,12},{12,8},{9,1... | collective-permute-start | bytes 786440 | tf_op jit(solution)/shard_map/ppermute | solution.py:656
  26.6 1.5 %collective-permute-start = (bf16[256,512]{1,0:T(8,128)(2,1)S(1)}, bf16[256,512]{1,0:T(8,128)(2,1)S(1)}, u32[]{:S(2)}, u32[]{:S(2)}) collective-permute-start(bf16[256,512]{1,0:T(8,128)(2,1)S(1)} %get-tuple-element.43.sent_ref), channel_id=1, source_target_pairs={{0,4},{4,0},{1,5},{5,1},{2,6},{6,2},{3,7},{7,3},{8,12},{12,8},{9,1... | collective-permute-start | bytes 786440 | tf_op jit(solution)/shard_map/ppermute | solution.py:655
  29.3 10.2 %collective-permute-start.3 = (bf16[64,1152]{1,0:T(8,128)(2,1)S(1)}, bf16[64,1152]{1,0:T(8,128)(2,1)S(1)}, u32[]{:S(2)}, u32[]{:S(2)}) collective-permute-start(bf16[64,1152]{1,0:T(8,128)(2,1)S(1)} %get-tuple-element.47), channel_id=1, source_target_pairs={{0,64},{64,128},{128,192},{192,0},{1,65},{65,129},{129,193},{193,1... | collective-permute-start | bytes 442376 | tf_op jit(solution)/shard_map/ppermute | solution.py:615
  30.7 11.8 %collective-permute-start.4 = (bf16[64,1152]{1,0:T(8,128)(2,1)S(1)}, bf16[64,1152]{1,0:T(8,128)(2,1)S(1)}, u32[]{:S(2)}, u32[]{:S(2)}) collective-permute-start(bf16[64,1152]{1,0:T(8,128)(2,1)S(1)} %get-tuple-element.48), channel_id=1, source_target_pairs={{0,128},{64,192},{128,0},{192,64},{1,129},{65,193},{129,1},{193,65... | collective-permute-start | bytes 442376 | tf_op jit(solution)/shard_map/ppermute | solution.py:615
  33.3 9.2 %collective-permute-start.5 = (bf16[64,1152]{1,0:T(8,128)(2,1)S(1)}, bf16[64,1152]{1,0:T(8,128)(2,1)S(1)}, u32[]{:S(2)}, u32[]{:S(2)}) collective-permute-start(bf16[64,1152]{1,0:T(8,128)(2,1)S(1)} %get-tuple-element.49), channel_id=1, source_target_pairs={{0,192},{64,0},{128,64},{192,128},{1,193},{65,1},{129,65},{193,129... | collective-permute-start | bytes 442376 | tf_op jit(solution)/shard_map/ppermute | solution.py:615
  39.1 3.5 %collective-permute-start.2 = (bf16[256,256]{1,0:T(8,128)(2,1)S(1)}, bf16[256,256]{1,0:T(8,128)(2,1)S(1)}, u32[]{:S(2)}, u32[]{:S(2)}) collective-permute-start(bf16[256,256]{1,0:T(8,128)(2,1)S(1)} %collect.1.kv_ref), channel_id=1, source_target_pairs={{0,4},{4,0},{1,5},{5,1},{2,6},{6,2},{3,7},{7,3},{8,12},{12,8},{9,1... | collective-permute-start | bytes 393224 | tf_op jit(solution)/shard_map/ppermute | solution.py:661
  43.5 21.8 %all-to-all-start.1 = ((bf16[8,256,128]{2,1,0:T(8,128)(2,1)}), bf16[8,256,128]{2,1,0:T(8,128)(2,1)S(1)}, u32[]{:S(2)}, u32[]{:S(2)}) async-start(bf16[8,256,128]{2,1,0:T(8,128)(2,1)} %relation_places.1), calls=%async_computation.1 | async-start | bytes 1048576 | tf_op jit(solution)/shard_map/all_to_all | solution.py:663
  48.3 5.4 %copy-start.3 = (bf16[3,5,512,128]{3,2,1,0:T(8,128)(2,1)S(1)}, bf16[3,5,512,128]{3,2,1,0:T(8,128)(2,1)}, u32[]{:S(2)}) copy-start(bf16[3,5,512,128]{3,2,1,0:T(8,128)(2,1)} %param.23) | copy-start | bytes 5898244
  49.7 10.3 %collective-permute-start.8 = (bf16[64,1280]{1,0:T(8,128)(2,1)S(1)}, bf16[64,1280]{1,0:T(8,128)(2,1)S(1)}, u32[]{:S(2)}, u32[]{:S(2)}) collective-permute-start(bf16[64,1280]{1,0:T(8,128)(2,1)S(1)} %get-tuple-element.62), channel_id=1, source_target_pairs={{0,64},{64,128},{128,192},{192,0},{1,65},{65,129},{129,193},{193,1... | collective-permute-start | bytes 491528 | tf_op jit(solution)/shard_map/ppermute | solution.py:615
  50.5 9.6 %collective-permute-start.9 = (bf16[64,1280]{1,0:T(8,128)(2,1)S(1)}, bf16[64,1280]{1,0:T(8,128)(2,1)S(1)}, u32[]{:S(2)}, u32[]{:S(2)}) collective-permute-start(bf16[64,1280]{1,0:T(8,128)(2,1)S(1)} %get-tuple-element.63), channel_id=1, source_target_pairs={{0,128},{64,192},{128,0},{192,64},{1,129},{65,193},{129,1},{193,65... | collective-permute-start | bytes 491528 | tf_op jit(solution)/shard_map/ppermute | solution.py:615
  53.0 7.0 %collective-permute-start.10 = (bf16[64,1280]{1,0:T(8,128)(2,1)S(1)}, bf16[64,1280]{1,0:T(8,128)(2,1)S(1)}, u32[]{:S(2)}, u32[]{:S(2)}) collective-permute-start(bf16[64,1280]{1,0:T(8,128)(2,1)S(1)} %get-tuple-element.64), channel_id=1, source_target_pairs={{0,192},{64,0},{128,64},{192,128},{1,193},{65,1},{129,65},{193,129... | collective-permute-start | bytes 491528 | tf_op jit(solution)/shard_map/ppermute | solution.py:615
  55.4 3.5 %collective-permute-start.6 = (bf16[256,128]{1,0:T(8,128)(2,1)S(1)}, bf16[256,128]{1,0:T(8,128)(2,1)S(1)}, u32[]{:S(2)}, u32[]{:S(2)}) collective-permute-start(bf16[256,128]{1,0:T(8,128)(2,1)S(1)} %get-tuple-element.59), channel_id=1, source_target_pairs={{0,1},{1,0},{2,3},{3,2},{4,5},{5,4},{6,7},{7,6},{8,9},{9,8},{10,11... | collective-permute-start | bytes 196616 | tf_op jit(solution)/shard_map/ppermute | solution.py:667
  56.7 3.4 %collective-permute-start.7 = (bf16[256,128]{1,0:T(8,128)(2,1)S(1)}, bf16[256,128]{1,0:T(8,128)(2,1)S(1)}, u32[]{:S(2)}, u32[]{:S(2)}) collective-permute-start(bf16[256,128]{1,0:T(8,128)(2,1)S(1)} %get-tuple-element.60), channel_id=1, source_target_pairs={{0,1},{1,0},{2,3},{3,2},{4,5},{5,4},{6,7},{7,6},{8,9},{9,8},{10,11... | collective-permute-start | bytes 196616 | tf_op jit(solution)/shard_map/ppermute | solution.py:667
  66.0 3.4 %collective-permute-start.11 = (bf16[256,128]{1,0:T(8,128)(2,1)S(1)}, bf16[256,128]{1,0:T(8,128)(2,1)S(1)}, u32[]{:S(2)}, u32[]{:S(2)}) collective-permute-start(bf16[256,128]{1,0:T(8,128)(2,1)S(1)} %get-tuple-element.67.mine_ref), channel_id=1, source_target_pairs={{0,64},{64,0},{128,192},{192,128},{1,65},{65,1},{129,193},{193,129... | collective-permute-start | bytes 196616 | tf_op jit(solution)/shard_map/ppermute | solution.py:678
  66.0 16.4 %all-to-all-start.2 = ((bf16[8,8,1920]{2,1,0:T(8,128)(2,1)}), bf16[8,8,1920]{2,1,0:T(8,128)(2,1)S(1)}, u32[]{:S(2)}, u32[]{:S(2)}) async-start(bf16[8,8,1920]{2,1,0:T(8,128)(2,1)} %bitcast.8), calls=%async_computation.2 | async-start | bytes 491520 | tf_op jit(solution)/shard_map/all_to_all | solution.py:676
  69.5 7.3 %collective-permute-start.12 = (bf16[2,256,128]{2,1,0:T(8,128)(2,1)S(1)}, bf16[2,256,128]{2,1,0:T(8,128)(2,1)S(1)}, u32[]{:S(2)}, u32[]{:S(2)}) collective-permute-start(bf16[2,256,128]{2,1,0:T(8,128)(2,1)S(1)} %pad_maximum_fusion), channel_id=1, source_target_pairs={{0,192},{192,0},{64,128},{128,64},{1,193},{193,1},{65,129},{129,65... | collective-permute-start | bytes 393224 | tf_op jit(solution)/shard_map/ppermute | solution.py:679
  72.3 6.9 %collective-permute-start.16 = (bf16[256,128]{1,0:T(8,128)(2,1)S(1)}, bf16[256,128]{1,0:T(8,128)(2,1)S(1)}, u32[]{:S(2)}, u32[]{:S(2)}) collective-permute-start(bf16[256,128]{1,0:T(8,128)(2,1)S(1)} %add_convert_fusion.1), channel_id=1, source_target_pairs={{0,3},{3,0},{1,2},{2,1},{4,7},{7,4},{5,6},{6,5},{8,11},{11,8},{9,1... | collective-permute-start | bytes 196616 | tf_op jit(solution)/shard_map/ppermute | solution.py:670
  74.9 5.0 %collective-permute-start.13 = (bf16[256,128]{1,0:T(8,128)(2,1)S(1)}, bf16[256,128]{1,0:T(8,128)(2,1)S(1)}, u32[]{:S(2)}, u32[]{:S(2)}) collective-permute-start(bf16[256,128]{1,0:T(8,128)(2,1)S(1)} %get-tuple-element.67.mine_ref), channel_id=1, source_target_pairs={{0,4},{4,0},{1,5},{5,1},{2,6},{6,2},{3,7},{7,3},{8,12},{12,8},{9,1... | collective-permute-start | bytes 196616 | tf_op jit(solution)/shard_map/ppermute | solution.py:681
  76.8 3.1 %collective-permute-start.14 = (bf16[256,128]{1,0:T(8,128)(2,1)S(1)}, bf16[256,128]{1,0:T(8,128)(2,1)S(1)}, u32[]{:S(2)}, u32[]{:S(2)}) collective-permute-start(bf16[256,128]{1,0:T(8,128)(2,1)S(1)} %collective-permute-done.11.first_ref), channel_id=1, source_target_pairs={{0,4},{4,0},{1,5},{5,1},{2,6},{6,2},{3,7},{7,3},{8,12},{12,8},{9,1... | collective-permute-start | bytes 196616 | tf_op jit(solution)/shard_map/ppermute | solution.py:681
  76.8 3.4 %collective-permute-start.15 = (bf16[2,256,128]{2,1,0:T(8,128)(2,1)S(1)}, bf16[2,256,128]{2,1,0:T(8,128)(2,1)S(1)}, u32[]{:S(2)}, u32[]{:S(2)}) collective-permute-start(bf16[2,256,128]{2,1,0:T(8,128)(2,1)S(1)} %collective-permute-done.12.last_ref), channel_id=1, source_target_pairs={{0,4},{4,0},{1,5},{5,1},{2,6},{6,2},{3,7},{7,3},{8,12},{12,8},{9,1... | collective-permute-start | bytes 393224 | tf_op jit(solution)/shard_map/ppermute | solution.py:681

commit v4 on v3

--- a/solution.py
+++ b/solution.py
@@ -11,6 +11,7 @@
 WIDE = 128
 GROUP = 4
 UNROLL = 6
+EARLY = 4
 PROJ = 3 * TYPES
 
 F32 = jnp.float32
@@ -374,7 +375,7 @@
     pair_out[:, rows:] = got_ref[:, :rows]
     query = jnp.concatenate([ref[:, rows : rows + WIDE] for ref in (sent_ref, got_ref)], axis=0).astype(F32)
     kinds = jnp.concatenate([ref[:, rows + WIDE :] for ref in (sent_ref, got_ref)], axis=0).astype(F32)
-    for t in range(TYPES):
+    for t in range(EARLY):
         masked = jnp.where(kinds == float(t), query, 0.0).astype(BF16)
         products[:, t * WIDE : (t + 1) * WIDE] = mul(pair_out[...], masked, NN).astype(BF16)
     spread(place, products, outs)
@@ -383,13 +384,13 @@
         here = pl.ds(pl.multiple_of(block * REL_BLOCK, REL_BLOCK), REL_BLOCK)
         both = with_line(rel_ref[here, :].astype(F32) + rel_got_ref[here, :].astype(F32)).astype(BF16)
         for k in range(REL_BLOCK // TILE):
-            at = (TYPES + k) * WIDE
+            at = (EARLY + k) * WIDE
             outs[d][:, at : at + WIDE] = both[k * TILE : (k + 1) * TILE, :]
 
 
 def project_queries(place, mine, sent, got, rel, rel_got, count):
     feats, rows = mine.shape
-    wide = TYPES * WIDE
+    wide = EARLY * WIDE
     more = REL_BLOCK // TILE * WIDE
     return pl.pallas_call(
         project_queries_kernel,
@@ -440,7 +441,7 @@
     out = refs[-1]
     parts = []
     for k in range(REL_BLOCK // TILE):
-        at = (TYPES + k) * WIDE
+        at = (EARLY + k) * WIDE
         total = refs[0][:, at : at + WIDE].astype(F32)
         for ref in refs[1:-1]:
             total = total + ref[:, at : at + WIDE].astype(F32)
@@ -492,12 +493,12 @@
     outs, products = refs[:-1], refs[-1]
     rows = kv_ref.shape[0]
     kinds = jnp.concatenate([ref[:, rows + WIDE :] for ref in (sent_ref, got_ref)], axis=0).astype(F32)
-    for p in range(2):
-        part = jnp.concatenate(
-            [ref[:, p * WIDE : (p + 1) * WIDE] for ref in (kv_ref, got_kv_ref)], axis=0
-        ).astype(F32)
-        for t in range(TYPES):
-            at = (p * TYPES + t) * WIDE
+    for p in range(3):
+        pair = (sent_ref, got_ref) if p == 0 else (kv_ref, got_kv_ref)
+        column_at = rows if p == 0 else (p - 1) * WIDE
+        part = jnp.concatenate([ref[:, column_at : column_at + WIDE] for ref in pair], axis=0).astype(F32)
+        for t in range(EARLY if p == 0 else 0, TYPES):
+            at = (p * TYPES + t - EARLY) * WIDE
             masked = jnp.where(kinds == float(t), part, 0.0).astype(BF16)
             products[:, at : at + WIDE] = mul(pair_ref[...], masked, NN).astype(BF16)
     spread(place, products, outs)
@@ -505,7 +506,7 @@
 
 def project(place, pair, kv, got_kv, sent, got, count):
     feats = pair.shape[0]
-    wide = 2 * TYPES * WIDE
+    wide = (PROJ - EARLY) * WIDE
     return pl.pallas_call(
         project_kernel,
         out_shape=(jax.ShapeDtypeStruct((feats // count, wide), BF16),) * count,
@@ -553,17 +554,14 @@
     )(place, sent, kv, weights)
 
 
-def relation_kernel(place, mine_ref, first_ref, last_ref, c_mine_ref, c_first_ref, c_last_ref, out_ref, flat):
+def relation_kernel(place, near_ref, far_ref, c_near_ref, c_far_ref, out_ref, flat):
     y = place[1]
-    last = 3 - y
-    owners = (y, y + 1 - 2 * lax.rem(y, 2), last, last + 1 - 2 * lax.rem(last, 2))
-    for core, refs in (
-        (place[0], (mine_ref, first_ref, last_ref.at[0], last_ref.at[1])),
-        (1 - place[0], (c_mine_ref, c_first_ref, c_last_ref.at[0], c_last_ref.at[1])),
-    ):
-        for owner, ref in zip(owners, refs):
+    far = 3 - y
+    owners = (y, y + 1 - 2 * lax.rem(y, 2), far, far + 1 - 2 * lax.rem(far, 2))
+    for core, refs in ((place[0], (near_ref, far_ref)), (1 - place[0], (c_near_ref, c_far_ref))):
+        for n, owner in enumerate(owners):
             at = pl.multiple_of((core * len(owners) + owner) * REL_ROWS, 16)
-            flat[pl.ds(at, REL_ROWS), :] = ref[:REL_ROWS, :].astype(F32)
+            flat[pl.ds(at, REL_ROWS), :] = refs[n // 2][n % 2, :REL_ROWS, :].astype(F32)
     for w in range(2):
         for r in range(RELS):
             at = (w * RELS + r) * TILE
@@ -575,7 +573,7 @@
     return pl.pallas_call(
         relation_kernel,
         out_shape=jax.ShapeDtypeStruct((2, RELS, 2, TILE, TILE), F32),
-        in_specs=[SMEM] + [VMEM] * 6,
+        in_specs=[SMEM] + [VMEM] * 4,
         out_specs=VMEM,
         scratch_shapes=[pltpu.VMEM((2 * RELS * TILE, WIDE), F32)],
         compiler_params=pltpu.CompilerParams(vmem_limit_bytes=LIMIT),
@@ -587,7 +585,7 @@
 def place_sum_kernel(*refs):
     out = refs[-1]
     half = (len(refs) - 1) // 2
-    narrow = TYPES * WIDE
+    narrow = EARLY * WIDE
     for at, group in ((0, refs[:half]), (narrow, refs[half:-1])):
         width = narrow if at == 0 else group[0].shape[1]
         total = group[0][:, :width].astype(F32)
@@ -676,8 +674,9 @@
     by_z = lax.all_to_all(by_y.reshape(z_count, -1, PROJ * WIDE), "z", 0, 0, tiled=True)
     rel_mine, prior = relation_sum(rel_z)
     rel_first = lax.ppermute(rel_mine, "y", next_y)
-    rel_last = lax.ppermute(jnp.stack([rel_mine, rel_first]), "y", last_y)
-    blocks = (rel_mine, rel_first, rel_last)
+    rel_near = jnp.stack([rel_mine, rel_first])
+    rel_far = lax.ppermute(rel_near, "y", last_y)
+    blocks = (rel_near, rel_far)
     grad_rel = relations(place, *blocks, *(lax.ppermute(block, "core", swap) for block in blocks))
     by_z, grad_rel, grad_feats = lax.optimization_barrier((by_z, grad_rel, grad_feats))
     grad_proj = jnp.sum(by_z.astype(F32), axis=0).reshape(-1, 3, TYPES, WIDE)

time: 83.6 us -> 82.9 us (level)
    ppermute x1, starting transfers between devices: 2.84 us -> 1.5 us  [per_device(): rel_far = lax.ppermute(rel_near, 'y', last_y)]
    all_to_all x1, starting transfers between devices: 3.43 us -> 4.36 us  [per_device(): lax.all_to_all(by_y.reshape(z_count, -1, PROJ * WIDE), 'z', 0, 0, tiled=T...]
    ppermute x3 -> x2, starting transfers between devices: 4.32 us -> 4.69 us  [per_device(): lax.ppermute(block, 'core', swap)]
  transfers between devices with their start and end apart: 20 -> 19, of which waited for: 8 -> 9; matrix products, arithmetic and copies ran while one was open for 1% -> 1% of each run, Pallas kernels for 10% -> 10%
where the time goes in v4:
time: 82.9 us; the launch traced here: 82.4 us
  starting transfers between devices  46 us (55%)
  Pallas kernels  17.1 us (21%)
  waiting for transfers between devices  16 us (19%)
  other arithmetic  1.43 us (2%)
  local copies, waits for them, and re-layouts  1.12 us (1%)
    all_to_all x1, starting transfers between devices, per_device(): incoming = lax.all_to_all(send, ('y', 'z', 'core'), 0, 0, tiled=True)  16.5 us
    ppermute x6, starting transfers between devices, shifted(): lax.ppermute(blocks[d], axis, [(i, (i + d) % count) for i in range(count)])  8.91 us
    pallas_call x1, Pallas kernels, attend(): pl.pallas_call(attend_kernel, out_shape=(jax.ShapeDtypeStruct((2 * dests...  6.94 us
    all_to_all x1, starting transfers between devices, per_device(): lax.all_to_all(relation_places(q_arrived, z_count), 'z', 0, 0, tiled=True)  4.74 us
    ppermute x2, starting transfers between devices, per_device(): lax.ppermute(block, 'core', swap)  4.69 us
    all_to_all x1, waiting for transfers between devices, per_device(): incoming = lax.all_to_all(send, ('y', 'z', 'core'), 0, 0, tiled=True)  4.46 us
    all_to_all x1, starting transfers between devices, per_device(): lax.all_to_all(by_y.reshape(z_count, -1, PROJ * WIDE), 'z', 0, 0, tiled=T...  4.36 us
    all_to_all x1, waiting for transfers between devices, per_device(): lax.all_to_all(relation_places(q_arrived, z_count), 'z', 0, 0, tiled=True)  4.06 us
  transfers between devices with their start and end apart: 19, of which 9 were waited for; matrix products, arithmetic and copies ran while one was open for 1% of the time, Pallas kernels for 10%

profile of v4, /device:TPU:1, one launch (start us, length us, event | category | flops | bytes accessed | tf_op | source)
XLA Modules:
  0.0 82.4 jit_solution(217330069674167777)
XLA Ops:
  0.7 6.9 %attend.1 = (bf16[2816,128]{1,0:T(8,128)(2,1)}, bf16[64,24,128]{2,1,0:T(8,128)(2,1)}) custom-call(s32[3,40]{1,0:T(4,128)} %bitcast.18, f32[2,15]{1,0:T(2,128)} %bitcast.20, bf16[256,128]{1,0:T(8,128)(2,1)} %q_hbm.1, bf16[256,128]{1,0:T(8,128)(2,1)} %g_hbm.1, bf16[256,128]{1,0:T(8,128)(2,1)} %ko_hbm.1, bf16[256,128]{1,0:T(8,128)(2,1)} %vo_hbm.1, ...), custom_call_target="tpu_custom_call" | custom-call | flops 3000000000 | bytes 4000000 | tf_op jit(solution)/shard_map/attend/pallas_call | solution.py:280
  7.6 16.5 %all-to-all-start = ((bf16[64,24,128]{2,1,0:T(8,128)(2,1)}), bf16[64,24,128]{2,1,0:T(8,128)(2,1)S(1)}, u32[]{:S(2)}, u32[]{:S(2)}) async-start(bf16[64,24,128]{2,1,0:T(8,128)(2,1)} %get-tuple-element.51), calls=%async_computation | async-start | bytes 786432 | tf_op jit(solution)/shard_map/all_to_all | solution.py:651
  24.2 1.1 %copy-done = bf16[2816,128]{1,0:T(8,128)(2,1)S(1)} copy-done((bf16[2816,128]{1,0:T(8,128)(2,1)S(1)}, bf16[2816,128]{1,0:T(8,128)(2,1)}, u32[]{:S(2)}) %copy-start) | copy-done | bytes 720920
  26.7 1.1 %collective-permute-done.1.rel_got_ref = bf16[1024,128]{1,0:T(8,128)(2,1)S(1)} collective-permute-done((bf16[1024,128]{1,0:T(8,128)(2,1)S(1)}, bf16[1024,128]{1,0:T(8,128)(2,1)S(1)}, u32[]{:S(2)}, u32[]{:S(2)}) %collective-permute-start.1) | collective-permute-done | bytes 262176 | tf_op jit(solution)/shard_map/ppermute | solution.py:654
  28.2 1.1 %project_queries.1 = (bf16[256,512]{1,0:T(8,128)(2,1)S(1)}, bf16[64,1024]{1,0:T(8,128)(2,1)S(1)}, bf16[64,1024]{1,0:T(8,128)(2,1)S(1)}, bf16[64,1024]{1,0:T(8,128)(2,1)S(1)}, bf16[64,1024]{1,0:T(8,128)(2,1)S(1)}) custom-call(s32[3]{0:T(128)S(1)} %pad_add_fusion.place, bf16[256,256]{1,0:T(8,128)(2,1)S(1)} %get-tuple-element.42.mine_ref, ...), custom_call_target="tpu_custom_call" | custom-call | flops 1000000000 | bytes 2000000 | tf_op jit(solution)/shard_map/project_queries/pallas_call | solution.py:395
  29.2 1.4 %collective-permute-start.3 = (bf16[64,1024]{1,0:T(8,128)(2,1)S(1)}, bf16[64,1024]{1,0:T(8,128)(2,1)S(1)}, u32[]{:S(2)}, u32[]{:S(2)}) collective-permute-start(bf16[64,1024]{1,0:T(8,128)(2,1)S(1)} %get-tuple-element.47), channel_id=1, source_target_pairs={{0,64},{64,128},{128,192},{192,0},{1,65},{65,129},{129,193},{193,1... | collective-permute-start | bytes 393224 | tf_op jit(solution)/shard_map/ppermute | solution.py:613
  30.6 2.6 %collective-permute-start.4 = (bf16[64,1024]{1,0:T(8,128)(2,1)S(1)}, bf16[64,1024]{1,0:T(8,128)(2,1)S(1)}, u32[]{:S(2)}, u32[]{:S(2)}) collective-permute-start(bf16[64,1024]{1,0:T(8,128)(2,1)S(1)} %get-tuple-element.48), channel_id=1, source_target_pairs={{0,128},{64,192},{128,0},{192,64},{1,129},{65,193},{129,1},{193,65... | collective-permute-start | bytes 393224 | tf_op jit(solution)/shard_map/ppermute | solution.py:613
  33.2 1.1 %collective-permute-start.5 = (bf16[64,1024]{1,0:T(8,128)(2,1)S(1)}, bf16[64,1024]{1,0:T(8,128)(2,1)S(1)}, u32[]{:S(2)}, u32[]{:S(2)}) collective-permute-start(bf16[64,1024]{1,0:T(8,128)(2,1)S(1)} %get-tuple-element.49), channel_id=1, source_target_pairs={{0,192},{64,0},{128,64},{192,128},{1,193},{65,1},{129,65},{193,129... | collective-permute-start | bytes 393224 | tf_op jit(solution)/shard_map/ppermute | solution.py:613
  34.3 4.5 %all-to-all-done.inc_ref = bf16[64,24,128]{2,1,0:T(8,128)(2,1)S(1)} async-done(((bf16[64,24,128]{2,1,0:T(8,128)(2,1)}), bf16[64,24,128]{2,1,0:T(8,128)(2,1)S(1)}, u32[]{:S(2)}, u32[]{:S(2)}) %all-to-all-start) | async-done | bytes 393248 | tf_op jit(solution)/shard_map/all_to_all | solution.py:651
  39.6 2.3 %collective-permute-done.4.refs_2_ = bf16[64,1024]{1,0:T(8,128)(2,1)S(1)} collective-permute-done((bf16[64,1024]{1,0:T(8,128)(2,1)S(1)}, bf16[64,1024]{1,0:T(8,128)(2,1)S(1)}, u32[]{:S(2)}, u32[]{:S(2)}) %collective-permute-start.4) | collective-permute-done | bytes 131104 | tf_op jit(solution)/shard_map/ppermute | solution.py:613
  42.8 4.7 %all-to-all-start.1 = ((bf16[8,256,128]{2,1,0:T(8,128)(2,1)}), bf16[8,256,128]{2,1,0:T(8,128)(2,1)S(1)}, u32[]{:S(2)}, u32[]{:S(2)}) async-start(bf16[8,256,128]{2,1,0:T(8,128)(2,1)} %relation_places.1), calls=%async_computation.1 | async-start | bytes 1048576 | tf_op jit(solution)/shard_map/all_to_all | solution.py:661
  47.5 1.6 %project.1 = (bf16[64,1408]{1,0:T(8,128)(2,1)S(1)}, bf16[64,1408]{1,0:T(8,128)(2,1)S(1)}, bf16[64,1408]{1,0:T(8,128)(2,1)S(1)}, bf16[64,1408]{1,0:T(8,128)(2,1)S(1)}) custom-call(s32[3]{0:T(128)S(1)} %pad_add_fusion.place, bf16[256,512]{1,0:T(8,128)(2,1)S(1)} %get-tuple-element.56.pair_ref, bf16[256,256]{1,0:T(8,128)(2,1)S(1)} %collect.1.kv_ref, ...), custom_call_target="tpu_custom_call" | custom-call | flops 1000000000 | bytes 4000000 | tf_op jit(solution)/shard_map/project/pallas_call | solution.py:510
  49.9 2.3 %collective-permute-start.9 = (bf16[64,1408]{1,0:T(8,128)(2,1)S(1)}, bf16[64,1408]{1,0:T(8,128)(2,1)S(1)}, u32[]{:S(2)}, u32[]{:S(2)}) collective-permute-start(bf16[64,1408]{1,0:T(8,128)(2,1)S(1)} %get-tuple-element.63), channel_id=1, source_target_pairs={{0,128},{64,192},{128,0},{192,64},{1,129},{65,193},{129,1},{193,65... | collective-permute-start | bytes 540680 | tf_op jit(solution)/shard_map/ppermute | solution.py:613
  53.0 1.7 %features.1 = (bf16[256,128]{1,0:T(8,128)(2,1)S(1)}, bf16[256,128]{1,0:T(8,128)(2,1)S(1)}, bf16[256,128]{1,0:T(8,128)(2,1)S(1)}, bf16[256,128]{1,0:T(8,128)(2,1)S(1)}) custom-call(s32[3]{0:T(128)S(1)} %pad_add_fusion.place, bf16[256,512]{1,0:T(8,128)(2,1)S(1)} %get-tuple-element.43.sent_ref, bf16[256,256]{1,0:T(8,128)(2,1)S(1)} %collect.1.kv_ref, ...), custom_call_target="tpu_custom_call" | custom-call | flops 1000000000 | bytes 3000000 | tf_op jit(solution)/shard_map/features/pallas_call | solution.py:545
  54.8 1.3 %collective-permute-start.6 = (bf16[256,128]{1,0:T(8,128)(2,1)S(1)}, bf16[256,128]{1,0:T(8,128)(2,1)S(1)}, u32[]{:S(2)}, u32[]{:S(2)}) collective-permute-start(bf16[256,128]{1,0:T(8,128)(2,1)S(1)} %get-tuple-element.59), channel_id=1, source_target_pairs={{0,1},{1,0},{2,3},{3,2},{4,5},{5,4},{6,7},{7,6},{8,9},{9,8},{10,11... | collective-permute-start | bytes 196616 | tf_op jit(solution)/shard_map/ppermute | solution.py:665
  56.3 1.9 %collective-permute-done.6 = bf16[256,128]{1,0:T(8,128)(2,1)S(1)} collective-permute-done((bf16[256,128]{1,0:T(8,128)(2,1)S(1)}, bf16[256,128]{1,0:T(8,128)(2,1)S(1)}, u32[]{:S(2)}, u32[]{:S(2)}) %collective-permute-start.6) | collective-permute-done | bytes 65568 | tf_op jit(solution)/shard_map/ppermute | solution.py:665
  58.3 1.2 %collective-permute-done.7 = bf16[256,128]{1,0:T(8,128)(2,1)S(1)} collective-permute-done((bf16[256,128]{1,0:T(8,128)(2,1)S(1)}, bf16[256,128]{1,0:T(8,128)(2,1)S(1)}, u32[]{:S(2)}, u32[]{:S(2)}) %collective-permute-start.7) | collective-permute-done | bytes 65568 | tf_op jit(solution)/shard_map/ppermute | solution.py:665
  60.5 4.1 %all-to-all-done.1.inc_ref = bf16[8,256,128]{2,1,0:T(8,128)(2,1)S(1)} async-done(((bf16[8,256,128]{2,1,0:T(8,128)(2,1)}), bf16[8,256,128]{2,1,0:T(8,128)(2,1)S(1)}, u32[]{:S(2)}, u32[]{:S(2)}) %all-to-all-start.1) | async-done | bytes 524320 | tf_op jit(solution)/shard_map/all_to_all | solution.py:661
  65.4 4.4 %all-to-all-start.2 = ((bf16[8,8,1920]{2,1,0:T(8,128)(2,1)}), bf16[8,8,1920]{2,1,0:T(8,128)(2,1)S(1)}, u32[]{:S(2)}, u32[]{:S(2)}) async-start(bf16[8,8,1920]{2,1,0:T(8,128)(2,1)} %bitcast.8), calls=%async_computation.2 | async-start | bytes 491520 | tf_op jit(solution)/shard_map/all_to_all | solution.py:674
  69.8 1.5 %collective-permute-start.12 = (bf16[2,256,128]{2,1,0:T(8,128)(2,1)S(1)}, bf16[2,256,128]{2,1,0:T(8,128)(2,1)S(1)}, u32[]{:S(2)}, u32[]{:S(2)}) collective-permute-start(bf16[2,256,128]{2,1,0:T(8,128)(2,1)S(1)} %pad_maximum_fusion.near_ref), channel_id=1, source_target_pairs={{0,192},{192,0},{64,128},{128,64},{1,193},{193,1},{65,129},{129,65... | collective-permute-start | bytes 393224 | tf_op jit(solution)/shard_map/ppermute | solution.py:678
  71.3 2.6 %collective-permute-start.15 = (bf16[256,128]{1,0:T(8,128)(2,1)S(1)}, bf16[256,128]{1,0:T(8,128)(2,1)S(1)}, u32[]{:S(2)}, u32[]{:S(2)}) collective-permute-start(bf16[256,128]{1,0:T(8,128)(2,1)S(1)} %add_convert_fusion.1), channel_id=1, source_target_pairs={{0,3},{3,0},{1,2},{2,1},{4,7},{7,4},{5,6},{6,5},{8,11},{11,8},{9,1... | collective-permute-start | bytes 196616 | tf_op jit(solution)/shard_map/ppermute | solution.py:668
  73.9 2.3 %collective-permute-start.13 = (bf16[2,256,128]{2,1,0:T(8,128)(2,1)S(1)}, bf16[2,256,128]{2,1,0:T(8,128)(2,1)S(1)}, u32[]{:S(2)}, u32[]{:S(2)}) collective-permute-start(bf16[2,256,128]{2,1,0:T(8,128)(2,1)S(1)} %pad_maximum_fusion.near_ref), channel_id=1, source_target_pairs={{0,4},{4,0},{1,5},{5,1},{2,6},{6,2},{3,7},{7,3},{8,12},{12,8},{9,1... | collective-permute-start | bytes 393224 | tf_op jit(solution)/shard_map/ppermute | solution.py:680
  76.1 2.4 %collective-permute-start.14 = (bf16[2,256,128]{2,1,0:T(8,128)(2,1)S(1)}, bf16[2,256,128]{2,1,0:T(8,128)(2,1)S(1)}, u32[]{:S(2)}, u32[]{:S(2)}) collective-permute-start(bf16[2,256,128]{2,1,0:T(8,128)(2,1)S(1)} %collective-permute-done.12.far_ref), channel_id=1, source_target_pairs={{0,4},{4,0},{1,5},{5,1},{2,6},{6,2},{3,7},{7,3},{8,12},{12,8},{9,1... | collective-permute-start | bytes 393224 | tf_op jit(solution)/shard_map/ppermute | solution.py:680
  79.6 2.2 %relations.1 = f32[2,15,2,64,64]{4,3,2,1,0:T(8,128)} custom-call(s32[3]{0:T(128)S(1)} %pad_add_fusion.place, bf16[2,256,128]{2,1,0:T(8,128)(2,1)S(1)} %pad_maximum_fusion.near_ref, bf16[2,256,128]{2,1,0:T(8,128)(2,1)S(1)} %collective-permute-done.12.far_ref, bf16[2,256,128]{2,1,0:T(8,128)(2,1)S(1)} %collective-permute-done.13.c_near_ref, ...), custom_call_target="tpu_custom_call" | custom-call | flops 1000000 | bytes 3000000 | tf_op jit(solution)/shard_map/relations/pallas_call | solution.py:573
  (37 shorter events, 9.0 us)
Async XLA Ops:
  0.6 23.6 %copy-start.1 = (bf16[256,512]{1,0:T(8,128)(2,1)S(1)}, bf16[256,512]{1,0:T(8,128)(2,1)}, u32[]{:S(2)}) copy-start(bf16[256,512]{1,0:T(8,128)(2,1)} %nf_ref.1) | copy-start | bytes 786436
  0.6 23.6 %copy-start.2 = (s32[256]{0:T(256)S(1)}, s32[256]{0:T(256)}, u32[]{:S(2)}) copy-start(s32[256]{0:T(256)} %param.14) | copy-start | bytes 3076
  7.6 31.2 %all-to-all-start = ((bf16[64,24,128]{2,1,0:T(8,128)(2,1)}), bf16[64,24,128]{2,1,0:T(8,128)(2,1)S(1)}, u32[]{:S(2)}, u32[]{:S(2)}) async-start(bf16[64,24,128]{2,1,0:T(8,128)(2,1)} %get-tuple-element.51), calls=%async_computation | async-start | bytes 786432 | tf_op jit(solution)/shard_map/all_to_all | solution.py:651
  24.2 1.1 %copy-start = (bf16[2816,128]{1,0:T(8,128)(2,1)S(1)}, bf16[2816,128]{1,0:T(8,128)(2,1)}, u32[]{:S(2)}) copy-start(bf16[2816,128]{1,0:T(8,128)(2,1)} %get-tuple-element.40.pack_ref) | copy-start | bytes 2162692
  26.1 1.7 %collective-permute-start.1 = (bf16[1024,128]{1,0:T(8,128)(2,1)S(1)}, bf16[1024,128]{1,0:T(8,128)(2,1)S(1)}, u32[]{:S(2)}, u32[]{:S(2)}) collective-permute-start(bf16[1024,128]{1,0:T(8,128)(2,1)S(1)} %get-tuple-element.45), channel_id=1, source_target_pairs={{0,4},{4,0},{1,5},{5,1},{2,6},{6,2},{3,7},{7,3},{8,12},{12,8},{9,1... | collective-permute-start | bytes 786440 | tf_op jit(solution)/shard_map/ppermute | solution.py:654
  26.6 1.5 %collective-permute-start = (bf16[256,512]{1,0:T(8,128)(2,1)S(1)}, bf16[256,512]{1,0:T(8,128)(2,1)S(1)}, u32[]{:S(2)}, u32[]{:S(2)}) collective-permute-start(bf16[256,512]{1,0:T(8,128)(2,1)S(1)} %get-tuple-element.43.sent_ref), channel_id=1, source_target_pairs={{0,4},{4,0},{1,5},{5,1},{2,6},{6,2},{3,7},{7,3},{8,12},{12,8},{9,1... | collective-permute-start | bytes 786440 | tf_op jit(solution)/shard_map/ppermute | solution.py:653
  29.2 10.3 %collective-permute-start.3 = (bf16[64,1024]{1,0:T(8,128)(2,1)S(1)}, bf16[64,1024]{1,0:T(8,128)(2,1)S(1)}, u32[]{:S(2)}, u32[]{:S(2)}) collective-permute-start(bf16[64,1024]{1,0:T(8,128)(2,1)S(1)} %get-tuple-element.47), channel_id=1, source_target_pairs={{0,64},{64,128},{128,192},{192,0},{1,65},{65,129},{129,193},{193,1... | collective-permute-start | bytes 393224 | tf_op jit(solution)/shard_map/ppermute | solution.py:613
  30.6 11.2 %collective-permute-start.4 = (bf16[64,1024]{1,0:T(8,128)(2,1)S(1)}, bf16[64,1024]{1,0:T(8,128)(2,1)S(1)}, u32[]{:S(2)}, u32[]{:S(2)}) collective-permute-start(bf16[64,1024]{1,0:T(8,128)(2,1)S(1)} %get-tuple-element.48), channel_id=1, source_target_pairs={{0,128},{64,192},{128,0},{192,64},{1,129},{65,193},{129,1},{193,65... | collective-permute-start | bytes 393224 | tf_op jit(solution)/shard_map/ppermute | solution.py:613
  33.2 8.6 %collective-permute-start.5 = (bf16[64,1024]{1,0:T(8,128)(2,1)S(1)}, bf16[64,1024]{1,0:T(8,128)(2,1)S(1)}, u32[]{:S(2)}, u32[]{:S(2)}) collective-permute-start(bf16[64,1024]{1,0:T(8,128)(2,1)S(1)} %get-tuple-element.49), channel_id=1, source_target_pairs={{0,192},{64,0},{128,64},{192,128},{1,193},{65,1},{129,65},{193,129... | collective-permute-start | bytes 393224 | tf_op jit(solution)/shard_map/ppermute | solution.py:613
  39.1 2.8 %collective-permute-start.2 = (bf16[256,256]{1,0:T(8,128)(2,1)S(1)}, bf16[256,256]{1,0:T(8,128)(2,1)S(1)}, u32[]{:S(2)}, u32[]{:S(2)}) collective-permute-start(bf16[256,256]{1,0:T(8,128)(2,1)S(1)} %collect.1.kv_ref), channel_id=1, source_target_pairs={{0,4},{4,0},{1,5},{5,1},{2,6},{6,2},{3,7},{7,3},{8,12},{12,8},{9,1... | collective-permute-start | bytes 393224 | tf_op jit(solution)/shard_map/ppermute | solution.py:659
  42.8 21.8 %all-to-all-start.1 = ((bf16[8,256,128]{2,1,0:T(8,128)(2,1)}), bf16[8,256,128]{2,1,0:T(8,128)(2,1)S(1)}, u32[]{:S(2)}, u32[]{:S(2)}) async-start(bf16[8,256,128]{2,1,0:T(8,128)(2,1)} %relation_places.1), calls=%async_computation.1 | async-start | bytes 1048576 | tf_op jit(solution)/shard_map/all_to_all | solution.py:661
  47.5 5.5 %copy-start.3 = (bf16[3,5,512,128]{3,2,1,0:T(8,128)(2,1)S(1)}, bf16[3,5,512,128]{3,2,1,0:T(8,128)(2,1)}, u32[]{:S(2)}) copy-start(bf16[3,5,512,128]{3,2,1,0:T(8,128)(2,1)} %param.23) | copy-start | bytes 5898244
  49.1 10.3 %collective-permute-start.8 = (bf16[64,1408]{1,0:T(8,128)(2,1)S(1)}, bf16[64,1408]{1,0:T(8,128)(2,1)S(1)}, u32[]{:S(2)}, u32[]{:S(2)}) collective-permute-start(bf16[64,1408]{1,0:T(8,128)(2,1)S(1)} %get-tuple-element.62), channel_id=1, source_target_pairs={{0,64},{64,128},{128,192},{192,0},{1,65},{65,129},{129,193},{193,1... | collective-permute-start | bytes 540680 | tf_op jit(solution)/shard_map/ppermute | solution.py:613
  49.9 9.6 %collective-permute-start.9 = (bf16[64,1408]{1,0:T(8,128)(2,1)S(1)}, bf16[64,1408]{1,0:T(8,128)(2,1)S(1)}, u32[]{:S(2)}, u32[]{:S(2)}) collective-permute-start(bf16[64,1408]{1,0:T(8,128)(2,1)S(1)} %get-tuple-element.63), channel_id=1, source_target_pairs={{0,128},{64,192},{128,0},{192,64},{1,129},{65,193},{129,1},{193,65... | collective-permute-start | bytes 540680 | tf_op jit(solution)/shard_map/ppermute | solution.py:613
  52.1 7.6 %collective-permute-start.10 = (bf16[64,1408]{1,0:T(8,128)(2,1)S(1)}, bf16[64,1408]{1,0:T(8,128)(2,1)S(1)}, u32[]{:S(2)}, u32[]{:S(2)}) collective-permute-start(bf16[64,1408]{1,0:T(8,128)(2,1)S(1)} %get-tuple-element.64), channel_id=1, source_target_pairs={{0,192},{64,0},{128,64},{192,128},{1,193},{65,1},{129,65},{193,129... | collective-permute-start | bytes 540680 | tf_op jit(solution)/shard_map/ppermute | solution.py:613
  54.8 3.5 %collective-permute-start.6 = (bf16[256,128]{1,0:T(8,128)(2,1)S(1)}, bf16[256,128]{1,0:T(8,128)(2,1)S(1)}, u32[]{:S(2)}, u32[]{:S(2)}) collective-permute-start(bf16[256,128]{1,0:T(8,128)(2,1)S(1)} %get-tuple-element.59), channel_id=1, source_target_pairs={{0,1},{1,0},{2,3},{3,2},{4,5},{5,4},{6,7},{7,6},{8,9},{9,8},{10,11... | collective-permute-start | bytes 196616 | tf_op jit(solution)/shard_map/ppermute | solution.py:665
  56.1 3.4 %collective-permute-start.7 = (bf16[256,128]{1,0:T(8,128)(2,1)S(1)}, bf16[256,128]{1,0:T(8,128)(2,1)S(1)}, u32[]{:S(2)}, u32[]{:S(2)}) collective-permute-start(bf16[256,128]{1,0:T(8,128)(2,1)S(1)} %get-tuple-element.60), channel_id=1, source_target_pairs={{0,1},{1,0},{2,3},{3,2},{4,5},{5,4},{6,7},{7,6},{8,9},{9,8},{10,11... | collective-permute-start | bytes 196616 | tf_op jit(solution)/shard_map/ppermute | solution.py:665
  65.3 4.4 %collective-permute-start.11 = (bf16[256,128]{1,0:T(8,128)(2,1)S(1)}, bf16[256,128]{1,0:T(8,128)(2,1)S(1)}, u32[]{:S(2)}, u32[]{:S(2)}) collective-permute-start(bf16[256,128]{1,0:T(8,128)(2,1)S(1)} %get-tuple-element.67), channel_id=1, source_target_pairs={{0,64},{64,0},{128,192},{192,128},{1,65},{65,1},{129,193},{193,129... | collective-permute-start | bytes 196616 | tf_op jit(solution)/shard_map/ppermute | solution.py:676
  65.4 16.4 %all-to-all-start.2 = ((bf16[8,8,1920]{2,1,0:T(8,128)(2,1)}), bf16[8,8,1920]{2,1,0:T(8,128)(2,1)S(1)}, u32[]{:S(2)}, u32[]{:S(2)}) async-start(bf16[8,8,1920]{2,1,0:T(8,128)(2,1)} %bitcast.8), calls=%async_computation.2 | async-start | bytes 491520 | tf_op jit(solution)/shard_map/all_to_all | solution.py:674
  69.8 6.4 %collective-permute-start.12 = (bf16[2,256,128]{2,1,0:T(8,128)(2,1)S(1)}, bf16[2,256,128]{2,1,0:T(8,128)(2,1)S(1)}, u32[]{:S(2)}, u32[]{:S(2)}) collective-permute-start(bf16[2,256,128]{2,1,0:T(8,128)(2,1)S(1)} %pad_maximum_fusion.near_ref), channel_id=1, source_target_pairs={{0,192},{192,0},{64,128},{128,64},{1,193},{193,1},{65,129},{129,65... | collective-permute-start | bytes 393224 | tf_op jit(solution)/shard_map/ppermute | solution.py:678
  71.3 7.3 %collective-permute-start.15 = (bf16[256,128]{1,0:T(8,128)(2,1)S(1)}, bf16[256,128]{1,0:T(8,128)(2,1)S(1)}, u32[]{:S(2)}, u32[]{:S(2)}) collective-permute-start(bf16[256,128]{1,0:T(8,128)(2,1)S(1)} %add_convert_fusion.1), channel_id=1, source_target_pairs={{0,3},{3,0},{1,2},{2,1},{4,7},{7,4},{5,6},{6,5},{8,11},{11,8},{9,1... | collective-permute-start | bytes 196616 | tf_op jit(solution)/shard_map/ppermute | solution.py:668
  73.9 5.4 %collective-permute-start.13 = (bf16[2,256,128]{2,1,0:T(8,128)(2,1)S(1)}, bf16[2,256,128]{2,1,0:T(8,128)(2,1)S(1)}, u32[]{:S(2)}, u32[]{:S(2)}) collective-permute-start(bf16[2,256,128]{2,1,0:T(8,128)(2,1)S(1)} %pad_maximum_fusion.near_ref), channel_id=1, source_target_pairs={{0,4},{4,0},{1,5},{5,1},{2,6},{6,2},{3,7},{7,3},{8,12},{12,8},{9,1... | collective-permute-start | bytes 393224 | tf_op jit(solution)/shard_map/ppermute | solution.py:680
  76.1 3.4 %collective-permute-start.14 = (bf16[2,256,128]{2,1,0:T(8,128)(2,1)S(1)}, bf16[2,256,128]{2,1,0:T(8,128)(2,1)S(1)}, u32[]{:S(2)}, u32[]{:S(2)}) collective-permute-start(bf16[2,256,128]{2,1,0:T(8,128)(2,1)S(1)} %collective-permute-done.12.far_ref), channel_id=1, source_target_pairs={{0,4},{4,0},{1,5},{5,1},{2,6},{6,2},{3,7},{7,3},{8,12},{12,8},{9,1... | collective-permute-start | bytes 393224 | tf_op jit(solution)/shard_map/ppermute | solution.py:680

commit v5 on v4

--- a/solution.py
+++ b/solution.py
@@ -54,7 +54,7 @@
     pack_out, send_out,
     edges, listed, prior_in, q_ref, g_ref, rel_ref, rows_ref, k_ref, v_ref, sems,
     wbd, qg, keep, prior, kvm, probs, exps, logs, grads,
-    denom, delta, dprior, dkv, dwk, dwv, dq, drel, ids_ref,
+    denom, shrink, delta, dprior, dkv, dwk, dwv, dq, drel, ids_ref,
 ):
     count = edges.shape[1]
     places = kvm.shape[0]
@@ -175,7 +175,8 @@
         total = None
         for u in range(GROUP):
             b, r, live = entry(i + u)
-            ex = jnp.exp(prior[pl.ds(r, 1), :] * both[u * TILE : (u + 1) * TILE, :WIDE]) * (keep[b] * live)
+            ex = jnp.exp(prior[pl.ds(r, 1), :] * both[u * TILE : (u + 1) * TILE, :WIDE])
+            ex = jnp.where(keep[b] * live > 0.0, ex, 0.0)
             exps[i + u] = ex
             total = ex if total is None else total + ex
         denom[a] += jnp.sum(total, axis=0, keepdims=True)
@@ -185,7 +186,7 @@
         a = tile_of(group)
         total = None
         for u in range(GROUP):
-            soft = exps[i + u] * denom[a]
+            soft = exps[i + u] * shrink[a] * denom[a]
             exps[i + u] = soft
             prob = soft.astype(BF16)
             probs[i + u] = prob
@@ -222,7 +223,8 @@
         lax.fori_loop(0, (used + UNROLL - 1) // UNROLL, some, 0)
 
     sweep(scores)
-    denom[...] = 1.0 / denom[...]
+    shrink[...] = jnp.where(denom[...] > 1e18, 2.0**-64, 1.0)
+    denom[...] = 1.0 / (denom[...] * shrink[...])
     sweep(normalise)
     sweep(backward)
 
@@ -305,6 +307,7 @@
             pltpu.VMEM((places, TILE, WIDE), F32),
             pltpu.VMEM((places, TILE, WIDE), F32),
             pltpu.VMEM((places, TILE, WIDE), F32),
+            pltpu.VMEM((dests, 1, WIDE), F32),
             pltpu.VMEM((dests, 1, WIDE), F32),
             pltpu.VMEM((dests, 1, WIDE), F32),
             pltpu.VMEM((16, WIDE), F32),

time: 82.9 us -> 83 us (level)
  Pallas kernels: 17.1 us -> 20.7 us
  starting transfers between devices: 46 us -> 42.7 us
    pallas_call x1, Pallas kernels: 6.94 us -> 10.6 us  [attend(): pl.pallas_call(attend_kernel, out_shape=(jax.ShapeDtypeStruct((2 * dests...]
    all_to_all x1, starting transfers between devices: 16.5 us -> 13.2 us  [per_device(): incoming = lax.all_to_all(send, ('y', 'z', 'core'), 0, 0, tiled=True)]
where the time goes in v5:
time: 83 us; the launch traced here: 82.7 us
  starting transfers between devices  42.7 us (51%)
  Pallas kernels  20.7 us (25%)
  waiting for transfers between devices  16 us (19%)
  other arithmetic  1.43 us (2%)
  local copies, waits for them, and re-layouts  1.12 us (1%)
    all_to_all x1, starting transfers between devices, per_device(): incoming = lax.all_to_all(send, ('y', 'z', 'core'), 0, 0, tiled=True)  13.2 us
    pallas_call x1, Pallas kernels, attend(): pl.pallas_call(attend_kernel, out_shape=(jax.ShapeDtypeStruct((2 * dests...  10.6 us
    ppermute x6, starting transfers between devices, shifted(): lax.ppermute(blocks[d], axis, [(i, (i + d) % count) for i in range(count)])  8.91 us
    all_to_all x1, starting transfers between devices, per_device(): lax.all_to_all(relation_places(q_arrived, z_count), 'z', 0, 0, tiled=True)  4.75 us
    ppermute x2, starting transfers between devices, per_device(): lax.ppermute(block, 'core', swap)  4.68 us
    all_to_all x1, waiting for transfers between devices, per_device(): incoming = lax.all_to_all(send, ('y', 'z', 'core'), 0, 0, tiled=True)  4.46 us
    all_to_all x1, starting transfers between devices, per_device(): lax.all_to_all(by_y.reshape(z_count, -1, PROJ * WIDE), 'z', 0, 0, tiled=T...  4.35 us
    all_to_all x1, waiting for transfers between devices, per_device(): lax.all_to_all(relation_places(q_arrived, z_count), 'z', 0, 0, tiled=True)  4.07 us
  transfers between devices with their start and end apart: 19, of which 9 were waited for; matrix products, arithmetic and copies ran while one was open for 1% of the time, Pallas kernels for 10%

profile of v5, /device:TPU:1, one launch (start us, length us, event | category | flops | bytes accessed | tf_op | source)
XLA Modules:
  0.0 82.7 jit_solution(16738023104713771302)
XLA Ops:
  0.7 10.6 %attend.1 = (bf16[2816,128]{1,0:T(8,128)(2,1)}, bf16[64,24,128]{2,1,0:T(8,128)(2,1)}) custom-call(s32[3,40]{1,0:T(4,128)} %bitcast.18, f32[2,15]{1,0:T(2,128)} %bitcast.20, bf16[256,128]{1,0:T(8,128)(2,1)} %q_hbm.1, bf16[256,128]{1,0:T(8,128)(2,1)} %g_hbm.1, bf16[256,128]{1,0:T(8,128)(2,1)} %ko_hbm.1, bf16[256,128]{1,0:T(8,128)(2,1)} %vo_hbm.1, ...), custom_call_target="tpu_custom_call" | custom-call | flops 3000000000 | bytes 4000000 | tf_op jit(solution)/shard_map/attend/pallas_call | solution.py:282
  11.2 13.2 %all-to-all-start = ((bf16[64,24,128]{2,1,0:T(8,128)(2,1)}), bf16[64,24,128]{2,1,0:T(8,128)(2,1)S(1)}, u32[]{:S(2)}, u32[]{:S(2)}) async-start(bf16[64,24,128]{2,1,0:T(8,128)(2,1)} %get-tuple-element.51), calls=%async_computation | async-start | bytes 786432 | tf_op jit(solution)/shard_map/all_to_all | solution.py:654
  24.5 1.1 %copy-done = bf16[2816,128]{1,0:T(8,128)(2,1)S(1)} copy-done((bf16[2816,128]{1,0:T(8,128)(2,1)S(1)}, bf16[2816,128]{1,0:T(8,128)(2,1)}, u32[]{:S(2)}) %copy-start) | copy-done | bytes 720920
  27.0 1.1 %collective-permute-done.1.rel_got_ref = bf16[1024,128]{1,0:T(8,128)(2,1)S(1)} collective-permute-done((bf16[1024,128]{1,0:T(8,128)(2,1)S(1)}, bf16[1024,128]{1,0:T(8,128)(2,1)S(1)}, u32[]{:S(2)}, u32[]{:S(2)}) %collective-permute-start.1) | collective-permute-done | bytes 262176 | tf_op jit(solution)/shard_map/ppermute | solution.py:657
  28.4 1.1 %project_queries.1 = (bf16[256,512]{1,0:T(8,128)(2,1)S(1)}, bf16[64,1024]{1,0:T(8,128)(2,1)S(1)}, bf16[64,1024]{1,0:T(8,128)(2,1)S(1)}, bf16[64,1024]{1,0:T(8,128)(2,1)S(1)}, bf16[64,1024]{1,0:T(8,128)(2,1)S(1)}) custom-call(s32[3]{0:T(128)S(1)} %pad_add_fusion.place, bf16[256,256]{1,0:T(8,128)(2,1)S(1)} %get-tuple-element.42.mine_ref, ...), custom_call_target="tpu_custom_call" | custom-call | flops 1000000000 | bytes 2000000 | tf_op jit(solution)/shard_map/project_queries/pallas_call | solution.py:398
  29.5 1.4 %collective-permute-start.3 = (bf16[64,1024]{1,0:T(8,128)(2,1)S(1)}, bf16[64,1024]{1,0:T(8,128)(2,1)S(1)}, u32[]{:S(2)}, u32[]{:S(2)}) collective-permute-start(bf16[64,1024]{1,0:T(8,128)(2,1)S(1)} %get-tuple-element.47), channel_id=1, source_target_pairs={{0,64},{64,128},{128,192},{192,0},{1,65},{65,129},{129,193},{193,1... | collective-permute-start | bytes 393224 | tf_op jit(solution)/shard_map/ppermute | solution.py:616
  30.9 2.6 %collective-permute-start.4 = (bf16[64,1024]{1,0:T(8,128)(2,1)S(1)}, bf16[64,1024]{1,0:T(8,128)(2,1)S(1)}, u32[]{:S(2)}, u32[]{:S(2)}) collective-permute-start(bf16[64,1024]{1,0:T(8,128)(2,1)S(1)} %get-tuple-element.48), channel_id=1, source_target_pairs={{0,128},{64,192},{128,0},{192,64},{1,129},{65,193},{129,1},{193,65... | collective-permute-start | bytes 393224 | tf_op jit(solution)/shard_map/ppermute | solution.py:616
  33.5 1.1 %collective-permute-start.5 = (bf16[64,1024]{1,0:T(8,128)(2,1)S(1)}, bf16[64,1024]{1,0:T(8,128)(2,1)S(1)}, u32[]{:S(2)}, u32[]{:S(2)}) collective-permute-start(bf16[64,1024]{1,0:T(8,128)(2,1)S(1)} %get-tuple-element.49), channel_id=1, source_target_pairs={{0,192},{64,0},{128,64},{192,128},{1,193},{65,1},{129,65},{193,129... | collective-permute-start | bytes 393224 | tf_op jit(solution)/shard_map/ppermute | solution.py:616
  34.6 4.5 %all-to-all-done.inc_ref = bf16[64,24,128]{2,1,0:T(8,128)(2,1)S(1)} async-done(((bf16[64,24,128]{2,1,0:T(8,128)(2,1)}), bf16[64,24,128]{2,1,0:T(8,128)(2,1)S(1)}, u32[]{:S(2)}, u32[]{:S(2)}) %all-to-all-start) | async-done | bytes 393248 | tf_op jit(solution)/shard_map/all_to_all | solution.py:654
  39.8 2.3 %collective-permute-done.4.refs_2_ = bf16[64,1024]{1,0:T(8,128)(2,1)S(1)} collective-permute-done((bf16[64,1024]{1,0:T(8,128)(2,1)S(1)}, bf16[64,1024]{1,0:T(8,128)(2,1)S(1)}, u32[]{:S(2)}, u32[]{:S(2)}) %collective-permute-start.4) | collective-permute-done | bytes 131104 | tf_op jit(solution)/shard_map/ppermute | solution.py:616
  43.1 4.7 %all-to-all-start.1 = ((bf16[8,256,128]{2,1,0:T(8,128)(2,1)}), bf16[8,256,128]{2,1,0:T(8,128)(2,1)S(1)}, u32[]{:S(2)}, u32[]{:S(2)}) async-start(bf16[8,256,128]{2,1,0:T(8,128)(2,1)} %relation_places.1), calls=%async_computation.1 | async-start | bytes 1048576 | tf_op jit(solution)/shard_map/all_to_all | solution.py:664
  47.8 1.6 %project.1 = (bf16[64,1408]{1,0:T(8,128)(2,1)S(1)}, bf16[64,1408]{1,0:T(8,128)(2,1)S(1)}, bf16[64,1408]{1,0:T(8,128)(2,1)S(1)}, bf16[64,1408]{1,0:T(8,128)(2,1)S(1)}) custom-call(s32[3]{0:T(128)S(1)} %pad_add_fusion.place, bf16[256,512]{1,0:T(8,128)(2,1)S(1)} %get-tuple-element.56.pair_ref, bf16[256,256]{1,0:T(8,128)(2,1)S(1)} %collect.1.kv_ref, ...), custom_call_target="tpu_custom_call" | custom-call | flops 1000000000 | bytes 4000000 | tf_op jit(solution)/shard_map/project/pallas_call | solution.py:513
  50.1 2.3 %collective-permute-start.9 = (bf16[64,1408]{1,0:T(8,128)(2,1)S(1)}, bf16[64,1408]{1,0:T(8,128)(2,1)S(1)}, u32[]{:S(2)}, u32[]{:S(2)}) collective-permute-start(bf16[64,1408]{1,0:T(8,128)(2,1)S(1)} %get-tuple-element.63), channel_id=1, source_target_pairs={{0,128},{64,192},{128,0},{192,64},{1,129},{65,193},{129,1},{193,65... | collective-permute-start | bytes 540680 | tf_op jit(solution)/shard_map/ppermute | solution.py:616
  53.3 1.7 %features.1 = (bf16[256,128]{1,0:T(8,128)(2,1)S(1)}, bf16[256,128]{1,0:T(8,128)(2,1)S(1)}, bf16[256,128]{1,0:T(8,128)(2,1)S(1)}, bf16[256,128]{1,0:T(8,128)(2,1)S(1)}) custom-call(s32[3]{0:T(128)S(1)} %pad_add_fusion.place, bf16[256,512]{1,0:T(8,128)(2,1)S(1)} %get-tuple-element.43.sent_ref, bf16[256,256]{1,0:T(8,128)(2,1)S(1)} %collect.1.kv_ref, ...), custom_call_target="tpu_custom_call" | custom-call | flops 1000000000 | bytes 3000000 | tf_op jit(solution)/shard_map/features/pallas_call | solution.py:548
  55.0 1.3 %collective-permute-start.6 = (bf16[256,128]{1,0:T(8,128)(2,1)S(1)}, bf16[256,128]{1,0:T(8,128)(2,1)S(1)}, u32[]{:S(2)}, u32[]{:S(2)}) collective-permute-start(bf16[256,128]{1,0:T(8,128)(2,1)S(1)} %get-tuple-element.59), channel_id=1, source_target_pairs={{0,1},{1,0},{2,3},{3,2},{4,5},{5,4},{6,7},{7,6},{8,9},{9,8},{10,11... | collective-permute-start | bytes 196616 | tf_op jit(solution)/shard_map/ppermute | solution.py:668
  56.6 1.9 %collective-permute-done.6 = bf16[256,128]{1,0:T(8,128)(2,1)S(1)} collective-permute-done((bf16[256,128]{1,0:T(8,128)(2,1)S(1)}, bf16[256,128]{1,0:T(8,128)(2,1)S(1)}, u32[]{:S(2)}, u32[]{:S(2)}) %collective-permute-start.6) | collective-permute-done | bytes 65568 | tf_op jit(solution)/shard_map/ppermute | solution.py:668
  58.5 1.2 %collective-permute-done.7 = bf16[256,128]{1,0:T(8,128)(2,1)S(1)} collective-permute-done((bf16[256,128]{1,0:T(8,128)(2,1)S(1)}, bf16[256,128]{1,0:T(8,128)(2,1)S(1)}, u32[]{:S(2)}, u32[]{:S(2)}) %collective-permute-start.7) | collective-permute-done | bytes 65568 | tf_op jit(solution)/shard_map/ppermute | solution.py:668
  60.8 4.1 %all-to-all-done.1.inc_ref = bf16[8,256,128]{2,1,0:T(8,128)(2,1)S(1)} async-done(((bf16[8,256,128]{2,1,0:T(8,128)(2,1)}), bf16[8,256,128]{2,1,0:T(8,128)(2,1)S(1)}, u32[]{:S(2)}, u32[]{:S(2)}) %all-to-all-start.1) | async-done | bytes 524320 | tf_op jit(solution)/shard_map/all_to_all | solution.py:664
  65.7 4.4 %all-to-all-start.2 = ((bf16[8,8,1920]{2,1,0:T(8,128)(2,1)}), bf16[8,8,1920]{2,1,0:T(8,128)(2,1)S(1)}, u32[]{:S(2)}, u32[]{:S(2)}) async-start(bf16[8,8,1920]{2,1,0:T(8,128)(2,1)} %bitcast.8), calls=%async_computation.2 | async-start | bytes 491520 | tf_op jit(solution)/shard_map/all_to_all | solution.py:677
  70.0 1.5 %collective-permute-start.12 = (bf16[2,256,128]{2,1,0:T(8,128)(2,1)S(1)}, bf16[2,256,128]{2,1,0:T(8,128)(2,1)S(1)}, u32[]{:S(2)}, u32[]{:S(2)}) collective-permute-start(bf16[2,256,128]{2,1,0:T(8,128)(2,1)S(1)} %pad_maximum_fusion.near_ref), channel_id=1, source_target_pairs={{0,192},{192,0},{64,128},{128,64},{1,193},{193,1},{65,129},{129,65... | collective-permute-start | bytes 393224 | tf_op jit(solution)/shard_map/ppermute | solution.py:681
  71.6 2.6 %collective-permute-start.15 = (bf16[256,128]{1,0:T(8,128)(2,1)S(1)}, bf16[256,128]{1,0:T(8,128)(2,1)S(1)}, u32[]{:S(2)}, u32[]{:S(2)}) collective-permute-start(bf16[256,128]{1,0:T(8,128)(2,1)S(1)} %add_convert_fusion.1), channel_id=1, source_target_pairs={{0,3},{3,0},{1,2},{2,1},{4,7},{7,4},{5,6},{6,5},{8,11},{11,8},{9,1... | collective-permute-start | bytes 196616 | tf_op jit(solution)/shard_map/ppermute | solution.py:671
  74.1 2.3 %collective-permute-start.13 = (bf16[2,256,128]{2,1,0:T(8,128)(2,1)S(1)}, bf16[2,256,128]{2,1,0:T(8,128)(2,1)S(1)}, u32[]{:S(2)}, u32[]{:S(2)}) collective-permute-start(bf16[2,256,128]{2,1,0:T(8,128)(2,1)S(1)} %pad_maximum_fusion.near_ref), channel_id=1, source_target_pairs={{0,4},{4,0},{1,5},{5,1},{2,6},{6,2},{3,7},{7,3},{8,12},{12,8},{9,1... | collective-permute-start | bytes 393224 | tf_op jit(solution)/shard_map/ppermute | solution.py:683
  76.4 2.4 %collective-permute-start.14 = (bf16[2,256,128]{2,1,0:T(8,128)(2,1)S(1)}, bf16[2,256,128]{2,1,0:T(8,128)(2,1)S(1)}, u32[]{:S(2)}, u32[]{:S(2)}) collective-permute-start(bf16[2,256,128]{2,1,0:T(8,128)(2,1)S(1)} %collective-permute-done.12.far_ref), channel_id=1, source_target_pairs={{0,4},{4,0},{1,5},{5,1},{2,6},{6,2},{3,7},{7,3},{8,12},{12,8},{9,1... | collective-permute-start | bytes 393224 | tf_op jit(solution)/shard_map/ppermute | solution.py:683
  79.8 2.2 %relations.1 = f32[2,15,2,64,64]{4,3,2,1,0:T(8,128)} custom-call(s32[3]{0:T(128)S(1)} %pad_add_fusion.place, bf16[2,256,128]{2,1,0:T(8,128)(2,1)S(1)} %pad_maximum_fusion.near_ref, bf16[2,256,128]{2,1,0:T(8,128)(2,1)S(1)} %collective-permute-done.12.far_ref, bf16[2,256,128]{2,1,0:T(8,128)(2,1)S(1)} %collective-permute-done.13.c_near_ref, ...), custom_call_target="tpu_custom_call" | custom-call | flops 1000000 | bytes 3000000 | tf_op jit(solution)/shard_map/relations/pallas_call | solution.py:576
  (37 shorter events, 8.9 us)
Async XLA Ops:
  0.6 23.9 %copy-start.1 = (bf16[256,512]{1,0:T(8,128)(2,1)S(1)}, bf16[256,512]{1,0:T(8,128)(2,1)}, u32[]{:S(2)}) copy-start(bf16[256,512]{1,0:T(8,128)(2,1)} %nf_ref.1) | copy-start | bytes 786436
  0.6 23.8 %copy-start.2 = (s32[256]{0:T(256)S(1)}, s32[256]{0:T(256)}, u32[]{:S(2)}) copy-start(s32[256]{0:T(256)} %param.14) | copy-start | bytes 3076
  11.2 27.8 %all-to-all-start = ((bf16[64,24,128]{2,1,0:T(8,128)(2,1)}), bf16[64,24,128]{2,1,0:T(8,128)(2,1)S(1)}, u32[]{:S(2)}, u32[]{:S(2)}) async-start(bf16[64,24,128]{2,1,0:T(8,128)(2,1)} %get-tuple-element.51), calls=%async_computation | async-start | bytes 786432 | tf_op jit(solution)/shard_map/all_to_all | solution.py:654
  24.5 1.1 %copy-start = (bf16[2816,128]{1,0:T(8,128)(2,1)S(1)}, bf16[2816,128]{1,0:T(8,128)(2,1)}, u32[]{:S(2)}) copy-start(bf16[2816,128]{1,0:T(8,128)(2,1)} %get-tuple-element.40.pack_ref) | copy-start | bytes 2162692
  26.3 1.7 %collective-permute-start.1 = (bf16[1024,128]{1,0:T(8,128)(2,1)S(1)}, bf16[1024,128]{1,0:T(8,128)(2,1)S(1)}, u32[]{:S(2)}, u32[]{:S(2)}) collective-permute-start(bf16[1024,128]{1,0:T(8,128)(2,1)S(1)} %get-tuple-element.45), channel_id=1, source_target_pairs={{0,4},{4,0},{1,5},{5,1},{2,6},{6,2},{3,7},{7,3},{8,12},{12,8},{9,1... | collective-permute-start | bytes 786440 | tf_op jit(solution)/shard_map/ppermute | solution.py:657
  26.9 1.5 %collective-permute-start = (bf16[256,512]{1,0:T(8,128)(2,1)S(1)}, bf16[256,512]{1,0:T(8,128)(2,1)S(1)}, u32[]{:S(2)}, u32[]{:S(2)}) collective-permute-start(bf16[256,512]{1,0:T(8,128)(2,1)S(1)} %get-tuple-element.43.sent_ref), channel_id=1, source_target_pairs={{0,4},{4,0},{1,5},{5,1},{2,6},{6,2},{3,7},{7,3},{8,12},{12,8},{9,1... | collective-permute-start | bytes 786440 | tf_op jit(solution)/shard_map/ppermute | solution.py:656
  29.5 10.3 %collective-permute-start.3 = (bf16[64,1024]{1,0:T(8,128)(2,1)S(1)}, bf16[64,1024]{1,0:T(8,128)(2,1)S(1)}, u32[]{:S(2)}, u32[]{:S(2)}) collective-permute-start(bf16[64,1024]{1,0:T(8,128)(2,1)S(1)} %get-tuple-element.47), channel_id=1, source_target_pairs={{0,64},{64,128},{128,192},{192,0},{1,65},{65,129},{129,193},{193,1... | collective-permute-start | bytes 393224 | tf_op jit(solution)/shard_map/ppermute | solution.py:616
  30.9 11.2 %collective-permute-start.4 = (bf16[64,1024]{1,0:T(8,128)(2,1)S(1)}, bf16[64,1024]{1,0:T(8,128)(2,1)S(1)}, u32[]{:S(2)}, u32[]{:S(2)}) collective-permute-start(bf16[64,1024]{1,0:T(8,128)(2,1)S(1)} %get-tuple-element.48), channel_id=1, source_target_pairs={{0,128},{64,192},{128,0},{192,64},{1,129},{65,193},{129,1},{193,65... | collective-permute-start | bytes 393224 | tf_op jit(solution)/shard_map/ppermute | solution.py:616
  33.5 8.6 %collective-permute-start.5 = (bf16[64,1024]{1,0:T(8,128)(2,1)S(1)}, bf16[64,1024]{1,0:T(8,128)(2,1)S(1)}, u32[]{:S(2)}, u32[]{:S(2)}) collective-permute-start(bf16[64,1024]{1,0:T(8,128)(2,1)S(1)} %get-tuple-element.49), channel_id=1, source_target_pairs={{0,192},{64,0},{128,64},{192,128},{1,193},{65,1},{129,65},{193,129... | collective-permute-start | bytes 393224 | tf_op jit(solution)/shard_map/ppermute | solution.py:616
  39.3 2.8 %collective-permute-start.2 = (bf16[256,256]{1,0:T(8,128)(2,1)S(1)}, bf16[256,256]{1,0:T(8,128)(2,1)S(1)}, u32[]{:S(2)}, u32[]{:S(2)}) collective-permute-start(bf16[256,256]{1,0:T(8,128)(2,1)S(1)} %collect.1.kv_ref), channel_id=1, source_target_pairs={{0,4},{4,0},{1,5},{5,1},{2,6},{6,2},{3,7},{7,3},{8,12},{12,8},{9,1... | collective-permute-start | bytes 393224 | tf_op jit(solution)/shard_map/ppermute | solution.py:662
  43.1 21.8 %all-to-all-start.1 = ((bf16[8,256,128]{2,1,0:T(8,128)(2,1)}), bf16[8,256,128]{2,1,0:T(8,128)(2,1)S(1)}, u32[]{:S(2)}, u32[]{:S(2)}) async-start(bf16[8,256,128]{2,1,0:T(8,128)(2,1)} %relation_places.1), calls=%async_computation.1 | async-start | bytes 1048576 | tf_op jit(solution)/shard_map/all_to_all | solution.py:664
  47.8 5.5 %copy-start.3 = (bf16[3,5,512,128]{3,2,1,0:T(8,128)(2,1)S(1)}, bf16[3,5,512,128]{3,2,1,0:T(8,128)(2,1)}, u32[]{:S(2)}) copy-start(bf16[3,5,512,128]{3,2,1,0:T(8,128)(2,1)} %param.23) | copy-start | bytes 5898244
  49.4 10.3 %collective-permute-start.8 = (bf16[64,1408]{1,0:T(8,128)(2,1)S(1)}, bf16[64,1408]{1,0:T(8,128)(2,1)S(1)}, u32[]{:S(2)}, u32[]{:S(2)}) collective-permute-start(bf16[64,1408]{1,0:T(8,128)(2,1)S(1)} %get-tuple-element.62), channel_id=1, source_target_pairs={{0,64},{64,128},{128,192},{192,0},{1,65},{65,129},{129,193},{193,1... | collective-permute-start | bytes 540680 | tf_op jit(solution)/shard_map/ppermute | solution.py:616
  50.1 9.6 %collective-permute-start.9 = (bf16[64,1408]{1,0:T(8,128)(2,1)S(1)}, bf16[64,1408]{1,0:T(8,128)(2,1)S(1)}, u32[]{:S(2)}, u32[]{:S(2)}) collective-permute-start(bf16[64,1408]{1,0:T(8,128)(2,1)S(1)} %get-tuple-element.63), channel_id=1, source_target_pairs={{0,128},{64,192},{128,0},{192,64},{1,129},{65,193},{129,1},{193,65... | collective-permute-start | bytes 540680 | tf_op jit(solution)/shard_map/ppermute | solution.py:616
  52.4 7.6 %collective-permute-start.10 = (bf16[64,1408]{1,0:T(8,128)(2,1)S(1)}, bf16[64,1408]{1,0:T(8,128)(2,1)S(1)}, u32[]{:S(2)}, u32[]{:S(2)}) collective-permute-start(bf16[64,1408]{1,0:T(8,128)(2,1)S(1)} %get-tuple-element.64), channel_id=1, source_target_pairs={{0,192},{64,0},{128,64},{192,128},{1,193},{65,1},{129,65},{193,129... | collective-permute-start | bytes 540680 | tf_op jit(solution)/shard_map/ppermute | solution.py:616
  55.0 3.5 %collective-permute-start.6 = (bf16[256,128]{1,0:T(8,128)(2,1)S(1)}, bf16[256,128]{1,0:T(8,128)(2,1)S(1)}, u32[]{:S(2)}, u32[]{:S(2)}) collective-permute-start(bf16[256,128]{1,0:T(8,128)(2,1)S(1)} %get-tuple-element.59), channel_id=1, source_target_pairs={{0,1},{1,0},{2,3},{3,2},{4,5},{5,4},{6,7},{7,6},{8,9},{9,8},{10,11... | collective-permute-start | bytes 196616 | tf_op jit(solution)/shard_map/ppermute | solution.py:668
  56.3 3.4 %collective-permute-start.7 = (bf16[256,128]{1,0:T(8,128)(2,1)S(1)}, bf16[256,128]{1,0:T(8,128)(2,1)S(1)}, u32[]{:S(2)}, u32[]{:S(2)}) collective-permute-start(bf16[256,128]{1,0:T(8,128)(2,1)S(1)} %get-tuple-element.60), channel_id=1, source_target_pairs={{0,1},{1,0},{2,3},{3,2},{4,5},{5,4},{6,7},{7,6},{8,9},{9,8},{10,11... | collective-permute-start | bytes 196616 | tf_op jit(solution)/shard_map/ppermute | solution.py:668
  65.6 4.4 %collective-permute-start.11 = (bf16[256,128]{1,0:T(8,128)(2,1)S(1)}, bf16[256,128]{1,0:T(8,128)(2,1)S(1)}, u32[]{:S(2)}, u32[]{:S(2)}) collective-permute-start(bf16[256,128]{1,0:T(8,128)(2,1)S(1)} %get-tuple-element.67), channel_id=1, source_target_pairs={{0,64},{64,0},{128,192},{192,128},{1,65},{65,1},{129,193},{193,129... | collective-permute-start | bytes 196616 | tf_op jit(solution)/shard_map/ppermute | solution.py:679
  65.7 16.4 %all-to-all-start.2 = ((bf16[8,8,1920]{2,1,0:T(8,128)(2,1)}), bf16[8,8,1920]{2,1,0:T(8,128)(2,1)S(1)}, u32[]{:S(2)}, u32[]{:S(2)}) async-start(bf16[8,8,1920]{2,1,0:T(8,128)(2,1)} %bitcast.8), calls=%async_computation.2 | async-start | bytes 491520 | tf_op jit(solution)/shard_map/all_to_all | solution.py:677
  70.0 6.4 %collective-permute-start.12 = (bf16[2,256,128]{2,1,0:T(8,128)(2,1)S(1)}, bf16[2,256,128]{2,1,0:T(8,128)(2,1)S(1)}, u32[]{:S(2)}, u32[]{:S(2)}) collective-permute-start(bf16[2,256,128]{2,1,0:T(8,128)(2,1)S(1)} %pad_maximum_fusion.near_ref), channel_id=1, source_target_pairs={{0,192},{192,0},{64,128},{128,64},{1,193},{193,1},{65,129},{129,65... | collective-permute-start | bytes 393224 | tf_op jit(solution)/shard_map/ppermute | solution.py:681
  71.6 7.3 %collective-permute-start.15 = (bf16[256,128]{1,0:T(8,128)(2,1)S(1)}, bf16[256,128]{1,0:T(8,128)(2,1)S(1)}, u32[]{:S(2)}, u32[]{:S(2)}) collective-permute-start(bf16[256,128]{1,0:T(8,128)(2,1)S(1)} %add_convert_fusion.1), channel_id=1, source_target_pairs={{0,3},{3,0},{1,2},{2,1},{4,7},{7,4},{5,6},{6,5},{8,11},{11,8},{9,1... | collective-permute-start | bytes 196616 | tf_op jit(solution)/shard_map/ppermute | solution.py:671
  74.1 5.3 %collective-permute-start.13 = (bf16[2,256,128]{2,1,0:T(8,128)(2,1)S(1)}, bf16[2,256,128]{2,1,0:T(8,128)(2,1)S(1)}, u32[]{:S(2)}, u32[]{:S(2)}) collective-permute-start(bf16[2,256,128]{2,1,0:T(8,128)(2,1)S(1)} %pad_maximum_fusion.near_ref), channel_id=1, source_target_pairs={{0,4},{4,0},{1,5},{5,1},{2,6},{6,2},{3,7},{7,3},{8,12},{12,8},{9,1... | collective-permute-start | bytes 393224 | tf_op jit(solution)/shard_map/ppermute | solution.py:683
  76.4 3.4 %collective-permute-start.14 = (bf16[2,256,128]{2,1,0:T(8,128)(2,1)S(1)}, bf16[2,256,128]{2,1,0:T(8,128)(2,1)S(1)}, u32[]{:S(2)}, u32[]{:S(2)}) collective-permute-start(bf16[2,256,128]{2,1,0:T(8,128)(2,1)S(1)} %collective-permute-done.12.far_ref), channel_id=1, source_target_pairs={{0,4},{4,0},{1,5},{5,1},{2,6},{6,2},{3,7},{7,3},{8,12},{12,8},{9,1... | collective-permute-start | bytes 393224 | tf_op jit(solution)/shard_map/ppermute | solution.py:683

commit v6 on v5

--- a/solution.py
+++ b/solution.py
@@ -51,8 +51,8 @@
 
 def attend_kernel(
     edges_hbm, prior_hbm, q_hbm, g_hbm, ko_hbm, vo_hbm, kh_hbm, vh_hbm, rel_hbm, rows_hbm,
-    pack_out, send_out,
-    edges, listed, prior_in, q_ref, g_ref, rel_ref, rows_ref, k_ref, v_ref, sems,
+    pack_hbm, send_hbm,
+    pack_out, send_out, out_sems, edges, listed, prior_in, q_ref, g_ref, rel_ref, rows_ref, k_ref, v_ref, sems,
     wbd, qg, keep, prior, kvm, probs, exps, logs, grads,
     denom, shrink, delta, dprior, dkv, dwk, dwv, dq, drel, ids_ref,
 ):
@@ -237,17 +237,6 @@
         for w in range(2):
             at = at_own + (1 + w) * own + b * TILE
             pack_out[at : at + TILE, :] = dkv[b, :, w * WIDE : (w + 1) * WIDE].astype(BF16)
-    for b in range(halo_tiles):
-        back = dkv[own_tiles + b]
-        block = jnp.concatenate(
-            [
-                back[:, :WIDE].reshape(8, 8, WIDE),
-                back[:, WIDE:].reshape(8, 8, WIDE),
-                jnp.broadcast_to(ids_ref[8 * b : 8 * b + 8, :].reshape(8, 1, WIDE), (8, 8, WIDE)),
-            ],
-            axis=1,
-        )
-        send_out[8 * b : 8 * b + 8] = block.astype(BF16)
     for w, ref in enumerate((dwk, dwv)):
         for r in range(RELS):
             at = (w * RELS + r) * TILE
@@ -268,6 +257,23 @@
             to = (w * dests + y) * REL_BLOCK
             pack_out[to : to + REL_ROWS, :] = drel[at : at + REL_ROWS, :].astype(BF16)
             pack_out[to + REL_ROWS : to + REL_BLOCK, :] = tail
+    pack_copy = pltpu.make_async_copy(pack_out, pack_hbm, out_sems.at[0])
+    pack_copy.start()
+    for b in range(halo_tiles):
+        back = dkv[own_tiles + b]
+        block = jnp.concatenate(
+            [
+                back[:, :WIDE].reshape(8, 8, WIDE),
+                back[:, WIDE:].reshape(8, 8, WIDE),
+                jnp.broadcast_to(ids_ref[8 * b : 8 * b + 8, :].reshape(8, 1, WIDE), (8, 8, WIDE)),
+            ],
+            axis=1,
+        )
+        send_out[8 * b : 8 * b + 8] = block.astype(BF16)
+    send_copy = pltpu.make_async_copy(send_out, send_hbm, out_sems.at[1])
+    send_copy.start()
+    pack_copy.wait()
+    send_copy.wait()
 
 
 def attend(edges, rel_prior, queries, grad_output, key_rows, value_rows, halo_keys, halo_values, rel_weight, halo_rows):
@@ -286,8 +292,11 @@
             jax.ShapeDtypeStruct((slabs, BLOCK, WIDE), BF16),
         ),
         in_specs=[HBM] * 10,
-        out_specs=(VMEM,) * 2,
+        out_specs=(HBM,) * 2,
         scratch_shapes=[
+            pltpu.VMEM((2 * dests * REL_BLOCK + 3 * rows, WIDE), BF16),
+            pltpu.VMEM((slabs, BLOCK, WIDE), BF16),
+            pltpu.SemaphoreType.DMA((2,)),
             pltpu.SMEM(edges.shape, jnp.int32),
             pltpu.SMEM((places + 1,), jnp.int32),
             pltpu.SMEM(rel_prior.shape, F32),

time: 83 us -> 82.8 us (level)
  Pallas kernels: 20.7 us -> 17.2 us
  starting transfers between devices: 42.7 us -> 46.1 us
    pallas_call x1, Pallas kernels: 10.6 us -> 7.04 us  [attend(): pl.pallas_call(attend_kernel, out_shape=(jax.ShapeDtypeStruct((2 * dests...]
    all_to_all x1, starting transfers between devices: 13.2 us -> 16.6 us  [per_device(): incoming = lax.all_to_all(send, ('y', 'z', 'core'), 0, 0, tiled=True)]
where the time goes in v6:
time: 82.8 us; the launch traced here: 82.5 us
  starting transfers between devices  46.1 us (56%)
  Pallas kernels  17.2 us (21%)
  waiting for transfers between devices  16 us (19%)
  other arithmetic  1.43 us (2%)
  local copies, waits for them, and re-layouts  1.12 us (1%)
    all_to_all x1, starting transfers between devices, per_device(): incoming = lax.all_to_all(send, ('y', 'z', 'core'), 0, 0, tiled=True)  16.6 us
    ppermute x6, starting transfers between devices, shifted(): lax.ppermute(blocks[d], axis, [(i, (i + d) % count) for i in range(count)])  8.92 us
    pallas_call x1, Pallas kernels, attend(): pl.pallas_call(attend_kernel, out_shape=(jax.ShapeDtypeStruct((2 * dests...  7.04 us
    all_to_all x1, starting transfers between devices, per_device(): lax.all_to_all(relation_places(q_arrived, z_count), 'z', 0, 0, tiled=True)  4.74 us
    ppermute x2, starting transfers between devices, per_device(): lax.ppermute(block, 'core', swap)  4.68 us
    all_to_all x1, waiting for transfers between devices, per_device(): incoming = lax.all_to_all(send, ('y', 'z', 'core'), 0, 0, tiled=True)  4.46 us
    all_to_all x1, starting transfers between devices, per_device(): lax.all_to_all(by_y.reshape(z_count, -1, PROJ * WIDE), 'z', 0, 0, tiled=T...  4.36 us
    all_to_all x1, waiting for transfers between devices, per_device(): lax.all_to_all(relation_places(q_arrived, z_count), 'z', 0, 0, tiled=True)  4.07 us
  transfers between devices with their start and end apart: 19, of which 9 were waited for; matrix products, arithmetic and copies ran while one was open for 1% of the time, Pallas kernels for 10%

profile of v6, /device:TPU:1, one launch (start us, length us, event | category | flops | bytes accessed | tf_op | source)
XLA Modules:
  0.0 82.5 jit_solution(13205856348721537080)
XLA Ops:
  0.7 7.0 %attend.1 = (bf16[2816,128]{1,0:T(8,128)(2,1)}, bf16[64,24,128]{2,1,0:T(8,128)(2,1)}) custom-call(s32[3,40]{1,0:T(4,128)} %bitcast.18, f32[2,15]{1,0:T(2,128)} %bitcast.20, bf16[256,128]{1,0:T(8,128)(2,1)} %q_hbm.1, bf16[256,128]{1,0:T(8,128)(2,1)} %g_hbm.1, bf16[256,128]{1,0:T(8,128)(2,1)} %ko_hbm.1, bf16[256,128]{1,0:T(8,128)(2,1)} %vo_hbm.1, ...), custom_call_target="tpu_custom_call" | custom-call | flops 3000000000 | bytes 4000000 | tf_op jit(solution)/shard_map/attend/pallas_call | solution.py:288
  7.7 16.6 %all-to-all-start = ((bf16[64,24,128]{2,1,0:T(8,128)(2,1)}), bf16[64,24,128]{2,1,0:T(8,128)(2,1)S(1)}, u32[]{:S(2)}, u32[]{:S(2)}) async-start(bf16[64,24,128]{2,1,0:T(8,128)(2,1)} %get-tuple-element.51), calls=%async_computation | async-start | bytes 786432 | tf_op jit(solution)/shard_map/all_to_all | solution.py:663
  24.4 1.1 %copy-done = bf16[2816,128]{1,0:T(8,128)(2,1)S(1)} copy-done((bf16[2816,128]{1,0:T(8,128)(2,1)S(1)}, bf16[2816,128]{1,0:T(8,128)(2,1)}, u32[]{:S(2)}) %copy-start) | copy-done | bytes 720920
  26.8 1.1 %collective-permute-done.1.rel_got_ref = bf16[1024,128]{1,0:T(8,128)(2,1)S(1)} collective-permute-done((bf16[1024,128]{1,0:T(8,128)(2,1)S(1)}, bf16[1024,128]{1,0:T(8,128)(2,1)S(1)}, u32[]{:S(2)}, u32[]{:S(2)}) %collective-permute-start.1) | collective-permute-done | bytes 262176 | tf_op jit(solution)/shard_map/ppermute | solution.py:666
  28.3 1.1 %project_queries.1 = (bf16[256,512]{1,0:T(8,128)(2,1)S(1)}, bf16[64,1024]{1,0:T(8,128)(2,1)S(1)}, bf16[64,1024]{1,0:T(8,128)(2,1)S(1)}, bf16[64,1024]{1,0:T(8,128)(2,1)S(1)}, bf16[64,1024]{1,0:T(8,128)(2,1)S(1)}) custom-call(s32[3]{0:T(128)S(1)} %pad_add_fusion.place, bf16[256,256]{1,0:T(8,128)(2,1)S(1)} %get-tuple-element.42.mine_ref, ...), custom_call_target="tpu_custom_call" | custom-call | flops 1000000000 | bytes 2000000 | tf_op jit(solution)/shard_map/project_queries/pallas_call | solution.py:407
  29.4 1.4 %collective-permute-start.3 = (bf16[64,1024]{1,0:T(8,128)(2,1)S(1)}, bf16[64,1024]{1,0:T(8,128)(2,1)S(1)}, u32[]{:S(2)}, u32[]{:S(2)}) collective-permute-start(bf16[64,1024]{1,0:T(8,128)(2,1)S(1)} %get-tuple-element.47), channel_id=1, source_target_pairs={{0,64},{64,128},{128,192},{192,0},{1,65},{65,129},{129,193},{193,1... | collective-permute-start | bytes 393224 | tf_op jit(solution)/shard_map/ppermute | solution.py:625
  30.7 2.6 %collective-permute-start.4 = (bf16[64,1024]{1,0:T(8,128)(2,1)S(1)}, bf16[64,1024]{1,0:T(8,128)(2,1)S(1)}, u32[]{:S(2)}, u32[]{:S(2)}) collective-permute-start(bf16[64,1024]{1,0:T(8,128)(2,1)S(1)} %get-tuple-element.48), channel_id=1, source_target_pairs={{0,128},{64,192},{128,0},{192,64},{1,129},{65,193},{129,1},{193,65... | collective-permute-start | bytes 393224 | tf_op jit(solution)/shard_map/ppermute | solution.py:625
  33.3 1.1 %collective-permute-start.5 = (bf16[64,1024]{1,0:T(8,128)(2,1)S(1)}, bf16[64,1024]{1,0:T(8,128)(2,1)S(1)}, u32[]{:S(2)}, u32[]{:S(2)}) collective-permute-start(bf16[64,1024]{1,0:T(8,128)(2,1)S(1)} %get-tuple-element.49), channel_id=1, source_target_pairs={{0,192},{64,0},{128,64},{192,128},{1,193},{65,1},{129,65},{193,129... | collective-permute-start | bytes 393224 | tf_op jit(solution)/shard_map/ppermute | solution.py:625
  34.4 4.5 %all-to-all-done.inc_ref = bf16[64,24,128]{2,1,0:T(8,128)(2,1)S(1)} async-done(((bf16[64,24,128]{2,1,0:T(8,128)(2,1)}), bf16[64,24,128]{2,1,0:T(8,128)(2,1)S(1)}, u32[]{:S(2)}, u32[]{:S(2)}) %all-to-all-start) | async-done | bytes 393248 | tf_op jit(solution)/shard_map/all_to_all | solution.py:663
  39.7 2.3 %collective-permute-done.4.refs_2_ = bf16[64,1024]{1,0:T(8,128)(2,1)S(1)} collective-permute-done((bf16[64,1024]{1,0:T(8,128)(2,1)S(1)}, bf16[64,1024]{1,0:T(8,128)(2,1)S(1)}, u32[]{:S(2)}, u32[]{:S(2)}) %collective-permute-start.4) | collective-permute-done | bytes 131104 | tf_op jit(solution)/shard_map/ppermute | solution.py:625
  42.9 4.7 %all-to-all-start.1 = ((bf16[8,256,128]{2,1,0:T(8,128)(2,1)}), bf16[8,256,128]{2,1,0:T(8,128)(2,1)S(1)}, u32[]{:S(2)}, u32[]{:S(2)}) async-start(bf16[8,256,128]{2,1,0:T(8,128)(2,1)} %relation_places.1), calls=%async_computation.1 | async-start | bytes 1048576 | tf_op jit(solution)/shard_map/all_to_all | solution.py:673
  47.7 1.6 %project.1 = (bf16[64,1408]{1,0:T(8,128)(2,1)S(1)}, bf16[64,1408]{1,0:T(8,128)(2,1)S(1)}, bf16[64,1408]{1,0:T(8,128)(2,1)S(1)}, bf16[64,1408]{1,0:T(8,128)(2,1)S(1)}) custom-call(s32[3]{0:T(128)S(1)} %pad_add_fusion.place, bf16[256,512]{1,0:T(8,128)(2,1)S(1)} %get-tuple-element.56.pair_ref, bf16[256,256]{1,0:T(8,128)(2,1)S(1)} %collect.1.kv_ref, ...), custom_call_target="tpu_custom_call" | custom-call | flops 1000000000 | bytes 4000000 | tf_op jit(solution)/shard_map/project/pallas_call | solution.py:522
  50.0 2.3 %collective-permute-start.9 = (bf16[64,1408]{1,0:T(8,128)(2,1)S(1)}, bf16[64,1408]{1,0:T(8,128)(2,1)S(1)}, u32[]{:S(2)}, u32[]{:S(2)}) collective-permute-start(bf16[64,1408]{1,0:T(8,128)(2,1)S(1)} %get-tuple-element.63), channel_id=1, source_target_pairs={{0,128},{64,192},{128,0},{192,64},{1,129},{65,193},{129,1},{193,65... | collective-permute-start | bytes 540680 | tf_op jit(solution)/shard_map/ppermute | solution.py:625
  53.1 1.7 %features.1 = (bf16[256,128]{1,0:T(8,128)(2,1)S(1)}, bf16[256,128]{1,0:T(8,128)(2,1)S(1)}, bf16[256,128]{1,0:T(8,128)(2,1)S(1)}, bf16[256,128]{1,0:T(8,128)(2,1)S(1)}) custom-call(s32[3]{0:T(128)S(1)} %pad_add_fusion.place, bf16[256,512]{1,0:T(8,128)(2,1)S(1)} %get-tuple-element.43.sent_ref, bf16[256,256]{1,0:T(8,128)(2,1)S(1)} %collect.1.kv_ref, ...), custom_call_target="tpu_custom_call" | custom-call | flops 1000000000 | bytes 3000000 | tf_op jit(solution)/shard_map/features/pallas_call | solution.py:557
  54.9 1.3 %collective-permute-start.6 = (bf16[256,128]{1,0:T(8,128)(2,1)S(1)}, bf16[256,128]{1,0:T(8,128)(2,1)S(1)}, u32[]{:S(2)}, u32[]{:S(2)}) collective-permute-start(bf16[256,128]{1,0:T(8,128)(2,1)S(1)} %get-tuple-element.59), channel_id=1, source_target_pairs={{0,1},{1,0},{2,3},{3,2},{4,5},{5,4},{6,7},{7,6},{8,9},{9,8},{10,11... | collective-permute-start | bytes 196616 | tf_op jit(solution)/shard_map/ppermute | solution.py:677
  56.4 1.9 %collective-permute-done.6 = bf16[256,128]{1,0:T(8,128)(2,1)S(1)} collective-permute-done((bf16[256,128]{1,0:T(8,128)(2,1)S(1)}, bf16[256,128]{1,0:T(8,128)(2,1)S(1)}, u32[]{:S(2)}, u32[]{:S(2)}) %collective-permute-start.6) | collective-permute-done | bytes 65568 | tf_op jit(solution)/shard_map/ppermute | solution.py:677
  58.4 1.2 %collective-permute-done.7 = bf16[256,128]{1,0:T(8,128)(2,1)S(1)} collective-permute-done((bf16[256,128]{1,0:T(8,128)(2,1)S(1)}, bf16[256,128]{1,0:T(8,128)(2,1)S(1)}, u32[]{:S(2)}, u32[]{:S(2)}) %collective-permute-start.7) | collective-permute-done | bytes 65568 | tf_op jit(solution)/shard_map/ppermute | solution.py:677
  60.6 4.1 %all-to-all-done.1.inc_ref = bf16[8,256,128]{2,1,0:T(8,128)(2,1)S(1)} async-done(((bf16[8,256,128]{2,1,0:T(8,128)(2,1)}), bf16[8,256,128]{2,1,0:T(8,128)(2,1)S(1)}, u32[]{:S(2)}, u32[]{:S(2)}) %all-to-all-start.1) | async-done | bytes 524320 | tf_op jit(solution)/shard_map/all_to_all | solution.py:673
  65.5 4.4 %all-to-all-start.2 = ((bf16[8,8,1920]{2,1,0:T(8,128)(2,1)}), bf16[8,8,1920]{2,1,0:T(8,128)(2,1)S(1)}, u32[]{:S(2)}, u32[]{:S(2)}) async-start(bf16[8,8,1920]{2,1,0:T(8,128)(2,1)} %bitcast.8), calls=%async_computation.2 | async-start | bytes 491520 | tf_op jit(solution)/shard_map/all_to_all | solution.py:686
  69.9 1.5 %collective-permute-start.12 = (bf16[2,256,128]{2,1,0:T(8,128)(2,1)S(1)}, bf16[2,256,128]{2,1,0:T(8,128)(2,1)S(1)}, u32[]{:S(2)}, u32[]{:S(2)}) collective-permute-start(bf16[2,256,128]{2,1,0:T(8,128)(2,1)S(1)} %pad_maximum_fusion.near_ref), channel_id=1, source_target_pairs={{0,192},{192,0},{64,128},{128,64},{1,193},{193,1},{65,129},{129,65... | collective-permute-start | bytes 393224 | tf_op jit(solution)/shard_map/ppermute | solution.py:690
  71.4 2.6 %collective-permute-start.15 = (bf16[256,128]{1,0:T(8,128)(2,1)S(1)}, bf16[256,128]{1,0:T(8,128)(2,1)S(1)}, u32[]{:S(2)}, u32[]{:S(2)}) collective-permute-start(bf16[256,128]{1,0:T(8,128)(2,1)S(1)} %add_convert_fusion.1), channel_id=1, source_target_pairs={{0,3},{3,0},{1,2},{2,1},{4,7},{7,4},{5,6},{6,5},{8,11},{11,8},{9,1... | collective-permute-start | bytes 196616 | tf_op jit(solution)/shard_map/ppermute | solution.py:680
  74.0 2.3 %collective-permute-start.13 = (bf16[2,256,128]{2,1,0:T(8,128)(2,1)S(1)}, bf16[2,256,128]{2,1,0:T(8,128)(2,1)S(1)}, u32[]{:S(2)}, u32[]{:S(2)}) collective-permute-start(bf16[2,256,128]{2,1,0:T(8,128)(2,1)S(1)} %pad_maximum_fusion.near_ref), channel_id=1, source_target_pairs={{0,4},{4,0},{1,5},{5,1},{2,6},{6,2},{3,7},{7,3},{8,12},{12,8},{9,1... | collective-permute-start | bytes 393224 | tf_op jit(solution)/shard_map/ppermute | solution.py:692
  76.3 2.4 %collective-permute-start.14 = (bf16[2,256,128]{2,1,0:T(8,128)(2,1)S(1)}, bf16[2,256,128]{2,1,0:T(8,128)(2,1)S(1)}, u32[]{:S(2)}, u32[]{:S(2)}) collective-permute-start(bf16[2,256,128]{2,1,0:T(8,128)(2,1)S(1)} %collective-permute-done.12.far_ref), channel_id=1, source_target_pairs={{0,4},{4,0},{1,5},{5,1},{2,6},{6,2},{3,7},{7,3},{8,12},{12,8},{9,1... | collective-permute-start | bytes 393224 | tf_op jit(solution)/shard_map/ppermute | solution.py:692
  79.7 2.2 %relations.1 = f32[2,15,2,64,64]{4,3,2,1,0:T(8,128)} custom-call(s32[3]{0:T(128)S(1)} %pad_add_fusion.place, bf16[2,256,128]{2,1,0:T(8,128)(2,1)S(1)} %pad_maximum_fusion.near_ref, bf16[2,256,128]{2,1,0:T(8,128)(2,1)S(1)} %collective-permute-done.12.far_ref, bf16[2,256,128]{2,1,0:T(8,128)(2,1)S(1)} %collective-permute-done.13.c_near_ref, ...), custom_call_target="tpu_custom_call" | custom-call | flops 1000000 | bytes 3000000 | tf_op jit(solution)/shard_map/relations/pallas_call | solution.py:585
  (37 shorter events, 9.0 us)
Async XLA Ops:
  0.6 23.7 %copy-start.1 = (bf16[256,512]{1,0:T(8,128)(2,1)S(1)}, bf16[256,512]{1,0:T(8,128)(2,1)}, u32[]{:S(2)}) copy-start(bf16[256,512]{1,0:T(8,128)(2,1)} %nf_ref.1) | copy-start | bytes 786436
  0.6 23.7 %copy-start.2 = (s32[256]{0:T(256)S(1)}, s32[256]{0:T(256)}, u32[]{:S(2)}) copy-start(s32[256]{0:T(256)} %param.14) | copy-start | bytes 3076
  7.7 31.2 %all-to-all-start = ((bf16[64,24,128]{2,1,0:T(8,128)(2,1)}), bf16[64,24,128]{2,1,0:T(8,128)(2,1)S(1)}, u32[]{:S(2)}, u32[]{:S(2)}) async-start(bf16[64,24,128]{2,1,0:T(8,128)(2,1)} %get-tuple-element.51), calls=%async_computation | async-start | bytes 786432 | tf_op jit(solution)/shard_map/all_to_all | solution.py:663
  24.3 1.1 %copy-start = (bf16[2816,128]{1,0:T(8,128)(2,1)S(1)}, bf16[2816,128]{1,0:T(8,128)(2,1)}, u32[]{:S(2)}) copy-start(bf16[2816,128]{1,0:T(8,128)(2,1)} %get-tuple-element.40.pack_ref) | copy-start | bytes 2162692
  26.2 1.7 %collective-permute-start.1 = (bf16[1024,128]{1,0:T(8,128)(2,1)S(1)}, bf16[1024,128]{1,0:T(8,128)(2,1)S(1)}, u32[]{:S(2)}, u32[]{:S(2)}) collective-permute-start(bf16[1024,128]{1,0:T(8,128)(2,1)S(1)} %get-tuple-element.45), channel_id=1, source_target_pairs={{0,4},{4,0},{1,5},{5,1},{2,6},{6,2},{3,7},{7,3},{8,12},{12,8},{9,1... | collective-permute-start | bytes 786440 | tf_op jit(solution)/shard_map/ppermute | solution.py:666
  26.7 1.5 %collective-permute-start = (bf16[256,512]{1,0:T(8,128)(2,1)S(1)}, bf16[256,512]{1,0:T(8,128)(2,1)S(1)}, u32[]{:S(2)}, u32[]{:S(2)}) collective-permute-start(bf16[256,512]{1,0:T(8,128)(2,1)S(1)} %get-tuple-element.43.sent_ref), channel_id=1, source_target_pairs={{0,4},{4,0},{1,5},{5,1},{2,6},{6,2},{3,7},{7,3},{8,12},{12,8},{9,1... | collective-permute-start | bytes 786440 | tf_op jit(solution)/shard_map/ppermute | solution.py:665
  29.4 10.3 %collective-permute-start.3 = (bf16[64,1024]{1,0:T(8,128)(2,1)S(1)}, bf16[64,1024]{1,0:T(8,128)(2,1)S(1)}, u32[]{:S(2)}, u32[]{:S(2)}) collective-permute-start(bf16[64,1024]{1,0:T(8,128)(2,1)S(1)} %get-tuple-element.47), channel_id=1, source_target_pairs={{0,64},{64,128},{128,192},{192,0},{1,65},{65,129},{129,193},{193,1... | collective-permute-start | bytes 393224 | tf_op jit(solution)/shard_map/ppermute | solution.py:625
  30.7 11.2 %collective-permute-start.4 = (bf16[64,1024]{1,0:T(8,128)(2,1)S(1)}, bf16[64,1024]{1,0:T(8,128)(2,1)S(1)}, u32[]{:S(2)}, u32[]{:S(2)}) collective-permute-start(bf16[64,1024]{1,0:T(8,128)(2,1)S(1)} %get-tuple-element.48), channel_id=1, source_target_pairs={{0,128},{64,192},{128,0},{192,64},{1,129},{65,193},{129,1},{193,65... | collective-permute-start | bytes 393224 | tf_op jit(solution)/shard_map/ppermute | solution.py:625
  33.3 8.6 %collective-permute-start.5 = (bf16[64,1024]{1,0:T(8,128)(2,1)S(1)}, bf16[64,1024]{1,0:T(8,128)(2,1)S(1)}, u32[]{:S(2)}, u32[]{:S(2)}) collective-permute-start(bf16[64,1024]{1,0:T(8,128)(2,1)S(1)} %get-tuple-element.49), channel_id=1, source_target_pairs={{0,192},{64,0},{128,64},{192,128},{1,193},{65,1},{129,65},{193,129... | collective-permute-start | bytes 393224 | tf_op jit(solution)/shard_map/ppermute | solution.py:625
  39.2 2.8 %collective-permute-start.2 = (bf16[256,256]{1,0:T(8,128)(2,1)S(1)}, bf16[256,256]{1,0:T(8,128)(2,1)S(1)}, u32[]{:S(2)}, u32[]{:S(2)}) collective-permute-start(bf16[256,256]{1,0:T(8,128)(2,1)S(1)} %collect.1.kv_ref), channel_id=1, source_target_pairs={{0,4},{4,0},{1,5},{5,1},{2,6},{6,2},{3,7},{7,3},{8,12},{12,8},{9,1... | collective-permute-start | bytes 393224 | tf_op jit(solution)/shard_map/ppermute | solution.py:671
  42.9 21.8 %all-to-all-start.1 = ((bf16[8,256,128]{2,1,0:T(8,128)(2,1)}), bf16[8,256,128]{2,1,0:T(8,128)(2,1)S(1)}, u32[]{:S(2)}, u32[]{:S(2)}) async-start(bf16[8,256,128]{2,1,0:T(8,128)(2,1)} %relation_places.1), calls=%async_computation.1 | async-start | bytes 1048576 | tf_op jit(solution)/shard_map/all_to_all | solution.py:673
  47.7 5.5 %copy-start.3 = (bf16[3,5,512,128]{3,2,1,0:T(8,128)(2,1)S(1)}, bf16[3,5,512,128]{3,2,1,0:T(8,128)(2,1)}, u32[]{:S(2)}) copy-start(bf16[3,5,512,128]{3,2,1,0:T(8,128)(2,1)} %param.23) | copy-start | bytes 5898244
  49.3 10.3 %collective-permute-start.8 = (bf16[64,1408]{1,0:T(8,128)(2,1)S(1)}, bf16[64,1408]{1,0:T(8,128)(2,1)S(1)}, u32[]{:S(2)}, u32[]{:S(2)}) collective-permute-start(bf16[64,1408]{1,0:T(8,128)(2,1)S(1)} %get-tuple-element.62), channel_id=1, source_target_pairs={{0,64},{64,128},{128,192},{192,0},{1,65},{65,129},{129,193},{193,1... | collective-permute-start | bytes 540680 | tf_op jit(solution)/shard_map/ppermute | solution.py:625
  50.0 9.6 %collective-permute-start.9 = (bf16[64,1408]{1,0:T(8,128)(2,1)S(1)}, bf16[64,1408]{1,0:T(8,128)(2,1)S(1)}, u32[]{:S(2)}, u32[]{:S(2)}) collective-permute-start(bf16[64,1408]{1,0:T(8,128)(2,1)S(1)} %get-tuple-element.63), channel_id=1, source_target_pairs={{0,128},{64,192},{128,0},{192,64},{1,129},{65,193},{129,1},{193,65... | collective-permute-start | bytes 540680 | tf_op jit(solution)/shard_map/ppermute | solution.py:625
  52.3 7.6 %collective-permute-start.10 = (bf16[64,1408]{1,0:T(8,128)(2,1)S(1)}, bf16[64,1408]{1,0:T(8,128)(2,1)S(1)}, u32[]{:S(2)}, u32[]{:S(2)}) collective-permute-start(bf16[64,1408]{1,0:T(8,128)(2,1)S(1)} %get-tuple-element.64), channel_id=1, source_target_pairs={{0,192},{64,0},{128,64},{192,128},{1,193},{65,1},{129,65},{193,129... | collective-permute-start | bytes 540680 | tf_op jit(solution)/shard_map/ppermute | solution.py:625
  54.9 3.5 %collective-permute-start.6 = (bf16[256,128]{1,0:T(8,128)(2,1)S(1)}, bf16[256,128]{1,0:T(8,128)(2,1)S(1)}, u32[]{:S(2)}, u32[]{:S(2)}) collective-permute-start(bf16[256,128]{1,0:T(8,128)(2,1)S(1)} %get-tuple-element.59), channel_id=1, source_target_pairs={{0,1},{1,0},{2,3},{3,2},{4,5},{5,4},{6,7},{7,6},{8,9},{9,8},{10,11... | collective-permute-start | bytes 196616 | tf_op jit(solution)/shard_map/ppermute | solution.py:677
  56.2 3.4 %collective-permute-start.7 = (bf16[256,128]{1,0:T(8,128)(2,1)S(1)}, bf16[256,128]{1,0:T(8,128)(2,1)S(1)}, u32[]{:S(2)}, u32[]{:S(2)}) collective-permute-start(bf16[256,128]{1,0:T(8,128)(2,1)S(1)} %get-tuple-element.60), channel_id=1, source_target_pairs={{0,1},{1,0},{2,3},{3,2},{4,5},{5,4},{6,7},{7,6},{8,9},{9,8},{10,11... | collective-permute-start | bytes 196616 | tf_op jit(solution)/shard_map/ppermute | solution.py:677
  65.4 4.4 %collective-permute-start.11 = (bf16[256,128]{1,0:T(8,128)(2,1)S(1)}, bf16[256,128]{1,0:T(8,128)(2,1)S(1)}, u32[]{:S(2)}, u32[]{:S(2)}) collective-permute-start(bf16[256,128]{1,0:T(8,128)(2,1)S(1)} %get-tuple-element.67), channel_id=1, source_target_pairs={{0,64},{64,0},{128,192},{192,128},{1,65},{65,1},{129,193},{193,129... | collective-permute-start | bytes 196616 | tf_op jit(solution)/shard_map/ppermute | solution.py:688
  65.5 16.4 %all-to-all-start.2 = ((bf16[8,8,1920]{2,1,0:T(8,128)(2,1)}), bf16[8,8,1920]{2,1,0:T(8,128)(2,1)S(1)}, u32[]{:S(2)}, u32[]{:S(2)}) async-start(bf16[8,8,1920]{2,1,0:T(8,128)(2,1)} %bitcast.8), calls=%async_computation.2 | async-start | bytes 491520 | tf_op jit(solution)/shard_map/all_to_all | solution.py:686
  69.9 6.4 %collective-permute-start.12 = (bf16[2,256,128]{2,1,0:T(8,128)(2,1)S(1)}, bf16[2,256,128]{2,1,0:T(8,128)(2,1)S(1)}, u32[]{:S(2)}, u32[]{:S(2)}) collective-permute-start(bf16[2,256,128]{2,1,0:T(8,128)(2,1)S(1)} %pad_maximum_fusion.near_ref), channel_id=1, source_target_pairs={{0,192},{192,0},{64,128},{128,64},{1,193},{193,1},{65,129},{129,65... | collective-permute-start | bytes 393224 | tf_op jit(solution)/shard_map/ppermute | solution.py:690
  71.4 7.3 %collective-permute-start.15 = (bf16[256,128]{1,0:T(8,128)(2,1)S(1)}, bf16[256,128]{1,0:T(8,128)(2,1)S(1)}, u32[]{:S(2)}, u32[]{:S(2)}) collective-permute-start(bf16[256,128]{1,0:T(8,128)(2,1)S(1)} %add_convert_fusion.1), channel_id=1, source_target_pairs={{0,3},{3,0},{1,2},{2,1},{4,7},{7,4},{5,6},{6,5},{8,11},{11,8},{9,1... | collective-permute-start | bytes 196616 | tf_op jit(solution)/shard_map/ppermute | solution.py:680
  74.0 5.4 %collective-permute-start.13 = (bf16[2,256,128]{2,1,0:T(8,128)(2,1)S(1)}, bf16[2,256,128]{2,1,0:T(8,128)(2,1)S(1)}, u32[]{:S(2)}, u32[]{:S(2)}) collective-permute-start(bf16[2,256,128]{2,1,0:T(8,128)(2,1)S(1)} %pad_maximum_fusion.near_ref), channel_id=1, source_target_pairs={{0,4},{4,0},{1,5},{5,1},{2,6},{6,2},{3,7},{7,3},{8,12},{12,8},{9,1... | collective-permute-start | bytes 393224 | tf_op jit(solution)/shard_map/ppermute | solution.py:692
  76.3 3.4 %collective-permute-start.14 = (bf16[2,256,128]{2,1,0:T(8,128)(2,1)S(1)}, bf16[2,256,128]{2,1,0:T(8,128)(2,1)S(1)}, u32[]{:S(2)}, u32[]{:S(2)}) collective-permute-start(bf16[2,256,128]{2,1,0:T(8,128)(2,1)S(1)} %collective-permute-done.12.far_ref), channel_id=1, source_target_pairs={{0,4},{4,0},{1,5},{5,1},{2,6},{6,2},{3,7},{7,3},{8,12},{12,8},{9,1... | collective-permute-start | bytes 393224 | tf_op jit(solution)/shard_map/ppermute | solution.py:692
